TPU v7x, 32 devices: a whole 2x2x4 slice. The times are simulated.
32 devices in a mesh: grp: 2 (over x), row: 8 (over z, y), col: 2 (over core).
Axes of the slice: x: 2, y: 2, z: 4, core: 2. Of those that a mesh axis runs over, the one named last changes fastest.
Arguments:
- counts: bfloat16 [256, 256, 256], P(('grp', 'row', 'col')), parts along dimension 0, may hold values from 1 to 576, as said below
- tile_pos: int32 [256], P(('grp', 'row', 'col')), parts along dimension 0, may hold values from -1 to 7, as said below
- omega_t: bfloat16 [64, 32768], P(None, 'col'), may hold values from -0.09375 to 0.09375
- psi: bfloat16 [64, 2048], P(None, 'row'), may hold values from -0.125 to 0.125
Outputs:
- range_sketch: float32 [64, 4096], P(None, ('grp', 'row')), parts along dimension 1
- corange: float32 [64, 65536], P(None, ('grp', 'col', 'row')), parts along dimension 1
There are 2 independent parts, one for each index of `grp`. A program takes and returns all parts, laid end to end along the dimension named above; an argument that names none is the same for every part. Nothing has to cross between parts.
Inputs may be any that keep to these rules, and one draw needn't show every extreme that they name: Positive counts; entries of empty slots are ignored. `tile_pos`: slot d of every device refers to a block of the d-th column range; every device holds at least one tile; in every draw some device fills all 8 slots and some column range receives a tile from every device of a col index.
All inputs are finite; a program needn't handle non-finite values.
Results may differ from a plain program's by a relative error of at most 0.003.
Values sent between devices are 32-bit elements; how exact they have to be, the bound alone decides.
No kernel may reach another device: no remote copies, remote signals or barrier semaphores. Data moves between devices by JAX's collectives and lax.ppermute only.
A program may use at most 128 MiB of HBM per device.

v0:
```python
import math

import jax
import jax.numpy as jnp
from jax import lax
from jax.sharding import PartitionSpec as P

shift_log = math.log(5.0)
highest = lax.Precision.HIGHEST


def on_device(counts, tile_pos, omega_t, psi):
    slots, tile, _ = counts.shape
    rank = omega_t.shape[0]
    width = omega_t.shape[1]
    cooccurrence_blocks = width // (slots * tile)
    live = tile_pos >= 0
    select = (
        tile_pos[:, None] == jnp.arange(cooccurrence_blocks, dtype=jnp.int32)[None, :]
    ).astype(jnp.float32)
    values = jnp.where(live[:, None, None], counts.astype(jnp.float32), 0.0)
    row_part = jnp.sum(values, axis=(0, 2))
    column_part = jnp.einsum(
        "db,dt->dbt", select, jnp.sum(values, axis=1), precision=highest
    ).reshape(width)
    row_sums = lax.psum(row_part, "col")
    column_sums = lax.psum(column_part, "row")
    smoothing_power = column_sums**0.75
    total = lax.psum(jnp.sum(smoothing_power), "col")
    smooth_tile = jnp.einsum(
        "db,dbt->dt",
        select,
        smoothing_power.reshape(slots, cooccurrence_blocks, tile),
        precision=highest,
    )
    safe = jnp.where(live[:, None], smooth_tile, 1.0)
    safe_counts = jnp.where(live[:, None, None], counts.astype(jnp.float32), 1.0)
    pmi = (
        jnp.log(safe_counts)
        + (jnp.log(total) - jnp.log(row_sums))[None, :, None]
        - jnp.log(safe)[:, None, :]
    )
    shifted_pmi_matrix = jnp.where(
        live[:, None, None], jnp.maximum(pmi - shift_log, 0.0), 0.0
    ).astype(jnp.bfloat16)
    selected_test_rows = jnp.einsum(
        "db,rdbt->rdt",
        select.astype(jnp.bfloat16),
        omega_t.reshape(rank, slots, cooccurrence_blocks, tile),
        preferred_element_type=jnp.float32,
    ).astype(jnp.bfloat16)
    partial_range_sketch = jnp.einsum(
        "qbn,bun->qu", selected_test_rows, shifted_pmi_matrix, preferred_element_type=jnp.float32
    )
    range_sketch = lax.psum(partial_range_sketch, "col")
    partial_contribution = jnp.einsum(
        "hg,xgl->xhl", psi, shifted_pmi_matrix, preferred_element_type=jnp.float32
    )
    incoming_blocks, anchor = (
        lax.all_to_all(partial_contribution, "row", split_axis=0, concat_axis=0, tiled=True),
        lax.all_to_all(
            tile_pos.astype(jnp.float32), "row", split_axis=0, concat_axis=0, tiled=True
        ),
    )
    onehot = (
        anchor[:, None] == jnp.arange(cooccurrence_blocks, dtype=jnp.float32)[None, :]
    ).astype(jnp.float32)
    corange = jnp.einsum("sb,srt->rbt", onehot, incoming_blocks, precision=highest).reshape(
        rank, cooccurrence_blocks * tile
    )
    return (range_sketch, corange)


def solution(mesh):
    placed = (
        P(("grp", "row", "col"), None, None),
        P(("grp", "row", "col")),
        P(None, "col"),
        P(None, "row"),
    )
    return jax.shard_map(
        on_device,
        mesh=mesh,
        in_specs=placed,
        out_specs=(P(None, ("grp", "row")), P(None, ("grp", "col", "row"))),
        check_vma=False,
    )
```

profile of v0, /device:TPU:0, one launch (start us, length us, event | category | flops | bytes accessed | tf_op | source)
XLA Modules:
  0.0 126.2 jit_solution(6382505826087773348)
XLA Ops:
  7.2 0.0 copy-start
  7.2 0.0 copy-start.1
  7.2 0.0 all-reduce.4.cloned.1.call-start
  7.2 0.7 broadcast_compare_fusion
  8.0 0.7 convert_bitcast_fusion
  8.7 1.7 %fusion = (f32[256]{0:T(256)S(1)}, f32[8,256]{1,0:T(8,128)S(1)}) fusion(bf16[8,256,256]{2,1,0:T(8,128)(2,1)} %param.4, pred[8]{0:T(512)(128)(4,1)S(1)} %broadcast_compare_fusion), kind=kLoop, calls=%fused_computation.2 | loop fusion | flops 2094848 | bytes 1057800 | tf_op jit(solution)/shard_map/reduce_sum | solution.py:22
  10.4 0.1 multiply_bitcast_fusion
  10.4 0.7 copy.16
  11.1 0.0 all-reduce.4.cloned.1.call-update
  11.1 0.7 convert_bitcast_fusion.1
  11.8 0.7 copy.8
  12.5 7.3 %all-to-all-start.1 = ((f32[8,1,1]{2,1,0:T(1,128)}), f32[8,1,1]{2,1,0:T(1,128)S(1)}, u32[]{:S(2)}, u32[]{:S(2)}) async-start(f32[8,1,1]{2,1,0:T(1,128)} %copy.8), calls=%async_computation.1 | async-start | bytes 8192 | tf_op jit(solution)/shard_map/all_to_all | solution.py:61
  19.8 63.4 %all-reduce.4.cloned.1.call-done = f32[16384]{0:T(1024)} async-done(((f32[16384]{0:T(1024)}), f32[16384]{0:T(1024)}) %all-reduce.4.cloned.1.call-update) | async-done | bytes 65552 | tf_op jit(solution)/shard_map/psum | solution.py:27
  83.2 1.5 %fusion.25 = (f32[]{:T(128)}, f32[16384]{0:T(1024)S(1)}) fusion(f32[16384]{0:T(1024)} %all-reduce.4.cloned.1.call-done), kind=kLoop, calls=%fused_computation.37 | loop fusion | flops 16383 | bytes 131076 | tf_op jit(solution)/shard_map/reduce_sum | solution.py:29
  84.7 3.1 %all-reduce = (f32[256]{0:T(256)S(1)}, f32[]{:T(128)}) all-reduce(f32[256]{0:T(256)S(1)} %get-tuple-element.2, f32[]{:T(128)} %get-tuple-element.6), channel_id=1, replica_groups=mesh['grp'=2,'row'=8,'col'=2] {'col'}, use_global_device_ids=true, to_apply=%region_5.6 | all-reduce | flops 257 | bytes 2056 | tf_op jit(solution)/shard_map/psum | solution.py:26
  88.5 0.2 fusion.16
  88.6 0.1 fusion.18
  88.7 0.7 fusion.8
  89.4 0.0 copy-start.2
  89.5 1.1 convolution_bitcast_fusion
  90.6 4.5 %all-to-all-start = ((f32[8,64,256]{2,1,0:T(8,128)}), f32[8,64,256]{2,1,0:T(8,128)}, u32[]{:S(2)}, u32[]{:S(2)}) async-start(f32[8,64,256]{2,1,0:T(8,128)} %convolution_bitcast_fusion), calls=%async_computation | async-start | bytes 1048576 | tf_op jit(solution)/shard_map/all_to_all | solution.py:60
  95.1 0.0 all-reduce.6.cloned.1.call-start
  95.2 0.5 copy.15
  95.7 0.7 fusion.9
  96.4 0.1 reduce
  96.5 1.1 convolution_bitcast_fusion.1
  97.6 0.0 all-reduce.6.cloned.1.call-update
  97.6 12.4 %all-to-all-done = f32[8,64,256]{2,1,0:T(8,128)} async-done(((f32[8,64,256]{2,1,0:T(8,128)}), f32[8,64,256]{2,1,0:T(8,128)}, u32[]{:S(2)}, u32[]{:S(2)}) %all-to-all-start) | async-done | bytes 524320 | tf_op jit(solution)/shard_map/all_to_all | solution.py:60
  110.0 1.7 %fusion.11 = f32[64,256,8]{1,2,0:T(8,128)S(1)} fusion(f32[8,64,256]{2,1,0:T(8,128)} %all-to-all-done, f32[8]{0:T(128)S(1)} %reduce), kind=kOutput, calls=%fused_computation.16 | convolution fusion | flops 12582976 | bytes 1048608 | tf_op jit(solution)/shard_map/sb,srt->rbt/dot_general | solution.py:68
  111.7 1.0 copy.17
  112.7 5.2 %all-reduce.6.cloned.1.call-done = f32[64,256]{1,0:T(8,128)} async-done(((f32[64,256]{1,0:T(8,128)}), f32[64,256]{1,0:T(8,128)}) %all-reduce.6.cloned.1.call-update) | async-done | bytes 65552 | tf_op jit(solution)/shard_map/psum | solution.py:55
  117.9 1.5 %copy.33 = f32[64,256]{1,0:T(8,128)} copy(f32[64,256]{1,0:T(8,128)} %all-reduce.6.cloned.1.call-done) | data formatting | bytes 131072
  (6 shorter events, 0.0 us)
Async XLA Ops:
  7.2 82.3 %copy-start = (bf16[64,256]{1,0:T(8,128)(2,1)S(1)}, bf16[64,256]{1,0:T(8,128)(2,1)}, u32[]{:S(2)}) copy-start(bf16[64,256]{1,0:T(8,128)(2,1)} %param.7) | copy-start | bytes 98308
  7.2 81.5 %copy-start.1 = (bf16[8,256,256]{2,1,0:T(8,128)(2,1)S(1)}, bf16[8,256,256]{2,1,0:T(8,128)(2,1)}, u32[]{:S(2)}) copy-start(bf16[8,256,256]{2,1,0:T(8,128)(2,1)} %param.4) | copy-start | bytes 3145732
  7.2 76.0 %all-reduce.4.cloned.1.call-start = ((), (), s32[]{:S(2)}) async-start(), calls=%async_computation.2 | async-start | bytes 131072 | tf_op jit(solution)/shard_map/psum | solution.py:27
  12.5 78.1 %all-to-all-start.1 = ((f32[8,1,1]{2,1,0:T(1,128)}), f32[8,1,1]{2,1,0:T(1,128)S(1)}, u32[]{:S(2)}, u32[]{:S(2)}) async-start(f32[8,1,1]{2,1,0:T(1,128)} %copy.8), calls=%async_computation.1 | async-start | bytes 8192 | tf_op jit(solution)/shard_map/all_to_all | solution.py:61
  89.4 5.7 %copy-start.2 = (bf16[64,16384]{1,0:T(8,128)(2,1)S(1)}, bf16[64,16384]{1,0:T(8,128)(2,1)}, u32[]{:S(2)}) copy-start(bf16[64,16384]{1,0:T(8,128)(2,1)} %param.6) | copy-start | bytes 6291460
  90.6 19.5 %all-to-all-start = ((f32[8,64,256]{2,1,0:T(8,128)}), f32[8,64,256]{2,1,0:T(8,128)}, u32[]{:S(2)}, u32[]{:S(2)}) async-start(f32[8,64,256]{2,1,0:T(8,128)} %convolution_bitcast_fusion), calls=%async_computation | async-start | bytes 1048576 | tf_op jit(solution)/shard_map/all_to_all | solution.py:60
  95.1 22.8 %all-reduce.6.cloned.1.call-start = ((), (), s32[]{:S(2)}) async-start(), calls=%async_computation.3 | async-start | bytes 131072 | tf_op jit(solution)/shard_map/psum | solution.py:55
Sparse Core Ops, SparseCore 0:
  12.0 71.1 all-reduce.3
  98.8 19.0 all-reduce.5
where the time goes:
time: 127 us; the launch traced here: 126 us
  waiting for transfers between devices  81.1 us (64%)
  between operations  14.8 us (12%)
  starting transfers between devices  11.9 us (9%)
  other arithmetic  6.29 us (5%)
  matrix products  4.7 us (4%)
  local copies, waits for them, and re-layouts  4.35 us (3%)
  blocking collectives  3.08 us (2%)
    psum x1, waiting for transfers between devices, on_device(): column_sums = lax.psum(column_part, 'row')  63.4 us
    all_to_all x1, waiting for transfers between devices, on_device(): lax.all_to_all(partial_contribution, 'row', split_axis=0, concat_axis=0,...  12.4 us
    all_to_all x1, starting transfers between devices, on_device(): lax.all_to_all(tile_pos.astype(jnp.float32), 'row', split_axis=0, concat_...  7.28 us
    psum x1, waiting for transfers between devices, on_device(): range_sketch = lax.psum(partial_range_sketch, 'col')  5.24 us
    all_to_all x1, starting transfers between devices, on_device(): lax.all_to_all(partial_contribution, 'row', split_axis=0, concat_axis=0,...  4.54 us
    unnamed x10, local copies, waits for them, and re-layouts  3.66 us
    psum x1, blocking collectives, on_device(): row_sums = lax.psum(row_part, 'col')  3.08 us
  transfers between devices with their start and end apart: 4, of which 3 were waited for; matrix products, arithmetic and copies ran while one was open for 8% of the time, Pallas kernels for 0%

commit v1 on v0

v1 whole, which is shorter than its diff:
```python
import math

import jax
import jax.numpy as jnp
from jax import lax
from jax.experimental import pallas as pl
from jax.experimental.pallas import tpu as pltpu
from jax.sharding import PartitionSpec as P

shift_log = math.log(5.0)
LANES = 128
VMEM_LIMIT = 48 * 1024 * 1024
PARAMS = pltpu.CompilerParams(vmem_limit_bytes=VMEM_LIMIT)
SMEM = pl.BlockSpec(memory_space=pltpu.SMEM)
VMEM = pl.BlockSpec(memory_space=pltpu.VMEM)
ANY = pl.BlockSpec(memory_space=pl.ANY)

NN = (((1,), (0,)), ((), ()))
NT = (((1,), (1,)), ((), ()))


def f32(*shape):
    return jax.ShapeDtypeStruct(shape, jnp.float32)


def sums_kernel(pos_ref, counts_ref, packet_ref, row_ref):
    slots, tile, _ = counts_ref.shape
    ones = jnp.ones((8, tile), jnp.bfloat16)

    def eight(g, rows):
        columns = []
        for s in range(8):
            x = counts_ref[g * 8 + s]
            pos = pos_ref[g * 8 + s]
            live = pos >= 0
            column = lax.dot_general(ones, x, NN, preferred_element_type=jnp.float32)
            row = lax.dot_general(ones, x, NT, preferred_element_type=jnp.float32)
            at = jnp.full((1, LANES), pos.astype(jnp.float32))
            columns.append(jnp.concatenate([jnp.where(live, column[:1], 0.0), at], axis=1))
            rows = rows + jnp.where(live, row, 0.0)
        packet_ref[pl.ds(pl.multiple_of(g * 8, 8), 8), :] = jnp.concatenate(columns)
        return rows

    row_ref[...] = lax.fori_loop(0, slots // 8, eight, jnp.zeros((8, tile), jnp.float32))


def margin_kernel(blocks, me_ref, all_ref, row_ref, term_ref, swap_ref, incoming_ref):
    rows, slots, width = all_ref.shape
    tile = width - LANES

    def add(j, sums):
        value = all_ref[j, :, :tile]
        at = all_ref[j, :, tile:]
        at = jnp.concatenate([at] * (tile // LANES), axis=1)
        return tuple(sums[p] + jnp.where(at == p, value, 0.0) for p in range(blocks))

    zero = jnp.zeros((slots, tile), jnp.float32)
    sums = lax.fori_loop(0, rows, add, (zero,) * blocks, unroll=8)
    own = all_ref[0, :, tile:]
    own = jnp.concatenate([own] * (tile // LANES), axis=1)
    chosen = zero
    total = zero
    for p in range(blocks):
        power = jnp.exp(0.75 * jnp.log(jnp.maximum(sums[p], 1e-30)))
        total = total + jnp.where(sums[p] > 0.0, power, 0.0)
        chosen = chosen + jnp.where(own == p, sums[p], 0.0)
    term_ref[...] = jnp.where(own >= 0.0, -0.75 * jnp.log(jnp.maximum(chosen, 1e-30)), 0.0)
    total = sum(total[:, k * LANES : (k + 1) * LANES] for k in range(tile // LANES))
    total = sum(total[k * 8 : (k + 1) * 8] for k in range(slots // 8))
    swap_ref[:, :tile] = row_ref[...]
    swap_ref[:, tile:] = total
    mine = lax.broadcasted_iota(jnp.int32, (slots, LANES), 0) == me_ref[0]
    for j in range(rows):
        at = jnp.where(mine, all_ref[j, :, tile:], 0.0)
        incoming_ref[j : j + 1, :] = jnp.sum(at, axis=0, keepdims=True).astype(jnp.int32)


def matrix_kernel(me_ref, pos_ref, counts_ref, term_ref, mine_ref, other_ref, psi_ref, matrix_ref, *out_refs):
    slots, tile, _ = counts_ref.shape
    both = mine_ref[...] + other_ref[...]
    total = jnp.sum(both[:, tile:])
    shift = jnp.log(jnp.full((8, tile), total)) - jnp.log(both[:, :tile]) - shift_log
    shift = jnp.transpose(shift)[:, :1]

    def eight(g, carry):
        terms = term_ref[pl.ds(pl.multiple_of(g * 8, 8), 8), :]
        for k in range(8):
            s = g * 8 + k
            x = jnp.log(counts_ref[s].astype(jnp.float32))
            x = x + shift + terms[k : k + 1]
            x = jnp.where(pos_ref[s] >= 0, jnp.maximum(x, 0.0), 0.0)
            matrix_ref[s] = x.astype(jnp.bfloat16)
        return carry

    lax.fori_loop(0, slots // 8, eight, 0)
    psi = psi_ref[...]
    for k, out_ref in enumerate(out_refs):
        s = jnp.bitwise_xor(me_ref[0], k)
        out_ref[...] = lax.dot_general(psi, matrix_ref[s], NN, preferred_element_type=jnp.float32)


def range_kernel(blocks, pos_ref, matrix_ref, omega_ref, out_ref, chosen_ref, sems):
    slots, tile, _ = matrix_ref.shape

    def fetch(s):
        at = s * blocks + jnp.maximum(pos_ref[s], 0)
        columns = pl.ds(pl.multiple_of(at * tile, tile), tile)
        return pltpu.make_async_copy(omega_ref.at[:, columns], chosen_ref.at[s], sems.at[s])

    for s in range(slots):
        fetch(s).start()
    for s in range(slots):
        fetch(s).wait()
    out = jnp.zeros(out_ref.shape, jnp.float32)
    for s in range(slots):
        out = out + lax.dot_general(chosen_ref[s], matrix_ref[s], NT, preferred_element_type=jnp.float32)
    out_ref[...] = out


def place_kernel(at_ref, *refs):
    *in_refs, out_ref = refs
    tile = in_refs[0].shape[1]
    out_ref[...] = jnp.zeros_like(out_ref)
    for k, ref in enumerate(in_refs):
        p = at_ref[k, 0]

        @pl.when(p >= 0)
        def _():
            columns = pl.ds(pl.multiple_of(p * tile, tile), tile)
            out_ref[:, columns] += ref[...]


def on_device(counts, tile_pos, omega_t, psi):
    slots, tile, _ = counts.shape
    rank, width = omega_t.shape
    blocks = width // (slots * tile)
    rows = slots
    me = lax.axis_index("row").astype(jnp.int32).reshape(1)

    def row_xor(x, k):
        return lax.ppermute(x, "row", [(i, i ^ k) for i in range(rows)])

    def other_col(x):
        return lax.ppermute(x, "col", [(0, 1), (1, 0)])

    packet, row_part = pl.pallas_call(
        sums_kernel,
        out_shape=(f32(slots, tile + LANES), f32(8, tile)),
        in_specs=[SMEM, VMEM],
        out_specs=(VMEM, VMEM),
        compiler_params=PARAMS,
        name="sums",
    )(tile_pos, counts)

    gathered = packet[None]
    step = 1
    while step < rows:
        gathered = jnp.concatenate([gathered, row_xor(gathered, step)])
        step *= 2

    term, swap, incoming_at = pl.pallas_call(
        lambda *refs: margin_kernel(blocks, *refs),
        out_shape=(f32(slots, tile), f32(8, tile + LANES), jax.ShapeDtypeStruct((rows, LANES), jnp.int32)),
        in_specs=[SMEM, VMEM, VMEM],
        out_specs=(VMEM, VMEM, VMEM),
        compiler_params=PARAMS,
        name="margins",
    )(me, gathered, row_part)
    other = other_col(swap)

    matrix, *parts = pl.pallas_call(
        matrix_kernel,
        out_shape=(jax.ShapeDtypeStruct(counts.shape, jnp.bfloat16),) + (f32(rank, tile),) * rows,
        in_specs=[SMEM, SMEM] + [VMEM] * 5,
        out_specs=(VMEM,) * (rows + 1),
        compiler_params=PARAMS,
        name="matrix",
    )(me, tile_pos, counts, term, swap, other, psi)

    order = sorted(range(1, rows), key=lambda k: (-(k & -2), k))
    arrived = {0: parts[0]}
    for k in order:
        arrived[k] = row_xor(parts[k], k)

    partial_range = pl.pallas_call(
        lambda *refs: range_kernel(blocks, *refs),
        out_shape=f32(rank, tile),
        in_specs=[SMEM, VMEM, ANY],
        out_specs=VMEM,
        scratch_shapes=[pltpu.VMEM((slots, rank, tile), jnp.bfloat16), pltpu.SemaphoreType.DMA((slots,))],
        compiler_params=PARAMS,
        name="range",
    )(tile_pos, matrix, omega_t)
    range_sketch = partial_range + other_col(partial_range)

    corange = pl.pallas_call(
        place_kernel,
        out_shape=f32(rank, blocks * tile),
        in_specs=[SMEM] + [VMEM] * rows,
        out_specs=VMEM,
        compiler_params=PARAMS,
        name="place",
    )(incoming_at, *[arrived[k] for k in range(rows)])
    return (range_sketch, corange)


def solution(mesh):
    placed = (
        P(("grp", "row", "col"), None, None),
        P(("grp", "row", "col")),
        P(None, "col"),
        P(None, "row"),
    )
    return jax.shard_map(
        on_device,
        mesh=mesh,
        in_specs=placed,
        out_specs=(P(None, ("grp", "row")), P(None, ("grp", "col", "row"))),
        check_vma=False,
    )
```

time: 127 us -> 45.3 us (0.36)
  waiting for transfers between devices: 81.1 us -> 13.1 us
  between operations: 14.8 us -> 0.69 us
  starting transfers between devices: 11.9 us -> 20.1 us
  other arithmetic: 6.29 us -> 0.65 us
  Pallas kernels: 0 us -> 5.49 us
  matrix products: 4.7 us -> 0 us
  blocking collectives: 3.08 us -> 0 us
    psum x2 -> x0, waiting for transfers between devices: 68.7 us -> none  [the longest x1 63.4 us: on_device(): column_sums = lax.psum(column_part, 'row')]
    ppermute x0 -> x12, starting transfers between devices: none -> 20.1 us  [the longest x10 19.8 us: row_xor(): return lax.ppermute(x, 'row', [(i, i ^ k) for i in range(rows)])]
    ppermute x0 -> x12, waiting for transfers between devices: none -> 13.1 us  [the longest x10 12 us: row_xor(): return lax.ppermute(x, 'row', [(i, i ^ k) for i in range(rows)])]
    all_to_all x2 -> x0, waiting for transfers between devices: 12.4 us -> none  [the longest x1 12.4 us: on_device(): lax.all_to_all(partial_contribution, 'row', split_axis=0, concat_axis=0,...]
    all_to_all x2 -> x0, starting transfers between devices: 11.8 us -> none  [the longest x1 7.28 us: on_device(): lax.all_to_all(tile_pos.astype(jnp.float32), 'row', split_axis=0, concat_...]
    pallas_call x0 -> x5, Pallas kernels: none -> 5.49 us  [the longest x1 1.69 us: on_device(): pl.pallas_call(matrix_kernel, out_shape=(jax.ShapeDtypeStruct(counts.shap...]
    dot_general x5 -> x0, matrix products: 4.7 us -> none  [the longest x1 1.69 us: on_device(): jnp.einsum('sb,srt->rbt', onehot, incoming_blocks, precision=highest)]
    reduce_sum x2 -> x0, other arithmetic: 3.15 us -> none  [the longest x1 1.66 us: on_device(): row_part = jnp.sum(values, axis=(0, 2))]
  transfers between devices with their start and end apart: 4 -> 12, of which waited for: 3 -> 6; matrix products, arithmetic and copies ran while one was open for 8% -> 1% of each run, Pallas kernels for 0% -> 0%
where the time goes in v1:
time: 45.3 us; the launch traced here: 45 us
  starting transfers between devices  20.1 us (44%)
  waiting for transfers between devices  13.1 us (29%)
  Pallas kernels  5.49 us (12%)
  local copies, waits for them, and re-layouts  4.88 us (11%)
  between operations  0.69 us (2%)
  other arithmetic  0.65 us (1%)
    ppermute x10, starting transfers between devices, row_xor(): return lax.ppermute(x, 'row', [(i, i ^ k) for i in range(rows)])  19.8 us
    ppermute x10, waiting for transfers between devices, row_xor(): return lax.ppermute(x, 'row', [(i, i ^ k) for i in range(rows)])  12 us
    unnamed x12, local copies, waits for them, and re-layouts  4.88 us
    pallas_call x1, Pallas kernels, on_device(): pl.pallas_call(matrix_kernel, out_shape=(jax.ShapeDtypeStruct(counts.shap...  1.69 us
    pallas_call x1, Pallas kernels, on_device(): pl.pallas_call(place_kernel, out_shape=f32(rank, blocks * tile), in_specs...  1.5 us
    pallas_call x1, Pallas kernels, on_device(): pl.pallas_call(lambda *refs: range_kernel(blocks, *refs), out_shape=f32(r...  1.17 us
    ppermute x2, waiting for transfers between devices, other_col(): return lax.ppermute(x, 'col', [(0, 1), (1, 0)])  1.17 us
    pallas_call x1, Pallas kernels, on_device(): pl.pallas_call(sums_kernel, out_shape=(f32(slots, tile + LANES), f32(8, t...  1.04 us
  transfers between devices with their start and end apart: 12, of which 6 were waited for; matrix products, arithmetic and copies ran while one was open for 1% of the time, Pallas kernels for 0%

profile of v1, /device:TPU:0, one launch (start us, length us, event | category | flops | bytes accessed | tf_op | source)
XLA Modules:
  0.0 45.0 jit_solution(6888217639382310627)
XLA Ops:
  0.6 1.2 %copy-done = bf16[8,256,256]{2,1,0:T(8,128)(2,1)S(1)} copy-done((bf16[8,256,256]{2,1,0:T(8,128)(2,1)S(1)}, bf16[8,256,256]{2,1,0:T(8,128)(2,1)}, u32[]{:S(2)}) %copy-start) | copy-done | bytes 1048600
  1.9 0.7 %copy-done.4 = s32[8]{0:T(128)S(1)} copy-done((s32[8]{0:T(128)S(1)}, s32[8]{0:T(128)}, u32[]{:S(2)}) %copy-start.4) | copy-done | bytes 56
  2.5 1.0 %sums.1 = (f32[8,384]{1,0:T(8,128)S(1)}, f32[8,256]{1,0:T(8,128)S(1)}) custom-call(s32[8]{0:T(128)S(1)} %copy-done.4, bf16[8,256,256]{2,1,0:T(8,128)(2,1)S(1)} %copy-done), custom_call_target="tpu_custom_call" | custom-call | tf_op jit(solution)/shard_map/sums/pallas_call | solution.py:146
  3.6 3.0 %collective-permute-start = (f32[1,8,384]{2,1,0:T(8,128)S(1)}, f32[1,8,384]{2,1,0:T(8,128)S(1)}, u32[]{:S(2)}, u32[]{:S(2)}) collective-permute-start(f32[1,8,384]{2,1,0:T(8,128)S(1)} %bitcast.2), channel_id=1, source_target_pairs={{0,2},{2,0},{4,6},{6,4},{8,10},{10,8},{12,14},{14,12},{1,3},{3,1},... | collective-permute-start | bytes 36872 | tf_op jit(solution)/shard_map/ppermute | solution.py:141
  6.6 1.7 %collective-permute-done = f32[1,8,384]{2,1,0:T(8,128)S(1)} collective-permute-done((f32[1,8,384]{2,1,0:T(8,128)S(1)}, f32[1,8,384]{2,1,0:T(8,128)S(1)}, u32[]{:S(2)}, u32[]{:S(2)}) %collective-permute-start) | collective-permute-done | bytes 12320 | tf_op jit(solution)/shard_map/ppermute | solution.py:141
  8.2 2.1 %collective-permute-start.1 = (f32[2,8,384]{2,1,0:T(8,128)S(1)}, f32[2,8,384]{2,1,0:T(8,128)S(1)}, u32[]{:S(2)}, u32[]{:S(2)}) collective-permute-start(f32[2,8,384]{2,1,0:T(8,128)S(1)} %pad_maximum_fusion.2), channel_id=1, source_target_pairs={{0,4},{2,6},{4,0},{6,2},{8,12},{10,14},{12,8},{14,10},{1,5},{3,7},... | collective-permute-start | bytes 73736 | tf_op jit(solution)/shard_map/ppermute | solution.py:141
  10.3 1.8 %collective-permute-done.1 = f32[2,8,384]{2,1,0:T(8,128)S(1)} collective-permute-done((f32[2,8,384]{2,1,0:T(8,128)S(1)}, f32[2,8,384]{2,1,0:T(8,128)S(1)}, u32[]{:S(2)}, u32[]{:S(2)}) %collective-permute-start.1) | collective-permute-done | bytes 24608 | tf_op jit(solution)/shard_map/ppermute | solution.py:141
  12.1 3.0 %collective-permute-start.2 = (f32[4,8,384]{2,1,0:T(8,128)S(1)}, f32[4,8,384]{2,1,0:T(8,128)S(1)}, u32[]{:S(2)}, u32[]{:S(2)}) collective-permute-start(f32[4,8,384]{2,1,0:T(8,128)S(1)} %pad_maximum_fusion.1), channel_id=1, source_target_pairs={{0,8},{2,10},{4,12},{6,14},{8,0},{10,2},{12,4},{14,6},{1,9},{3,11}... | collective-permute-start | bytes 147464 | tf_op jit(solution)/shard_map/ppermute | solution.py:141
  15.2 2.1 %collective-permute-done.2 = f32[4,8,384]{2,1,0:T(8,128)S(1)} collective-permute-done((f32[4,8,384]{2,1,0:T(8,128)S(1)}, f32[4,8,384]{2,1,0:T(8,128)S(1)}, u32[]{:S(2)}, u32[]{:S(2)}) %collective-permute-start.2) | collective-permute-done | bytes 49184 | tf_op jit(solution)/shard_map/ppermute | solution.py:141
  17.2 0.1 margins.1
  17.3 0.1 collective-permute-start.3
  17.4 1.2 %collective-permute-done.3.other_ref = f32[8,384]{1,0:T(8,128)S(1)} collective-permute-done((f32[8,384]{1,0:T(8,128)S(1)}, f32[8,384]{1,0:T(8,128)S(1)}, u32[]{:S(2)}, u32[]{:S(2)}) %collective-permute-start.3) | collective-permute-done | bytes 12320 | tf_op jit(solution)/shard_map/ppermute | solution.py:144
  18.6 0.8 %copy-done.3 = bf16[64,256]{1,0:T(8,128)(2,1)S(1)} copy-done((bf16[64,256]{1,0:T(8,128)(2,1)S(1)}, bf16[64,256]{1,0:T(8,128)(2,1)}, u32[]{:S(2)}) %copy-start.3) | copy-done | bytes 32792
  19.3 0.7 %copy-done.5 = s32[8]{0:T(128)S(1)} copy-done((s32[8]{0:T(128)S(1)}, s32[8]{0:T(128)}, u32[]{:S(2)}) %copy-start.5) | copy-done | bytes 56
  20.0 1.7 %matrix.1 = (bf16[8,256,256]{2,1,0:T(8,128)(2,1)S(1)}, f32[64,256]{1,0:T(8,128)S(1)}, f32[64,256]{1,0:T(8,128)S(1)}, f32[64,256]{1,0:T(8,128)S(1)}, f32[64,256]{...) custom-call(s32[1]{0:T(128)} %bitcast.refs_0_.me_ref, ...), custom_call_target="tpu_custom_call" | custom-call | tf_op jit(solution)/shard_map/matrix/pallas_call | solution.py:171
  21.7 0.0 copy-start.2
  21.7 1.6 %copy-done.2 = bf16[64,16384]{1,0:T(8,128)(2,1)S(1)} copy-done((bf16[64,16384]{1,0:T(8,128)(2,1)S(1)}, bf16[64,16384]{1,0:T(8,128)(2,1)}, u32[]{:S(2)}) %copy-start.2) | copy-done | bytes 2097176
  23.3 1.2 %range.1 = f32[64,256]{1,0:T(8,128)S(1)} custom-call(s32[8]{0:T(128)S(1)} %copy-done.5, bf16[8,256,256]{2,1,0:T(8,128)(2,1)S(1)} %get-tuple-element.20.refs_1_, bf16[64,16384]{1,0:T(8,128)(2,1)S(1)} %copy-done.2), custom_call_target="tpu_custom_call" | custom-call | tf_op jit(solution)/shard_map/range/pallas_call | solution.py:185
  24.5 0.2 collective-permute-start.4
  24.7 1.9 %collective-permute-start.5 = (f32[64,256]{1,0:T(8,128)S(1)}, f32[64,256]{1,0:T(8,128)S(1)}, u32[]{:S(2)}, u32[]{:S(2)}) collective-permute-start(f32[64,256]{1,0:T(8,128)S(1)} %get-tuple-element.23), channel_id=1, source_target_pairs={{0,2},{2,0},{4,6},{6,4},{8,10},{10,8},{12,14},{14,12},{1,3},{3,1},... | collective-permute-start | bytes 196616 | tf_op jit(solution)/shard_map/ppermute | solution.py:141
  26.5 1.6 %collective-permute-start.6 = (f32[64,256]{1,0:T(8,128)S(1)}, f32[64,256]{1,0:T(8,128)S(1)}, u32[]{:S(2)}, u32[]{:S(2)}) collective-permute-start(f32[64,256]{1,0:T(8,128)S(1)} %get-tuple-element.24), channel_id=1, source_target_pairs={{0,4},{2,6},{4,0},{6,2},{8,12},{10,14},{12,8},{14,10},{1,5},{3,7},... | collective-permute-start | bytes 196616 | tf_op jit(solution)/shard_map/ppermute | solution.py:141
  28.1 0.1 collective-permute-start.7
  28.2 3.0 %collective-permute-start.8 = (f32[64,256]{1,0:T(8,128)S(1)}, f32[64,256]{1,0:T(8,128)S(1)}, u32[]{:S(2)}, u32[]{:S(2)}) collective-permute-start(f32[64,256]{1,0:T(8,128)S(1)} %get-tuple-element.26), channel_id=1, source_target_pairs={{0,8},{2,10},{4,12},{6,14},{8,0},{10,2},{12,4},{14,6},{1,9},{3,11}... | collective-permute-start | bytes 196616 | tf_op jit(solution)/shard_map/ppermute | solution.py:141
  31.1 0.0 collective-permute-done.4
  31.2 1.2 %collective-permute-start.9 = (f32[64,256]{1,0:T(8,128)S(1)}, f32[64,256]{1,0:T(8,128)S(1)}, u32[]{:S(2)}, u32[]{:S(2)}) collective-permute-start(f32[64,256]{1,0:T(8,128)S(1)} %get-tuple-element.27), channel_id=1, source_target_pairs={{0,10},{2,8},{4,14},{6,12},{8,2},{10,0},{12,6},{14,4},{1,11},{3,9}... | collective-permute-start | bytes 196616 | tf_op jit(solution)/shard_map/ppermute | solution.py:141
  32.4 4.0 %collective-permute-start.10 = (f32[64,256]{1,0:T(8,128)S(1)}, f32[64,256]{1,0:T(8,128)S(1)}, u32[]{:S(2)}, u32[]{:S(2)}) collective-permute-start(f32[64,256]{1,0:T(8,128)S(1)} %get-tuple-element.28), channel_id=1, source_target_pairs={{0,12},{2,14},{4,8},{6,10},{8,4},{10,6},{12,0},{14,2},{1,13},{3,15... | collective-permute-start | bytes 196616 | tf_op jit(solution)/shard_map/ppermute | solution.py:141
  36.4 0.0 collective-permute-start.11
  36.4 0.6 %add.3 = f32[64,256]{1,0:T(8,128)} add(f32[64,256]{1,0:T(8,128)S(1)} %range.1, f32[64,256]{1,0:T(8,128)S(1)} %collective-permute-done.4) | non-fusion elementwise | flops 16384 | bytes 196608 | tf_op jit(solution)/shard_map/add | solution.py:194
  37.1 4.6 %collective-permute-done.9.refs_5_ = f32[64,256]{1,0:T(8,128)S(1)} collective-permute-done((f32[64,256]{1,0:T(8,128)S(1)}, f32[64,256]{1,0:T(8,128)S(1)}, u32[]{:S(2)}, u32[]{:S(2)}) %collective-permute-start.9) | collective-permute-done | bytes 65568 | tf_op jit(solution)/shard_map/ppermute | solution.py:141
  41.7 0.0 collective-permute-done.10.refs_6_
  41.7 1.8 %collective-permute-done.11.refs_7_ = f32[64,256]{1,0:T(8,128)S(1)} collective-permute-done((f32[64,256]{1,0:T(8,128)S(1)}, f32[64,256]{1,0:T(8,128)S(1)}, u32[]{:S(2)}, u32[]{:S(2)}) %collective-permute-start.11) | collective-permute-done | bytes 65568 | tf_op jit(solution)/shard_map/ppermute | solution.py:141
  43.5 1.5 %place.1 = f32[64,2048]{1,0:T(8,128)} custom-call(s32[8,128]{1,0:T(8,128)S(1)} %get-tuple-element.21.at_ref, f32[64,256]{1,0:T(8,128)S(1)} %get-tuple-element.22.refs_0_, f32[64,256]{1,0:T(8,128)S(1)} %collective-permute-done.5.refs_1_, f32[64,256]{1,0:T(8,128)S(1)} %collective-permute-done.6.refs_2_, f32[64,256]{1,0:T(8,128)S(1)} %collective-permute-done.7.refs_3_, ...), custom_call_target="tpu_custom_call" | custom-call | tf_op jit(solution)/shard_map/place/pallas_call | solution.py:196
  (13 shorter events, 0.0 us)
Async XLA Ops:
  0.6 1.2 %copy-start = (bf16[8,256,256]{2,1,0:T(8,128)(2,1)S(1)}, bf16[8,256,256]{2,1,0:T(8,128)(2,1)}, u32[]{:S(2)}) copy-start(bf16[8,256,256]{2,1,0:T(8,128)(2,1)} %counts_ref.3) | copy-start | bytes 3145732
  1.9 0.7 %copy-start.4 = (s32[8]{0:T(128)S(1)}, s32[8]{0:T(128)}, u32[]{:S(2)}) copy-start(s32[8]{0:T(128)} %refs_0_.1) | copy-start | bytes 100
  2.5 16.1 %copy-start.1 = (bf16[8,256,256]{2,1,0:T(8,128)(2,1)S(1)}, bf16[8,256,256]{2,1,0:T(8,128)(2,1)}, u32[]{:S(2)}) copy-start(bf16[8,256,256]{2,1,0:T(8,128)(2,1)} %counts_ref.3) | copy-start | bytes 3145732
  3.6 4.7 %collective-permute-start = (f32[1,8,384]{2,1,0:T(8,128)S(1)}, f32[1,8,384]{2,1,0:T(8,128)S(1)}, u32[]{:S(2)}, u32[]{:S(2)}) collective-permute-start(f32[1,8,384]{2,1,0:T(8,128)S(1)} %bitcast.2), channel_id=1, source_target_pairs={{0,2},{2,0},{4,6},{6,4},{8,10},{10,8},{12,14},{14,12},{1,3},{3,1},... | collective-permute-start | bytes 36872 | tf_op jit(solution)/shard_map/ppermute | solution.py:141
  8.2 3.9 %collective-permute-start.1 = (f32[2,8,384]{2,1,0:T(8,128)S(1)}, f32[2,8,384]{2,1,0:T(8,128)S(1)}, u32[]{:S(2)}, u32[]{:S(2)}) collective-permute-start(f32[2,8,384]{2,1,0:T(8,128)S(1)} %pad_maximum_fusion.2), channel_id=1, source_target_pairs={{0,4},{2,6},{4,0},{6,2},{8,12},{10,14},{12,8},{14,10},{1,5},{3,7},... | collective-permute-start | bytes 73736 | tf_op jit(solution)/shard_map/ppermute | solution.py:141
  12.1 5.1 %collective-permute-start.2 = (f32[4,8,384]{2,1,0:T(8,128)S(1)}, f32[4,8,384]{2,1,0:T(8,128)S(1)}, u32[]{:S(2)}, u32[]{:S(2)}) collective-permute-start(f32[4,8,384]{2,1,0:T(8,128)S(1)} %pad_maximum_fusion.1), channel_id=1, source_target_pairs={{0,8},{2,10},{4,12},{6,14},{8,0},{10,2},{12,4},{14,6},{1,9},{3,11}... | collective-permute-start | bytes 147464 | tf_op jit(solution)/shard_map/ppermute | solution.py:141
  17.3 1.2 %collective-permute-start.3 = (f32[8,384]{1,0:T(8,128)S(1)}, f32[8,384]{1,0:T(8,128)S(1)}, u32[]{:S(2)}, u32[]{:S(2)}) collective-permute-start(f32[8,384]{1,0:T(8,128)S(1)} %get-tuple-element.19.mine_ref), channel_id=1, source_target_pairs={{0,1},{1,0},{2,3},{3,2},{4,5},{5,4},{6,7},{7,6},{8,9},{9,8},{10,11... | collective-permute-start | bytes 36872 | tf_op jit(solution)/shard_map/ppermute | solution.py:144
  18.6 0.8 %copy-start.3 = (bf16[64,256]{1,0:T(8,128)(2,1)S(1)}, bf16[64,256]{1,0:T(8,128)(2,1)}, u32[]{:S(2)}) copy-start(bf16[64,256]{1,0:T(8,128)(2,1)} %psi_ref.1) | copy-start | bytes 98308
  19.3 0.7 %copy-start.5 = (s32[8]{0:T(128)S(1)}, s32[8]{0:T(128)}, u32[]{:S(2)}) copy-start(s32[8]{0:T(128)} %refs_0_.1) | copy-start | bytes 100
  21.7 1.6 %copy-start.2 = (bf16[64,16384]{1,0:T(8,128)(2,1)S(1)}, bf16[64,16384]{1,0:T(8,128)(2,1)}, u32[]{:S(2)}) copy-start(bf16[64,16384]{1,0:T(8,128)(2,1)} %refs_2_.1) | copy-start | bytes 6291460
  24.5 6.7 %collective-permute-start.4 = (f32[64,256]{1,0:T(8,128)S(1)}, f32[64,256]{1,0:T(8,128)S(1)}, u32[]{:S(2)}, u32[]{:S(2)}) collective-permute-start(f32[64,256]{1,0:T(8,128)S(1)} %range.1), channel_id=1, source_target_pairs={{0,1},{1,0},{2,3},{3,2},{4,5},{5,4},{6,7},{7,6},{8,9},{9,8},{10,11... | collective-permute-start | bytes 196616 | tf_op jit(solution)/shard_map/ppermute | solution.py:144
  24.7 7.7 %collective-permute-start.5 = (f32[64,256]{1,0:T(8,128)S(1)}, f32[64,256]{1,0:T(8,128)S(1)}, u32[]{:S(2)}, u32[]{:S(2)}) collective-permute-start(f32[64,256]{1,0:T(8,128)S(1)} %get-tuple-element.23), channel_id=1, source_target_pairs={{0,2},{2,0},{4,6},{6,4},{8,10},{10,8},{12,14},{14,12},{1,3},{3,1},... | collective-permute-start | bytes 196616 | tf_op jit(solution)/shard_map/ppermute | solution.py:141
  26.5 9.9 %collective-permute-start.6 = (f32[64,256]{1,0:T(8,128)S(1)}, f32[64,256]{1,0:T(8,128)S(1)}, u32[]{:S(2)}, u32[]{:S(2)}) collective-permute-start(f32[64,256]{1,0:T(8,128)S(1)} %get-tuple-element.24), channel_id=1, source_target_pairs={{0,4},{2,6},{4,0},{6,2},{8,12},{10,14},{12,8},{14,10},{1,5},{3,7},... | collective-permute-start | bytes 196616 | tf_op jit(solution)/shard_map/ppermute | solution.py:141
  28.1 8.9 %collective-permute-start.7 = (f32[64,256]{1,0:T(8,128)S(1)}, f32[64,256]{1,0:T(8,128)S(1)}, u32[]{:S(2)}, u32[]{:S(2)}) collective-permute-start(f32[64,256]{1,0:T(8,128)S(1)} %get-tuple-element.25), channel_id=1, source_target_pairs={{0,6},{2,4},{4,2},{6,0},{8,14},{10,12},{12,10},{14,8},{1,7},{3,5},... | collective-permute-start | bytes 196616 | tf_op jit(solution)/shard_map/ppermute | solution.py:141
  28.2 8.9 %collective-permute-start.8 = (f32[64,256]{1,0:T(8,128)S(1)}, f32[64,256]{1,0:T(8,128)S(1)}, u32[]{:S(2)}, u32[]{:S(2)}) collective-permute-start(f32[64,256]{1,0:T(8,128)S(1)} %get-tuple-element.26), channel_id=1, source_target_pairs={{0,8},{2,10},{4,12},{6,14},{8,0},{10,2},{12,4},{14,6},{1,9},{3,11}... | collective-permute-start | bytes 196616 | tf_op jit(solution)/shard_map/ppermute | solution.py:141
  31.2 10.6 %collective-permute-start.9 = (f32[64,256]{1,0:T(8,128)S(1)}, f32[64,256]{1,0:T(8,128)S(1)}, u32[]{:S(2)}, u32[]{:S(2)}) collective-permute-start(f32[64,256]{1,0:T(8,128)S(1)} %get-tuple-element.27), channel_id=1, source_target_pairs={{0,10},{2,8},{4,14},{6,12},{8,2},{10,0},{12,6},{14,4},{1,11},{3,9}... | collective-permute-start | bytes 196616 | tf_op jit(solution)/shard_map/ppermute | solution.py:141
  32.4 9.3 %collective-permute-start.10 = (f32[64,256]{1,0:T(8,128)S(1)}, f32[64,256]{1,0:T(8,128)S(1)}, u32[]{:S(2)}, u32[]{:S(2)}) collective-permute-start(f32[64,256]{1,0:T(8,128)S(1)} %get-tuple-element.28), channel_id=1, source_target_pairs={{0,12},{2,14},{4,8},{6,10},{8,4},{10,6},{12,0},{14,2},{1,13},{3,15... | collective-permute-start | bytes 196616 | tf_op jit(solution)/shard_map/ppermute | solution.py:141
  36.4 7.1 %collective-permute-start.11 = (f32[64,256]{1,0:T(8,128)S(1)}, f32[64,256]{1,0:T(8,128)S(1)}, u32[]{:S(2)}, u32[]{:S(2)}) collective-permute-start(f32[64,256]{1,0:T(8,128)S(1)} %get-tuple-element.29), channel_id=1, source_target_pairs={{0,14},{2,12},{4,10},{6,8},{8,6},{10,4},{12,2},{14,0},{1,15},{3,13... | collective-permute-start | bytes 196616 | tf_op jit(solution)/shard_map/ppermute | solution.py:141

commit v2 on v0

v2 whole, which is shorter than its diff:
```python
import math

import jax
import jax.numpy as jnp
from jax import lax
from jax.experimental import pallas as pl
from jax.experimental.pallas import tpu as pltpu
from jax.sharding import PartitionSpec as P

shift_log = math.log(5.0)
LANES = 128
EMPTY = -1e30
PARAMS = pltpu.CompilerParams(vmem_limit_bytes=40 * 1024 * 1024)
VMEM = pl.BlockSpec(memory_space=pltpu.VMEM)
HBM = pl.BlockSpec(memory_space=pltpu.HBM)

NN = (((1,), (0,)), ((), ()))
NT = (((1,), (1,)), ((), ()))


def f32(*shape):
    return jax.ShapeDtypeStruct(shape, jnp.float32)


def bf16(*shape):
    return jax.ShapeDtypeStruct(shape, jnp.bfloat16)


def sums_kernel(pos_hbm, counts_hbm, packet_ref, row_ref, counts_ref, pos_ref, pos_sem, sems):
    slots, tile, _ = counts_ref.shape
    fetch_pos = pltpu.make_async_copy(pos_hbm, pos_ref, pos_sem)
    fetch_pos.start()

    def fetch(s):
        return pltpu.make_async_copy(counts_hbm.at[s], counts_ref.at[s], sems.at[s])

    for s in range(slots):
        fetch(s).start()
    fetch_pos.wait()
    ones = jnp.ones((8, tile), jnp.bfloat16)

    def eight(g, rows):
        columns = []
        for k in range(8):
            s = g * 8 + k
            fetch(s).wait()
            x = counts_ref[s]
            pos = pos_ref[s]
            live = pos >= 0
            column = lax.dot_general(ones, x, NN, preferred_element_type=jnp.float32)
            row = lax.dot_general(ones, x, NT, preferred_element_type=jnp.float32)
            at = jnp.full((1, LANES), pos.astype(jnp.float32))
            columns.append(jnp.concatenate([jnp.where(live, column[:1], 0.0), at], axis=1))
            rows = rows + jnp.where(live, row, 0.0)
        packet_ref[pl.ds(pl.multiple_of(g * 8, 8), 8), :] = jnp.concatenate(columns)
        return rows

    rows = lax.fori_loop(0, slots // 8, eight, jnp.zeros((8, tile), jnp.float32))
    row_ref[...] = jnp.concatenate([rows, jnp.zeros((8, LANES), jnp.float32)], axis=1)


def prepare_kernel(blocks, pos_hbm, counts_ref, omega_hbm, psi_hbm, logs_ref, chosen_ref, psi_ref, pos_ref, sems):
    slots, tile, _ = counts_ref.shape
    fetch_pos = pltpu.make_async_copy(pos_hbm, pos_ref, sems.at[slots])
    fetch_psi = pltpu.make_async_copy(psi_hbm, psi_ref, sems.at[slots + 1])
    fetch_pos.start()
    fetch_psi.start()
    fetch_pos.wait()

    def fetch(s):
        at = s * blocks + jnp.maximum(pos_ref[s], 0)
        columns = pl.ds(pl.multiple_of(at * tile, tile), tile)
        return pltpu.make_async_copy(omega_hbm.at[:, columns], chosen_ref.at[s], sems.at[s])

    for s in range(slots):
        fetch(s).start()

    def one(s, carry):
        x = counts_ref[s].astype(jnp.float32)
        logs_ref[s] = jnp.log(jnp.where(pos_ref[s] >= 0, x, 1.0))
        return carry

    lax.fori_loop(0, slots, one, 0)
    for s in range(slots):
        fetch(s).wait()
    fetch_psi.wait()


def odd(r):
    return bin(r).count("1") % 2


def matrix_kernel(blocks, mine_ref, other_ref, logs_ref, psi_ref, matrix_ref, incoming_ref, *out_refs):
    slots, tile, _ = logs_ref.shape
    rows = slots
    wide = tile // LANES

    def column_sums(swapped):
        sums = [jnp.zeros((slots, tile), jnp.float32)] * blocks
        for r in range(rows):
            ref = other_ref if odd(r) != swapped else mine_ref
            value = ref[r * slots : (r + 1) * slots, :tile]
            at = ref[r * slots : (r + 1) * slots, tile:]
            at = jnp.concatenate([at] * wide, axis=1)
            sums = [s + jnp.where(at == p, value, 0.0) for p, s in enumerate(sums)]
        return sums

    def smooth_total(sums):
        total = jnp.zeros((slots, tile), jnp.float32)
        for s in sums:
            power = jnp.exp(0.75 * jnp.log(jnp.maximum(s, 1e-30)))
            total = total + jnp.where(s > 0.0, power, 0.0)
        return jnp.sum(total)

    sums = column_sums(False)
    first, second = smooth_total(sums), smooth_total(column_sums(True))
    total = first + second
    own = mine_ref[:slots, tile:]
    own = jnp.concatenate([own] * wide, axis=1)
    chosen = jnp.zeros((slots, tile), jnp.float32)
    for p in range(blocks):
        chosen = chosen + jnp.where(own == p, sums[p], 0.0)
    terms = jnp.where(own >= 0.0, -0.75 * jnp.log(jnp.maximum(chosen, 1e-30)), EMPTY)

    me = lax.axis_index("row")
    mine = lax.broadcasted_iota(jnp.int32, (slots, LANES), 0) == me
    for r in range(rows):
        ref = other_ref if odd(r) else mine_ref
        at = jnp.where(mine, ref[r * slots : (r + 1) * slots, tile:], 0.0)
        incoming_ref[r : r + 1, :] = jnp.sum(at, axis=0, keepdims=True).astype(jnp.int32)

    both = mine_ref[rows * slots :, :tile] + other_ref[rows * slots :, :tile]
    shift = jnp.log(jnp.full((8, tile), total)) - jnp.log(both) - shift_log
    shift = jnp.transpose(shift)[:, :1]

    for s in range(slots):
        x = logs_ref[s] + shift + terms[s : s + 1]
        matrix_ref[s] = jnp.maximum(x, 0.0).astype(jnp.bfloat16)
    psi = psi_ref[...]
    for k, out_ref in enumerate(out_refs):
        s = jnp.bitwise_xor(me, k)
        out_ref[...] = lax.dot_general(psi, matrix_ref[s], NN, preferred_element_type=jnp.float32)


def place(at_ref, refs, first, out_ref):
    tile = refs[0].shape[1]
    for k, ref in zip(first, refs, strict=True):
        p = at_ref[k, 0]

        @pl.when(p >= 0)
        def _():
            columns = pl.ds(pl.multiple_of(p * tile, tile), tile)
            out_ref[:, columns] += ref[...]


def early_kernel(order, at_ref, matrix_ref, chosen_ref, *refs):
    *in_refs, range_ref, out_ref = refs
    out = jnp.zeros(range_ref.shape, jnp.float32)
    for s in range(matrix_ref.shape[0]):
        out = out + lax.dot_general(chosen_ref[s], matrix_ref[s], NT, preferred_element_type=jnp.float32)
    range_ref[...] = out
    out_ref[...] = jnp.zeros_like(out_ref)
    place(at_ref, in_refs, order, out_ref)


def late_kernel(order, at_ref, early_ref, mine_ref, other_ref, *refs):
    *in_refs, range_hbm, out_hbm, range_ref, out_ref, sems = refs
    out_ref[...] = early_ref[...]
    place(at_ref, in_refs, order, out_ref)
    range_ref[...] = mine_ref[...] + other_ref[...]
    rank = out_ref.shape[0]
    copies = [pltpu.make_async_copy(range_ref, range_hbm, sems.at[rank // 8])]
    for k in range(rank // 8):
        some = pl.ds(k * 8, 8)
        copies.append(pltpu.make_async_copy(out_ref.at[some], out_hbm.at[some], sems.at[k]))
    for copy in copies:
        copy.start()
    for copy in copies:
        copy.wait()


def on_device(counts, tile_pos, omega_t, psi):
    slots, tile, _ = counts.shape
    rank, width = omega_t.shape
    blocks = width // (slots * tile)
    rows = slots
    DMA = pltpu.SemaphoreType.DMA

    def call(kernel, name, outs, ins, out_specs=None, scratch=(), cost=None):
        return pl.pallas_call(
            kernel,
            out_shape=outs,
            in_specs=ins,
            out_specs=out_specs or (VMEM,) * len(outs),
            scratch_shapes=scratch,
            compiler_params=PARAMS,
            cost_estimate=cost,
            name=name,
        )

    def row_xor(x, k):
        return lax.ppermute(x, "row", [(i, i ^ k) for i in range(rows)])

    def across(x, k):
        pairs = [(2 * i + c, 2 * (i ^ k) + 1 - c) for i in range(rows) for c in range(2)]
        return lax.ppermute(x, ("row", "col"), pairs)

    def other_col(x):
        return lax.ppermute(x, "col", [(0, 1), (1, 0)])

    counts, tile_pos, omega_t, psi = (
        pltpu.with_memory_space_constraint(x, pltpu.HBM) for x in (counts, tile_pos, omega_t, psi)
    )
    packet, row_part, held = call(
        sums_kernel,
        "sums",
        (f32(slots, tile + LANES), f32(8, tile + LANES), bf16(slots, tile, tile)),
        [HBM, HBM],
        scratch=[pltpu.SMEM((slots,), jnp.int32), DMA(()), DMA((slots,))],
    )(tile_pos, counts)

    logs, chosen, held_psi = call(
        lambda *refs: prepare_kernel(blocks, *refs),
        "prepare",
        (f32(slots, tile, tile), bf16(slots, rank, tile), bf16(*psi.shape)),
        [HBM, VMEM, HBM, HBM],
        scratch=[pltpu.SMEM((slots,), jnp.int32), DMA((slots + 2,))],
        cost=pl.CostEstimate(flops=40 * counts.size, bytes_accessed=6 * counts.size, transcendentals=counts.size),
    )(tile_pos, held, omega_t, psi)

    gathered = packet
    step = 1
    while step < rows:
        gathered = jnp.concatenate([gathered, across(gathered, step)])
        step *= 2
    gathered = jnp.concatenate([gathered, row_part])
    gathered, logs, chosen, held_psi = lax.optimization_barrier((gathered, logs, chosen, held_psi))
    other = other_col(gathered)

    matrix, incoming_at, *parts = call(
        lambda *refs: matrix_kernel(blocks, *refs),
        "matrix",
        (bf16(*counts.shape), jax.ShapeDtypeStruct((rows, LANES), jnp.int32)) + (f32(rank, tile),) * rows,
        [VMEM] * 4,
    )(gathered, other, logs, held_psi)

    order = sorted(range(1, rows), key=lambda k: (-(k & -2), k))
    arrived = [row_xor(parts[k], k) for k in order]
    half = (rows - 1) // 2
    at = pl.BlockSpec(memory_space=pltpu.SMEM)

    partial_range, early = call(
        lambda *refs: early_kernel([0] + order[:half], *refs),
        "early",
        (f32(rank, tile), f32(rank, blocks * tile)),
        [at] + [VMEM] * (3 + half),
    )(incoming_at, matrix, chosen, parts[0], *arrived[:half])
    other_range = other_col(partial_range)
    return call(
        lambda *refs: late_kernel(order[half:], *refs),
        "late",
        (f32(rank, tile), f32(rank, blocks * tile)),
        [at] + [VMEM] * (3 + rows - 1 - half),
        out_specs=(HBM, HBM),
        scratch=[pltpu.VMEM((rank, tile), jnp.float32), pltpu.VMEM((rank, blocks * tile), jnp.float32), DMA((rank // 8 + 1,))],
    )(incoming_at, early, partial_range, other_range, *arrived[half:])


def solution(mesh):
    placed = (
        P(("grp", "row", "col"), None, None),
        P(("grp", "row", "col")),
        P(None, "col"),
        P(None, "row"),
    )
    return jax.shard_map(
        on_device,
        mesh=mesh,
        in_specs=placed,
        out_specs=(P(None, ("grp", "row")), P(None, ("grp", "col", "row"))),
        check_vma=False,
    )
```

time: 127 us -> 38.4 us (0.30)
  waiting for transfers between devices: 81.1 us -> 7.82 us
  between operations: 14.8 us -> 0.71 us
  starting transfers between devices: 11.9 us -> 21.4 us
  Pallas kernels: 0 us -> 8.11 us
  other arithmetic: 6.29 us -> 0.01 us
  matrix products: 4.7 us -> 0 us
  local copies, waits for them, and re-layouts: 4.35 us -> 0.01 us
  blocking collectives: 3.08 us -> 0 us
    psum x2 -> x0, waiting for transfers between devices: 68.7 us -> none  [the longest x1 63.4 us: on_device(): column_sums = lax.psum(column_part, 'row')]
    ppermute x0 -> x12, starting transfers between devices: none -> 21.4 us  [the longest x7 13.7 us: row_xor(): return lax.ppermute(x, 'row', [(i, i ^ k) for i in range(rows)])]
    all_to_all x2 -> x0, waiting for transfers between devices: 12.4 us -> none  [the longest x1 12.4 us: on_device(): lax.all_to_all(partial_contribution, 'row', split_axis=0, concat_axis=0,...]
    all_to_all x2 -> x0, starting transfers between devices: 11.8 us -> none  [the longest x1 7.28 us: on_device(): lax.all_to_all(tile_pos.astype(jnp.float32), 'row', split_axis=0, concat_...]
    pallas_call x0 -> x5, Pallas kernels: none -> 8.11 us  [the longest x1 2.75 us: on_device(): call(sums_kernel, 'sums', (f32(slots, tile + LANES), f32(8, tile + LANES)...]
    ppermute x0 -> x12, waiting for transfers between devices: none -> 7.82 us  [the longest x3 3.29 us: across(): return lax.ppermute(x, ('row', 'col'), pairs)]
    dot_general x5 -> x0, matrix products: 4.7 us -> none  [the longest x1 1.69 us: on_device(): jnp.einsum('sb,srt->rbt', onehot, incoming_blocks, precision=highest)]
    unnamed x10 -> x4, local copies, waits for them, and re-layouts: 3.66 us -> 0.01 us
  transfers between devices with their start and end apart: 4 -> 12, of which waited for: 3 -> 8; matrix products, arithmetic and copies ran while one was open for 8% -> 0% of each run, Pallas kernels for 0% -> 7%
where the time goes in v2:
time: 38.4 us; the launch traced here: 38.1 us
  starting transfers between devices  21.4 us (56%)
  Pallas kernels  8.11 us (21%)
  waiting for transfers between devices  7.82 us (20%)
  between operations  0.71 us (2%)
    ppermute x7, starting transfers between devices, row_xor(): return lax.ppermute(x, 'row', [(i, i ^ k) for i in range(rows)])  13.7 us
    ppermute x3, starting transfers between devices, across(): return lax.ppermute(x, ('row', 'col'), pairs)  7.14 us
    ppermute x3, waiting for transfers between devices, across(): return lax.ppermute(x, ('row', 'col'), pairs)  3.29 us
    ppermute x7, waiting for transfers between devices, row_xor(): return lax.ppermute(x, 'row', [(i, i ^ k) for i in range(rows)])  3.2 us
    pallas_call x1, Pallas kernels, on_device(): call(sums_kernel, 'sums', (f32(slots, tile + LANES), f32(8, tile + LANES)...  2.75 us
    pallas_call x1, Pallas kernels, on_device(): call(lambda *refs: prepare_kernel(blocks, *refs), 'prepare', (f32(slots,...  1.63 us
    pallas_call x1, Pallas kernels, on_device(): call(lambda *refs: late_kernel(order[half:], *refs), 'late', (f32(rank, t...  1.56 us
    ppermute x2, waiting for transfers between devices, other_col(): return lax.ppermute(x, 'col', [(0, 1), (1, 0)])  1.34 us
  transfers between devices with their start and end apart: 12, of which 8 were waited for; matrix products, arithmetic and copies ran while one was open for 0% of the time, Pallas kernels for 7%

profile of v2, /device:TPU:0, one launch (start us, length us, event | category | flops | bytes accessed | tf_op | source)
XLA Modules:
  0.0 38.1 jit_solution(14479998569096300141)
XLA Ops:
  0.6 2.7 %sums.1 = (f32[8,384]{1,0:T(8,128)S(1)}, f32[8,384]{1,0:T(8,128)S(1)}, bf16[8,256,256]{2,1,0:T(8,128)(2,1)S(1)}) custom-call(s32[8]{0:T(128)} %refs_0_.1, bf16[8,256,256]{2,1,0:T(8,128)(2,1)} %counts_hbm.1), custom_call_target="tpu_custom_call" | custom-call | tf_op jit(solution)/shard_map/sums/pallas_call | solution.py:214
  3.4 2.5 %collective-permute-start = (f32[8,384]{1,0:T(8,128)S(1)}, f32[8,384]{1,0:T(8,128)S(1)}, u32[]{:S(2)}, u32[]{:S(2)}) collective-permute-start(f32[8,384]{1,0:T(8,128)S(1)} %get-tuple-element.24), channel_id=1, source_target_pairs={{0,3},{1,2},{2,1},{3,0},{4,7},{5,6},{6,5},{7,4},{8,11},{9,10},{10,... | collective-permute-start | bytes 36872 | tf_op jit(solution)/shard_map/ppermute | solution.py:206
  5.9 1.6 %prepare.1 = (f32[8,256,256]{2,1,0:T(8,128)S(1)}, bf16[8,64,256]{2,1,0:T(8,128)(2,1)S(1)}, bf16[64,256]{1,0:T(8,128)(2,1)S(1)}) custom-call(s32[8]{0:T(128)} %refs_0_.1, bf16[8,256,256]{2,1,0:T(8,128)(2,1)S(1)} %get-tuple-element.26.refs_1_, bf16[64,16384]{1,0:T(8,128)(2,1)} %refs_2_.1, bf16[64,256]{1,0:T(8,128)(2,1)} %refs_3_.1), custom_call_target="tpu_custom_call" | custom-call | flops 20971520 | bytes 3145728 | tf_op jit(solution)/shard_map/prepare/pallas_call | solution.py:222
  7.5 0.0 collective-permute-done
  7.5 1.9 %collective-permute-start.1 = (f32[16,384]{1,0:T(8,128)S(1)}, f32[16,384]{1,0:T(8,128)S(1)}, u32[]{:S(2)}, u32[]{:S(2)}) collective-permute-start(f32[16,384]{1,0:T(8,128)S(1)} %pad_maximum_fusion.1), channel_id=1, source_target_pairs={{0,5},{1,4},{2,7},{3,6},{4,1},{5,0},{6,3},{7,2},{8,13},{9,12},{10,... | collective-permute-start | bytes 73736 | tf_op jit(solution)/shard_map/ppermute | solution.py:206
  9.5 1.5 %collective-permute-done.1 = f32[16,384]{1,0:T(8,128)S(1)} collective-permute-done((f32[16,384]{1,0:T(8,128)S(1)}, f32[16,384]{1,0:T(8,128)S(1)}, u32[]{:S(2)}, u32[]{:S(2)}) %collective-permute-start.1) | collective-permute-done | bytes 24608 | tf_op jit(solution)/shard_map/ppermute | solution.py:206
  11.0 2.7 %collective-permute-start.2 = (f32[32,384]{1,0:T(8,128)S(1)}, f32[32,384]{1,0:T(8,128)S(1)}, u32[]{:S(2)}, u32[]{:S(2)}) collective-permute-start(f32[32,384]{1,0:T(8,128)S(1)} %pad_maximum_fusion), channel_id=1, source_target_pairs={{0,9},{1,8},{2,11},{3,10},{4,13},{5,12},{6,15},{7,14},{8,1},{9,0},... | collective-permute-start | bytes 147464 | tf_op jit(solution)/shard_map/ppermute | solution.py:206
  13.7 1.8 %collective-permute-done.2 = f32[32,384]{1,0:T(8,128)S(1)} collective-permute-done((f32[32,384]{1,0:T(8,128)S(1)}, f32[32,384]{1,0:T(8,128)S(1)}, u32[]{:S(2)}, u32[]{:S(2)}) %collective-permute-start.2) | collective-permute-done | bytes 49184 | tf_op jit(solution)/shard_map/ppermute | solution.py:206
  15.5 0.5 %collective-permute-start.3 = (f32[72,384]{1,0:T(8,128)S(1)}, f32[72,384]{1,0:T(8,128)S(1)}, u32[]{:S(2)}, u32[]{:S(2)}) collective-permute-start(f32[72,384]{1,0:T(8,128)S(1)} %constant_dynamic-update-slice_fusion.refs_0_), channel_id=1, source_target_pairs={{0,1},{1,0},{2,3},{3,2},{4,5},{5,4},{6,7},{7,6},{8,9},{9,8},{10,11... | collective-permute-start | bytes 331784 | tf_op jit(solution)/shard_map/ppermute | solution.py:209
  16.0 1.0 %collective-permute-done.3.refs_1_ = f32[72,384]{1,0:T(8,128)S(1)} collective-permute-done((f32[72,384]{1,0:T(8,128)S(1)}, f32[72,384]{1,0:T(8,128)S(1)}, u32[]{:S(2)}, u32[]{:S(2)}) %collective-permute-start.3) | collective-permute-done | bytes 110624 | tf_op jit(solution)/shard_map/ppermute | solution.py:209
  17.0 1.1 %matrix.1 = (bf16[8,256,256]{2,1,0:T(8,128)(2,1)S(1)}, s32[8,128]{1,0:T(8,128)S(1)}, f32[64,256]{1,0:T(8,128)S(1)}, f32[64,256]{1,0:T(8,128)S(1)}, f32[64,256]{1...) custom-call(f32[72,384]{1,0:T(8,128)S(1)} %constant_dynamic-update-s, ...), custom_call_target="tpu_custom_call" | custom-call | tf_op jit(solution)/shard_map/matrix/pallas_call | solution.py:240
  18.1 5.3 %collective-permute-start.4 = (f32[64,256]{1,0:T(8,128)S(1)}, f32[64,256]{1,0:T(8,128)S(1)}, u32[]{:S(2)}, u32[]{:S(2)}) collective-permute-start(f32[64,256]{1,0:T(8,128)S(1)} %get-tuple-element.37), channel_id=1, source_target_pairs={{0,12},{2,14},{4,8},{6,10},{8,4},{10,6},{12,0},{14,2},{1,13},{3,15... | collective-permute-start | bytes 196616 | tf_op jit(solution)/shard_map/ppermute | solution.py:202
  23.4 1.1 %collective-permute-start.5 = (f32[64,256]{1,0:T(8,128)S(1)}, f32[64,256]{1,0:T(8,128)S(1)}, u32[]{:S(2)}, u32[]{:S(2)}) collective-permute-start(f32[64,256]{1,0:T(8,128)S(1)} %get-tuple-element.38), channel_id=1, source_target_pairs={{0,14},{2,12},{4,10},{6,8},{8,6},{10,4},{12,2},{14,0},{1,15},{3,13... | collective-permute-start | bytes 196616 | tf_op jit(solution)/shard_map/ppermute | solution.py:202
  24.5 0.0 collective-permute-start.6
  24.5 2.8 %collective-permute-start.8 = (f32[64,256]{1,0:T(8,128)S(1)}, f32[64,256]{1,0:T(8,128)S(1)}, u32[]{:S(2)}, u32[]{:S(2)}) collective-permute-start(f32[64,256]{1,0:T(8,128)S(1)} %get-tuple-element.42), channel_id=1, source_target_pairs={{0,10},{2,8},{4,14},{6,12},{8,2},{10,0},{12,6},{14,4},{1,11},{3,9}... | collective-permute-start | bytes 196616 | tf_op jit(solution)/shard_map/ppermute | solution.py:202
  27.3 1.5 %collective-permute-start.9 = (f32[64,256]{1,0:T(8,128)S(1)}, f32[64,256]{1,0:T(8,128)S(1)}, u32[]{:S(2)}, u32[]{:S(2)}) collective-permute-start(f32[64,256]{1,0:T(8,128)S(1)} %get-tuple-element.43), channel_id=1, source_target_pairs={{0,4},{2,6},{4,0},{6,2},{8,12},{10,14},{12,8},{14,10},{1,5},{3,7},... | collective-permute-start | bytes 196616 | tf_op jit(solution)/shard_map/ppermute | solution.py:202
  28.8 0.0 collective-permute-done.4.refs_4_
  28.8 1.5 %collective-permute-start.10 = (f32[64,256]{1,0:T(8,128)S(1)}, f32[64,256]{1,0:T(8,128)S(1)}, u32[]{:S(2)}, u32[]{:S(2)}) collective-permute-start(f32[64,256]{1,0:T(8,128)S(1)} %get-tuple-element.44), channel_id=1, source_target_pairs={{0,6},{2,4},{4,2},{6,0},{8,14},{10,12},{12,10},{14,8},{1,7},{3,5},... | collective-permute-start | bytes 196616 | tf_op jit(solution)/shard_map/ppermute | solution.py:202
  30.3 0.5 %collective-permute-done.5.refs_5_ = f32[64,256]{1,0:T(8,128)S(1)} collective-permute-done((f32[64,256]{1,0:T(8,128)S(1)}, f32[64,256]{1,0:T(8,128)S(1)}, u32[]{:S(2)}, u32[]{:S(2)}) %collective-permute-start.5) | collective-permute-done | bytes 65568 | tf_op jit(solution)/shard_map/ppermute | solution.py:202
  30.8 1.5 %collective-permute-start.11 = (f32[64,256]{1,0:T(8,128)S(1)}, f32[64,256]{1,0:T(8,128)S(1)}, u32[]{:S(2)}, u32[]{:S(2)}) collective-permute-start(f32[64,256]{1,0:T(8,128)S(1)} %get-tuple-element.45), channel_id=1, source_target_pairs={{0,2},{2,0},{4,6},{6,4},{8,10},{10,8},{12,14},{14,12},{1,3},{3,1},... | collective-permute-start | bytes 196616 | tf_op jit(solution)/shard_map/ppermute | solution.py:202
  32.3 1.8 %collective-permute-done.6.refs_6_ = f32[64,256]{1,0:T(8,128)S(1)} collective-permute-done((f32[64,256]{1,0:T(8,128)S(1)}, f32[64,256]{1,0:T(8,128)S(1)}, u32[]{:S(2)}, u32[]{:S(2)}) %collective-permute-start.6) | collective-permute-done | bytes 65568 | tf_op jit(solution)/shard_map/ppermute | solution.py:202
  34.1 1.1 %early.1 = (f32[64,256]{1,0:T(8,128)S(1)}, f32[64,2048]{1,0:T(8,128)S(1)}) custom-call(s32[8,128]{1,0:T(8,128)S(1)} %get-tuple-element.33.refs_0_, bf16[8,256,256]{2,1,0:T(8,128)(2,1)S(1)} %get-tuple-element.34.refs_1_, bf16[8,64,256]{2,1,0:T(8,128)(2,1)S(1)} %get-tuple-element.35.refs_2_, f32[64,256]{1,0:T(8,128)S(1)} %get-tuple-element.36.refs_3_, ...), custom_call_target="tpu_custom_call" | custom-call | tf_op jit(solution)/shard_map/early/pallas_call | solution.py:252
  35.2 0.1 collective-permute-start.7
  35.3 0.0 collective-permute-done.8.refs_4_
  35.3 0.0 collective-permute-done.9.refs_5_
  35.3 0.4 %collective-permute-done.10.refs_6_ = f32[64,256]{1,0:T(8,128)S(1)} collective-permute-done((f32[64,256]{1,0:T(8,128)S(1)}, f32[64,256]{1,0:T(8,128)S(1)}, u32[]{:S(2)}, u32[]{:S(2)}) %collective-permute-start.10) | collective-permute-done | bytes 65568 | tf_op jit(solution)/shard_map/ppermute | solution.py:202
  35.7 0.4 %collective-permute-done.11.refs_7_ = f32[64,256]{1,0:T(8,128)S(1)} collective-permute-done((f32[64,256]{1,0:T(8,128)S(1)}, f32[64,256]{1,0:T(8,128)S(1)}, u32[]{:S(2)}, u32[]{:S(2)}) %collective-permute-start.11) | collective-permute-done | bytes 65568 | tf_op jit(solution)/shard_map/ppermute | solution.py:202
  36.2 0.4 collective-permute-done.7.refs_3_
  36.5 1.6 %late.1 = (f32[64,256]{1,0:T(8,128)}, f32[64,2048]{1,0:T(8,128)}) custom-call(s32[8,128]{1,0:T(8,128)S(1)} %get-tuple-element.33.refs_0_, f32[64,2048]{1,0:T(8,128)S(1)} %get-tuple-element.40.refs_1_, f32[64,256]{1,0:T(8,128)S(1)} %get-tuple-element.41.refs_2_, f32[64,256]{1,0:T(8,128)S(1)} %collective-permute-done.7.refs_3_, ...), custom_call_target="tpu_custom_call" | custom-call | tf_op jit(solution)/shard_map/late/pallas_call | solution.py:259
  (7 shorter events, 0.0 us)
Async XLA Ops:
  3.4 4.1 %collective-permute-start = (f32[8,384]{1,0:T(8,128)S(1)}, f32[8,384]{1,0:T(8,128)S(1)}, u32[]{:S(2)}, u32[]{:S(2)}) collective-permute-start(f32[8,384]{1,0:T(8,128)S(1)} %get-tuple-element.24), channel_id=1, source_target_pairs={{0,3},{1,2},{2,1},{3,0},{4,7},{5,6},{6,5},{7,4},{8,11},{9,10},{10,... | collective-permute-start | bytes 36872 | tf_op jit(solution)/shard_map/ppermute | solution.py:206
  7.5 3.5 %collective-permute-start.1 = (f32[16,384]{1,0:T(8,128)S(1)}, f32[16,384]{1,0:T(8,128)S(1)}, u32[]{:S(2)}, u32[]{:S(2)}) collective-permute-start(f32[16,384]{1,0:T(8,128)S(1)} %pad_maximum_fusion.1), channel_id=1, source_target_pairs={{0,5},{1,4},{2,7},{3,6},{4,1},{5,0},{6,3},{7,2},{8,13},{9,12},{10,... | collective-permute-start | bytes 73736 | tf_op jit(solution)/shard_map/ppermute | solution.py:206
  11.0 4.5 %collective-permute-start.2 = (f32[32,384]{1,0:T(8,128)S(1)}, f32[32,384]{1,0:T(8,128)S(1)}, u32[]{:S(2)}, u32[]{:S(2)}) collective-permute-start(f32[32,384]{1,0:T(8,128)S(1)} %pad_maximum_fusion), channel_id=1, source_target_pairs={{0,9},{1,8},{2,11},{3,10},{4,13},{5,12},{6,15},{7,14},{8,1},{9,0},... | collective-permute-start | bytes 147464 | tf_op jit(solution)/shard_map/ppermute | solution.py:206
  15.5 1.5 %collective-permute-start.3 = (f32[72,384]{1,0:T(8,128)S(1)}, f32[72,384]{1,0:T(8,128)S(1)}, u32[]{:S(2)}, u32[]{:S(2)}) collective-permute-start(f32[72,384]{1,0:T(8,128)S(1)} %constant_dynamic-update-slice_fusion.refs_0_), channel_id=1, source_target_pairs={{0,1},{1,0},{2,3},{3,2},{4,5},{5,4},{6,7},{7,6},{8,9},{9,8},{10,11... | collective-permute-start | bytes 331784 | tf_op jit(solution)/shard_map/ppermute | solution.py:209
  18.1 10.7 %collective-permute-start.4 = (f32[64,256]{1,0:T(8,128)S(1)}, f32[64,256]{1,0:T(8,128)S(1)}, u32[]{:S(2)}, u32[]{:S(2)}) collective-permute-start(f32[64,256]{1,0:T(8,128)S(1)} %get-tuple-element.37), channel_id=1, source_target_pairs={{0,12},{2,14},{4,8},{6,10},{8,4},{10,6},{12,0},{14,2},{1,13},{3,15... | collective-permute-start | bytes 196616 | tf_op jit(solution)/shard_map/ppermute | solution.py:202
  23.4 7.5 %collective-permute-start.5 = (f32[64,256]{1,0:T(8,128)S(1)}, f32[64,256]{1,0:T(8,128)S(1)}, u32[]{:S(2)}, u32[]{:S(2)}) collective-permute-start(f32[64,256]{1,0:T(8,128)S(1)} %get-tuple-element.38), channel_id=1, source_target_pairs={{0,14},{2,12},{4,10},{6,8},{8,6},{10,4},{12,2},{14,0},{1,15},{3,13... | collective-permute-start | bytes 196616 | tf_op jit(solution)/shard_map/ppermute | solution.py:202
  24.5 9.7 %collective-permute-start.6 = (f32[64,256]{1,0:T(8,128)S(1)}, f32[64,256]{1,0:T(8,128)S(1)}, u32[]{:S(2)}, u32[]{:S(2)}) collective-permute-start(f32[64,256]{1,0:T(8,128)S(1)} %get-tuple-element.39), channel_id=1, source_target_pairs={{0,8},{2,10},{4,12},{6,14},{8,0},{10,2},{12,4},{14,6},{1,9},{3,11}... | collective-permute-start | bytes 196616 | tf_op jit(solution)/shard_map/ppermute | solution.py:202
  24.5 10.8 %collective-permute-start.8 = (f32[64,256]{1,0:T(8,128)S(1)}, f32[64,256]{1,0:T(8,128)S(1)}, u32[]{:S(2)}, u32[]{:S(2)}) collective-permute-start(f32[64,256]{1,0:T(8,128)S(1)} %get-tuple-element.42), channel_id=1, source_target_pairs={{0,10},{2,8},{4,14},{6,12},{8,2},{10,0},{12,6},{14,4},{1,11},{3,9}... | collective-permute-start | bytes 196616 | tf_op jit(solution)/shard_map/ppermute | solution.py:202
  27.3 8.0 %collective-permute-start.9 = (f32[64,256]{1,0:T(8,128)S(1)}, f32[64,256]{1,0:T(8,128)S(1)}, u32[]{:S(2)}, u32[]{:S(2)}) collective-permute-start(f32[64,256]{1,0:T(8,128)S(1)} %get-tuple-element.43), channel_id=1, source_target_pairs={{0,4},{2,6},{4,0},{6,2},{8,12},{10,14},{12,8},{14,10},{1,5},{3,7},... | collective-permute-start | bytes 196616 | tf_op jit(solution)/shard_map/ppermute | solution.py:202
  28.8 7.0 %collective-permute-start.10 = (f32[64,256]{1,0:T(8,128)S(1)}, f32[64,256]{1,0:T(8,128)S(1)}, u32[]{:S(2)}, u32[]{:S(2)}) collective-permute-start(f32[64,256]{1,0:T(8,128)S(1)} %get-tuple-element.44), channel_id=1, source_target_pairs={{0,6},{2,4},{4,2},{6,0},{8,14},{10,12},{12,10},{14,8},{1,7},{3,5},... | collective-permute-start | bytes 196616 | tf_op jit(solution)/shard_map/ppermute | solution.py:202
  30.8 5.3 %collective-permute-start.11 = (f32[64,256]{1,0:T(8,128)S(1)}, f32[64,256]{1,0:T(8,128)S(1)}, u32[]{:S(2)}, u32[]{:S(2)}) collective-permute-start(f32[64,256]{1,0:T(8,128)S(1)} %get-tuple-element.45), channel_id=1, source_target_pairs={{0,2},{2,0},{4,6},{6,4},{8,10},{10,8},{12,14},{14,12},{1,3},{3,1},... | collective-permute-start | bytes 196616 | tf_op jit(solution)/shard_map/ppermute | solution.py:202
  35.2 1.3 %collective-permute-start.7 = (f32[64,256]{1,0:T(8,128)S(1)}, f32[64,256]{1,0:T(8,128)S(1)}, u32[]{:S(2)}, u32[]{:S(2)}) collective-permute-start(f32[64,256]{1,0:T(8,128)S(1)} %get-tuple-element.41.refs_2_), channel_id=1, source_target_pairs={{0,1},{1,0},{2,3},{3,2},{4,5},{5,4},{6,7},{7,6},{8,9},{9,8},{10,11... | collective-permute-start | bytes 196616 | tf_op jit(solution)/shard_map/ppermute | solution.py:209

commit v3 on v2

--- a/solution.py
+++ b/solution.py
@@ -30,33 +30,25 @@
     slots, tile, _ = counts_ref.shape
     fetch_pos = pltpu.make_async_copy(pos_hbm, pos_ref, pos_sem)
     fetch_pos.start()
-
-    def fetch(s):
-        return pltpu.make_async_copy(counts_hbm.at[s], counts_ref.at[s], sems.at[s])
-
-    for s in range(slots):
-        fetch(s).start()
+    fetches = [pltpu.make_async_copy(counts_hbm.at[s], counts_ref.at[s], sems.at[s]) for s in range(slots)]
+    for fetch in fetches:
+        fetch.start()
     fetch_pos.wait()
-    ones = jnp.ones((8, tile), jnp.bfloat16)
-
-    def eight(g, rows):
+
+    values = jnp.zeros((tile, tile), jnp.float32)
+    for g in range(0, slots, 8):
         columns = []
-        for k in range(8):
-            s = g * 8 + k
-            fetch(s).wait()
-            x = counts_ref[s]
-            pos = pos_ref[s]
-            live = pos >= 0
-            column = lax.dot_general(ones, x, NN, preferred_element_type=jnp.float32)
-            row = lax.dot_general(ones, x, NT, preferred_element_type=jnp.float32)
-            at = jnp.full((1, LANES), pos.astype(jnp.float32))
-            columns.append(jnp.concatenate([jnp.where(live, column[:1], 0.0), at], axis=1))
-            rows = rows + jnp.where(live, row, 0.0)
-        packet_ref[pl.ds(pl.multiple_of(g * 8, 8), 8), :] = jnp.concatenate(columns)
-        return rows
-
-    rows = lax.fori_loop(0, slots // 8, eight, jnp.zeros((8, tile), jnp.float32))
-    row_ref[...] = jnp.concatenate([rows, jnp.zeros((8, LANES), jnp.float32)], axis=1)
+        for s in range(g, g + 8):
+            fetches[s].wait()
+            x = jnp.where(pos_ref[s] >= 0, counts_ref[s].astype(jnp.float32), 0.0)
+            at = jnp.full((1, LANES), pos_ref[s].astype(jnp.float32))
+            columns.append(jnp.concatenate([jnp.sum(x, axis=0, keepdims=True), at], axis=1))
+            values = values + x
+        packet_ref[g : g + 8, :] = jnp.concatenate(columns)
+    narrow = sum(values[:, k : k + LANES] for k in range(0, tile, LANES))
+    rows = jnp.sum(jnp.transpose(narrow), axis=0, keepdims=True)
+    row_ref[:, :tile] = jnp.broadcast_to(rows, (8, tile))
+    row_ref[:, tile:] = jnp.zeros((8, LANES), jnp.float32)
 
 
 def prepare_kernel(blocks, pos_hbm, counts_ref, omega_hbm, psi_hbm, logs_ref, chosen_ref, psi_ref, pos_ref, sems):
@@ -86,21 +78,22 @@
     fetch_psi.wait()
 
 
-def odd(r):
-    return bin(r).count("1") % 2
-
-
-def matrix_kernel(blocks, mine_ref, other_ref, logs_ref, psi_ref, matrix_ref, incoming_ref, *out_refs):
+def stages(rows):
+    bits = [1 << k for k in range(2, rows.bit_length() - 1)]
+    return [[(1, 1), (2, 1), (3, 0)]] + [[(bit, 1)] for bit in bits]
+
+
+def matrix_kernel(blocks, offsets, mine_ref, other_ref, logs_ref, psi_ref, matrix_ref, incoming_ref, *out_refs):
     slots, tile, _ = logs_ref.shape
     rows = slots
     wide = tile // LANES
 
     def column_sums(swapped):
         sums = [jnp.zeros((slots, tile), jnp.float32)] * blocks
-        for r in range(rows):
-            ref = other_ref if odd(r) != swapped else mine_ref
-            value = ref[r * slots : (r + 1) * slots, :tile]
-            at = ref[r * slots : (r + 1) * slots, tile:]
+        for k, (_, c) in enumerate(offsets):
+            ref = other_ref if c != swapped else mine_ref
+            value = ref[k * slots : (k + 1) * slots, :tile]
+            at = ref[k * slots : (k + 1) * slots, tile:]
             at = jnp.concatenate([at] * wide, axis=1)
             sums = [s + jnp.where(at == p, value, 0.0) for p, s in enumerate(sums)]
         return sums
@@ -112,8 +105,8 @@
             total = total + jnp.where(s > 0.0, power, 0.0)
         return jnp.sum(total)
 
-    sums = column_sums(False)
-    first, second = smooth_total(sums), smooth_total(column_sums(True))
+    sums = column_sums(0)
+    first, second = smooth_total(sums), smooth_total(column_sums(1))
     total = first + second
     own = mine_ref[:slots, tile:]
     own = jnp.concatenate([own] * wide, axis=1)
@@ -124,9 +117,9 @@
 
     me = lax.axis_index("row")
     mine = lax.broadcasted_iota(jnp.int32, (slots, LANES), 0) == me
-    for r in range(rows):
-        ref = other_ref if odd(r) else mine_ref
-        at = jnp.where(mine, ref[r * slots : (r + 1) * slots, tile:], 0.0)
+    for k, (r, c) in enumerate(offsets):
+        ref = other_ref if c else mine_ref
+        at = jnp.where(mine, ref[k * slots : (k + 1) * slots, tile:], 0.0)
         incoming_ref[r : r + 1, :] = jnp.sum(at, axis=0, keepdims=True).astype(jnp.int32)
 
     both = mine_ref[rows * slots :, :tile] + other_ref[rows * slots :, :tile]
@@ -144,13 +137,10 @@
 
 def place(at_ref, refs, first, out_ref):
     tile = refs[0].shape[1]
-    for k, ref in zip(first, refs, strict=True):
-        p = at_ref[k, 0]
-
-        @pl.when(p >= 0)
-        def _():
-            columns = pl.ds(pl.multiple_of(p * tile, tile), tile)
-            out_ref[:, columns] += ref[...]
+    at = [jnp.max(at_ref[k : k + 1, :]) for k in first]
+    for p, ref in zip(at, refs, strict=True):
+        columns = pl.ds(pl.multiple_of(jnp.maximum(p, 0) * tile, tile), tile)
+        out_ref[:, columns] += jnp.where(p >= 0, ref[...], 0.0)
 
 
 def early_kernel(order, at_ref, matrix_ref, chosen_ref, *refs):
@@ -201,8 +191,8 @@
     def row_xor(x, k):
         return lax.ppermute(x, "row", [(i, i ^ k) for i in range(rows)])
 
-    def across(x, k):
-        pairs = [(2 * i + c, 2 * (i ^ k) + 1 - c) for i in range(rows) for c in range(2)]
+    def across(x, k, odd):
+        pairs = [(2 * i + c, 2 * (i ^ k) + (c ^ odd)) for i in range(rows) for c in range(2)]
         return lax.ppermute(x, ("row", "col"), pairs)
 
     def other_col(x):
@@ -229,38 +219,38 @@
     )(tile_pos, held, omega_t, psi)
 
     gathered = packet
-    step = 1
-    while step < rows:
-        gathered = jnp.concatenate([gathered, across(gathered, step)])
-        step *= 2
+    offsets = [(0, 0)]
+    for stage in stages(rows):
+        sent = [across(gathered, k, odd) for k, odd in stage]
+        gathered = jnp.concatenate([gathered] + sent)
+        offsets += [(r ^ k, c ^ odd) for k, odd in stage for r, c in offsets]
     gathered = jnp.concatenate([gathered, row_part])
     gathered, logs, chosen, held_psi = lax.optimization_barrier((gathered, logs, chosen, held_psi))
     other = other_col(gathered)
 
     matrix, incoming_at, *parts = call(
-        lambda *refs: matrix_kernel(blocks, *refs),
+        lambda *refs: matrix_kernel(blocks, offsets, *refs),
         "matrix",
         (bf16(*counts.shape), jax.ShapeDtypeStruct((rows, LANES), jnp.int32)) + (f32(rank, tile),) * rows,
         [VMEM] * 4,
     )(gathered, other, logs, held_psi)
 
-    order = sorted(range(1, rows), key=lambda k: (-(k & -2), k))
+    order = list(range(rows - 1, 0, -1))
     arrived = [row_xor(parts[k], k) for k in order]
-    half = (rows - 1) // 2
-    at = pl.BlockSpec(memory_space=pltpu.SMEM)
+    half = 2
 
     partial_range, early = call(
         lambda *refs: early_kernel([0] + order[:half], *refs),
         "early",
         (f32(rank, tile), f32(rank, blocks * tile)),
-        [at] + [VMEM] * (3 + half),
+        [VMEM] * (4 + half),
     )(incoming_at, matrix, chosen, parts[0], *arrived[:half])
     other_range = other_col(partial_range)
     return call(
         lambda *refs: late_kernel(order[half:], *refs),
         "late",
         (f32(rank, tile), f32(rank, blocks * tile)),
-        [at] + [VMEM] * (3 + rows - 1 - half),
+        [VMEM] * (4 + rows - 1 - half),
         out_specs=(HBM, HBM),
         scratch=[pltpu.VMEM((rank, tile), jnp.float32), pltpu.VMEM((rank, blocks * tile), jnp.float32), DMA((rank // 8 + 1,))],
     )(incoming_at, early, partial_range, other_range, *arrived[half:])

time: 38.4 us -> 34.6 us (0.901)
  Pallas kernels: 8.11 us -> 5.89 us
  starting transfers between devices: 21.4 us -> 19.2 us
  waiting for transfers between devices: 7.82 us -> 8.49 us
    ppermute x7, starting transfers between devices: 13.7 us -> 10.5 us  [row_xor(): return lax.ppermute(x, 'row', [(i, i ^ k) for i in range(rows)])]
    ppermute x7, waiting for transfers between devices: 3.2 us -> 4.65 us  [row_xor(): return lax.ppermute(x, 'row', [(i, i ^ k) for i in range(rows)])]
    pallas_call x1, Pallas kernels: 2.75 us -> 1.6 us  [on_device(): call(sums_kernel, 'sums', (f32(slots, tile + LANES), f32(8, tile + LANES)...]
    ppermute x2, starting transfers between devices: 0.58 us -> 1.57 us  [other_col(): return lax.ppermute(x, 'col', [(0, 1), (1, 0)])]
    pallas_call x1, Pallas kernels: 1.06 us -> 0.45 us  [on_device(): call(lambda *refs: early_kernel([0] + order[:half], *refs), 'early', (f32...]
    pallas_call x1, Pallas kernels: 1.56 us -> 1.11 us  [on_device(): call(lambda *refs: late_kernel(order[half:], *refs), 'late', (f32(rank, t...]
    ppermute x3 -> x4, waiting for transfers between devices: 3.29 us -> 2.87 us  [across(): return lax.ppermute(x, ('row', 'col'), pairs)]
    ppermute x3 -> x4, starting transfers between devices: 7.14 us -> 7.16 us  [across(): return lax.ppermute(x, ('row', 'col'), pairs)]
  transfers between devices with their start and end apart: 12 -> 13, of which waited for: 8 -> 7; matrix products, arithmetic and copies ran while one was open for 0% -> 0% of each run, Pallas kernels for 7% -> 6%
where the time goes in v3:
time: 34.6 us; the launch traced here: 34.3 us
  starting transfers between devices  19.2 us (55%)
  waiting for transfers between devices  8.49 us (25%)
  Pallas kernels  5.89 us (17%)
  between operations  0.68 us (2%)
    ppermute x7, starting transfers between devices, row_xor(): return lax.ppermute(x, 'row', [(i, i ^ k) for i in range(rows)])  10.5 us
    ppermute x4, starting transfers between devices, across(): return lax.ppermute(x, ('row', 'col'), pairs)  7.16 us
    ppermute x7, waiting for transfers between devices, row_xor(): return lax.ppermute(x, 'row', [(i, i ^ k) for i in range(rows)])  4.65 us
    ppermute x4, waiting for transfers between devices, across(): return lax.ppermute(x, ('row', 'col'), pairs)  2.87 us
    pallas_call x1, Pallas kernels, on_device(): call(lambda *refs: prepare_kernel(blocks, *refs), 'prepare', (f32(slots,...  1.63 us
    pallas_call x1, Pallas kernels, on_device(): call(sums_kernel, 'sums', (f32(slots, tile + LANES), f32(8, tile + LANES)...  1.6 us
    ppermute x2, starting transfers between devices, other_col(): return lax.ppermute(x, 'col', [(0, 1), (1, 0)])  1.57 us
    pallas_call x1, Pallas kernels, on_device(): call(lambda *refs: late_kernel(order[half:], *refs), 'late', (f32(rank, t...  1.11 us
  transfers between devices with their start and end apart: 13, of which 7 were waited for; matrix products, arithmetic and copies ran while one was open for 0% of the time, Pallas kernels for 6%

profile of v3, /device:TPU:0, one launch (start us, length us, event | category | flops | bytes accessed | tf_op | source)
XLA Modules:
  0.0 34.3 jit_solution(10563825860139072678)
XLA Ops:
  0.6 1.6 %sums.1 = (f32[8,384]{1,0:T(8,128)S(1)}, f32[8,384]{1,0:T(8,128)S(1)}, bf16[8,256,256]{2,1,0:T(8,128)(2,1)S(1)}) custom-call(s32[8]{0:T(128)} %refs_0_.1, bf16[8,256,256]{2,1,0:T(8,128)(2,1)} %counts_hbm.1), custom_call_target="tpu_custom_call" | custom-call | tf_op jit(solution)/shard_map/sums/pallas_call | solution.py:204
  2.2 4.0 %collective-permute-start.2 = (f32[8,384]{1,0:T(8,128)S(1)}, f32[8,384]{1,0:T(8,128)S(1)}, u32[]{:S(2)}, u32[]{:S(2)}) collective-permute-start(f32[8,384]{1,0:T(8,128)S(1)} %get-tuple-element.24), channel_id=1, source_target_pairs={{0,6},{1,7},{2,4},{3,5},{4,2},{5,3},{6,0},{7,1},{8,14},{9,15},{10,... | collective-permute-start | bytes 36872 | tf_op jit(solution)/shard_map/ppermute | solution.py:196
  6.3 0.0 collective-permute-start.1
  6.3 0.4 %collective-permute-start = (f32[8,384]{1,0:T(8,128)S(1)}, f32[8,384]{1,0:T(8,128)S(1)}, u32[]{:S(2)}, u32[]{:S(2)}) collective-permute-start(f32[8,384]{1,0:T(8,128)S(1)} %get-tuple-element.24), channel_id=1, source_target_pairs={{0,3},{1,2},{2,1},{3,0},{4,7},{5,6},{6,5},{7,4},{8,11},{9,10},{10,... | collective-permute-start | bytes 36872 | tf_op jit(solution)/shard_map/ppermute | solution.py:196
  6.6 1.6 %prepare.1 = (f32[8,256,256]{2,1,0:T(8,128)S(1)}, bf16[8,64,256]{2,1,0:T(8,128)(2,1)S(1)}, bf16[64,256]{1,0:T(8,128)(2,1)S(1)}) custom-call(s32[8]{0:T(128)} %refs_0_.1, bf16[8,256,256]{2,1,0:T(8,128)(2,1)S(1)} %get-tuple-element.26.refs_1_, bf16[64,16384]{1,0:T(8,128)(2,1)} %refs_2_.1, bf16[64,256]{1,0:T(8,128)(2,1)} %refs_3_.1), custom_call_target="tpu_custom_call" | custom-call | flops 20971520 | bytes 3145728 | tf_op jit(solution)/shard_map/prepare/pallas_call | solution.py:212
  8.3 0.0 collective-permute-done.2
  8.3 1.1 %collective-permute-done.1 = f32[8,384]{1,0:T(8,128)S(1)} collective-permute-done((f32[8,384]{1,0:T(8,128)S(1)}, f32[8,384]{1,0:T(8,128)S(1)}, u32[]{:S(2)}, u32[]{:S(2)}) %collective-permute-start.1) | collective-permute-done | bytes 12320 | tf_op jit(solution)/shard_map/ppermute | solution.py:196
  9.4 0.0 collective-permute-done
  9.4 2.8 %collective-permute-start.3 = (f32[32,384]{1,0:T(8,128)S(1)}, f32[32,384]{1,0:T(8,128)S(1)}, u32[]{:S(2)}, u32[]{:S(2)}) collective-permute-start(f32[32,384]{1,0:T(8,128)S(1)} %pad_maximum_fusion), channel_id=1, source_target_pairs={{0,9},{1,8},{2,11},{3,10},{4,13},{5,12},{6,15},{7,14},{8,1},{9,0},... | collective-permute-start | bytes 147464 | tf_op jit(solution)/shard_map/ppermute | solution.py:196
  12.2 1.8 %collective-permute-done.3 = f32[32,384]{1,0:T(8,128)S(1)} collective-permute-done((f32[32,384]{1,0:T(8,128)S(1)}, f32[32,384]{1,0:T(8,128)S(1)}, u32[]{:S(2)}, u32[]{:S(2)}) %collective-permute-start.3) | collective-permute-done | bytes 49184 | tf_op jit(solution)/shard_map/ppermute | solution.py:196
  14.0 1.6 %collective-permute-start.4 = (f32[72,384]{1,0:T(8,128)S(1)}, f32[72,384]{1,0:T(8,128)S(1)}, u32[]{:S(2)}, u32[]{:S(2)}) collective-permute-start(f32[72,384]{1,0:T(8,128)S(1)} %constant_dynamic-update-slice_fusion.refs_0_), channel_id=1, source_target_pairs={{0,1},{1,0},{2,3},{3,2},{4,5},{5,4},{6,7},{7,6},{8,9},{9,8},{10,11... | collective-permute-start | bytes 331784 | tf_op jit(solution)/shard_map/ppermute | solution.py:199
  15.5 1.0 %collective-permute-done.4.refs_1_ = f32[72,384]{1,0:T(8,128)S(1)} collective-permute-done((f32[72,384]{1,0:T(8,128)S(1)}, f32[72,384]{1,0:T(8,128)S(1)}, u32[]{:S(2)}, u32[]{:S(2)}) %collective-permute-start.4) | collective-permute-done | bytes 110624 | tf_op jit(solution)/shard_map/ppermute | solution.py:199
  16.5 1.1 %matrix.1 = (bf16[8,256,256]{2,1,0:T(8,128)(2,1)S(1)}, s32[8,128]{1,0:T(8,128)S(1)}, f32[64,256]{1,0:T(8,128)S(1)}, f32[64,256]{1,0:T(8,128)S(1)}, f32[64,256]{1...) custom-call(f32[72,384]{1,0:T(8,128)S(1)} %constant_dynamic-update-s, ...), custom_call_target="tpu_custom_call" | custom-call | tf_op jit(solution)/shard_map/matrix/pallas_call | solution.py:231
  17.6 4.1 %collective-permute-start.5 = (f32[64,256]{1,0:T(8,128)S(1)}, f32[64,256]{1,0:T(8,128)S(1)}, u32[]{:S(2)}, u32[]{:S(2)}) collective-permute-start(f32[64,256]{1,0:T(8,128)S(1)} %get-tuple-element.37), channel_id=1, source_target_pairs={{0,14},{2,12},{4,10},{6,8},{8,6},{10,4},{12,2},{14,0},{1,15},{3,13... | collective-permute-start | bytes 196616 | tf_op jit(solution)/shard_map/ppermute | solution.py:192
  21.7 0.0 collective-permute-start.6
  21.7 0.4 %collective-permute-start.8 = (f32[64,256]{1,0:T(8,128)S(1)}, f32[64,256]{1,0:T(8,128)S(1)}, u32[]{:S(2)}, u32[]{:S(2)}) collective-permute-start(f32[64,256]{1,0:T(8,128)S(1)} %get-tuple-element.41), channel_id=1, source_target_pairs={{0,10},{2,8},{4,14},{6,12},{8,2},{10,0},{12,6},{14,4},{1,11},{3,9}... | collective-permute-start | bytes 196616 | tf_op jit(solution)/shard_map/ppermute | solution.py:192
  22.1 3.2 %collective-permute-start.9 = (f32[64,256]{1,0:T(8,128)S(1)}, f32[64,256]{1,0:T(8,128)S(1)}, u32[]{:S(2)}, u32[]{:S(2)}) collective-permute-start(f32[64,256]{1,0:T(8,128)S(1)} %get-tuple-element.42), channel_id=1, source_target_pairs={{0,8},{2,10},{4,12},{6,14},{8,0},{10,2},{12,4},{14,6},{1,9},{3,11}... | collective-permute-start | bytes 196616 | tf_op jit(solution)/shard_map/ppermute | solution.py:192
  25.3 1.7 %collective-permute-start.10 = (f32[64,256]{1,0:T(8,128)S(1)}, f32[64,256]{1,0:T(8,128)S(1)}, u32[]{:S(2)}, u32[]{:S(2)}) collective-permute-start(f32[64,256]{1,0:T(8,128)S(1)} %get-tuple-element.43), channel_id=1, source_target_pairs={{0,6},{2,4},{4,2},{6,0},{8,14},{10,12},{12,10},{14,8},{1,7},{3,5},... | collective-permute-start | bytes 196616 | tf_op jit(solution)/shard_map/ppermute | solution.py:192
  27.0 0.0 collective-permute-done.5.refs_4_
  27.0 0.6 %collective-permute-start.11 = (f32[64,256]{1,0:T(8,128)S(1)}, f32[64,256]{1,0:T(8,128)S(1)}, u32[]{:S(2)}, u32[]{:S(2)}) collective-permute-start(f32[64,256]{1,0:T(8,128)S(1)} %get-tuple-element.44), channel_id=1, source_target_pairs={{0,4},{2,6},{4,0},{6,2},{8,12},{10,14},{12,8},{14,10},{1,5},{3,7},... | collective-permute-start | bytes 196616 | tf_op jit(solution)/shard_map/ppermute | solution.py:192
  27.5 0.7 %collective-permute-done.6.refs_5_ = f32[64,256]{1,0:T(8,128)S(1)} collective-permute-done((f32[64,256]{1,0:T(8,128)S(1)}, f32[64,256]{1,0:T(8,128)S(1)}, u32[]{:S(2)}, u32[]{:S(2)}) %collective-permute-start.6) | collective-permute-done | bytes 65568 | tf_op jit(solution)/shard_map/ppermute | solution.py:192
  28.2 0.6 %collective-permute-start.12 = (f32[64,256]{1,0:T(8,128)S(1)}, f32[64,256]{1,0:T(8,128)S(1)}, u32[]{:S(2)}, u32[]{:S(2)}) collective-permute-start(f32[64,256]{1,0:T(8,128)S(1)} %get-tuple-element.45), channel_id=1, source_target_pairs={{0,2},{2,0},{4,6},{6,4},{8,10},{10,8},{12,14},{14,12},{1,3},{3,1},... | collective-permute-start | bytes 196616 | tf_op jit(solution)/shard_map/ppermute | solution.py:192
  28.8 0.4 %early.1 = (f32[64,256]{1,0:T(8,128)S(1)}, f32[64,2048]{1,0:T(8,128)S(1)}) custom-call(s32[8,128]{1,0:T(8,128)S(1)} %get-tuple-element.33.refs_0_, bf16[8,256,256]{2,1,0:T(8,128)(2,1)S(1)} %get-tuple-element.34.refs_1_, bf16[8,64,256]{2,1,0:T(8,128)(2,1)S(1)} %get-tuple-element.35.refs_2_, f32[64,256]{1,0:T(8,128)S(1)} %get-tuple-element.36.refs_3_, ...), custom_call_target="tpu_custom_call" | custom-call | tf_op jit(solution)/shard_map/early/pallas_call | solution.py:242
  29.3 2.0 %collective-permute-done.8.refs_4_ = f32[64,256]{1,0:T(8,128)S(1)} collective-permute-done((f32[64,256]{1,0:T(8,128)S(1)}, f32[64,256]{1,0:T(8,128)S(1)}, u32[]{:S(2)}, u32[]{:S(2)}) %collective-permute-start.8) | collective-permute-done | bytes 65568 | tf_op jit(solution)/shard_map/ppermute | solution.py:192
  31.2 0.0 collective-permute-start.7
  31.2 1.5 %collective-permute-done.9.refs_5_ = f32[64,256]{1,0:T(8,128)S(1)} collective-permute-done((f32[64,256]{1,0:T(8,128)S(1)}, f32[64,256]{1,0:T(8,128)S(1)}, u32[]{:S(2)}, u32[]{:S(2)}) %collective-permute-start.9) | collective-permute-done | bytes 65568 | tf_op jit(solution)/shard_map/ppermute | solution.py:192
  32.7 0.0 collective-permute-done.10.refs_6_
  32.8 0.5 %collective-permute-done.11.refs_7_ = f32[64,256]{1,0:T(8,128)S(1)} collective-permute-done((f32[64,256]{1,0:T(8,128)S(1)}, f32[64,256]{1,0:T(8,128)S(1)}, u32[]{:S(2)}, u32[]{:S(2)}) %collective-permute-start.11) | collective-permute-done | bytes 65568 | tf_op jit(solution)/shard_map/ppermute | solution.py:192
  33.2 0.0 collective-permute-done.12.refs_8_
  33.2 0.0 collective-permute-done.7.refs_3_
  33.2 1.1 %late.1 = (f32[64,256]{1,0:T(8,128)}, f32[64,2048]{1,0:T(8,128)}) custom-call(s32[8,128]{1,0:T(8,128)S(1)} %get-tuple-element.33.refs_0_, f32[64,2048]{1,0:T(8,128)S(1)} %get-tuple-element.39.refs_1_, f32[64,256]{1,0:T(8,128)S(1)} %get-tuple-element.40.refs_2_, f32[64,256]{1,0:T(8,128)S(1)} %collective-permute-done.7.refs_3_, ...), custom_call_target="tpu_custom_call" | custom-call | tf_op jit(solution)/shard_map/late/pallas_call | solution.py:249
  (7 shorter events, 0.0 us)
Async XLA Ops:
  2.2 6.1 %collective-permute-start.2 = (f32[8,384]{1,0:T(8,128)S(1)}, f32[8,384]{1,0:T(8,128)S(1)}, u32[]{:S(2)}, u32[]{:S(2)}) collective-permute-start(f32[8,384]{1,0:T(8,128)S(1)} %get-tuple-element.24), channel_id=1, source_target_pairs={{0,6},{1,7},{2,4},{3,5},{4,2},{5,3},{6,0},{7,1},{8,14},{9,15},{10,... | collective-permute-start | bytes 36872 | tf_op jit(solution)/shard_map/ppermute | solution.py:196
  6.3 3.1 %collective-permute-start.1 = (f32[8,384]{1,0:T(8,128)S(1)}, f32[8,384]{1,0:T(8,128)S(1)}, u32[]{:S(2)}, u32[]{:S(2)}) collective-permute-start(f32[8,384]{1,0:T(8,128)S(1)} %get-tuple-element.24), channel_id=1, source_target_pairs={{0,5},{1,4},{2,7},{3,6},{4,1},{5,0},{6,3},{7,2},{8,13},{9,12},{10,... | collective-permute-start | bytes 36872 | tf_op jit(solution)/shard_map/ppermute | solution.py:196
  6.3 3.1 %collective-permute-start = (f32[8,384]{1,0:T(8,128)S(1)}, f32[8,384]{1,0:T(8,128)S(1)}, u32[]{:S(2)}, u32[]{:S(2)}) collective-permute-start(f32[8,384]{1,0:T(8,128)S(1)} %get-tuple-element.24), channel_id=1, source_target_pairs={{0,3},{1,2},{2,1},{3,0},{4,7},{5,6},{6,5},{7,4},{8,11},{9,10},{10,... | collective-permute-start | bytes 36872 | tf_op jit(solution)/shard_map/ppermute | solution.py:196
  9.4 4.5 %collective-permute-start.3 = (f32[32,384]{1,0:T(8,128)S(1)}, f32[32,384]{1,0:T(8,128)S(1)}, u32[]{:S(2)}, u32[]{:S(2)}) collective-permute-start(f32[32,384]{1,0:T(8,128)S(1)} %pad_maximum_fusion), channel_id=1, source_target_pairs={{0,9},{1,8},{2,11},{3,10},{4,13},{5,12},{6,15},{7,14},{8,1},{9,0},... | collective-permute-start | bytes 147464 | tf_op jit(solution)/shard_map/ppermute | solution.py:196
  14.0 2.5 %collective-permute-start.4 = (f32[72,384]{1,0:T(8,128)S(1)}, f32[72,384]{1,0:T(8,128)S(1)}, u32[]{:S(2)}, u32[]{:S(2)}) collective-permute-start(f32[72,384]{1,0:T(8,128)S(1)} %constant_dynamic-update-slice_fusion.refs_0_), channel_id=1, source_target_pairs={{0,1},{1,0},{2,3},{3,2},{4,5},{5,4},{6,7},{7,6},{8,9},{9,8},{10,11... | collective-permute-start | bytes 331784 | tf_op jit(solution)/shard_map/ppermute | solution.py:199
  17.6 9.4 %collective-permute-start.5 = (f32[64,256]{1,0:T(8,128)S(1)}, f32[64,256]{1,0:T(8,128)S(1)}, u32[]{:S(2)}, u32[]{:S(2)}) collective-permute-start(f32[64,256]{1,0:T(8,128)S(1)} %get-tuple-element.37), channel_id=1, source_target_pairs={{0,14},{2,12},{4,10},{6,8},{8,6},{10,4},{12,2},{14,0},{1,15},{3,13... | collective-permute-start | bytes 196616 | tf_op jit(solution)/shard_map/ppermute | solution.py:192
  21.7 6.6 %collective-permute-start.6 = (f32[64,256]{1,0:T(8,128)S(1)}, f32[64,256]{1,0:T(8,128)S(1)}, u32[]{:S(2)}, u32[]{:S(2)}) collective-permute-start(f32[64,256]{1,0:T(8,128)S(1)} %get-tuple-element.38), channel_id=1, source_target_pairs={{0,12},{2,14},{4,8},{6,10},{8,4},{10,6},{12,0},{14,2},{1,13},{3,15... | collective-permute-start | bytes 196616 | tf_op jit(solution)/shard_map/ppermute | solution.py:192
  21.7 9.5 %collective-permute-start.8 = (f32[64,256]{1,0:T(8,128)S(1)}, f32[64,256]{1,0:T(8,128)S(1)}, u32[]{:S(2)}, u32[]{:S(2)}) collective-permute-start(f32[64,256]{1,0:T(8,128)S(1)} %get-tuple-element.41), channel_id=1, source_target_pairs={{0,10},{2,8},{4,14},{6,12},{8,2},{10,0},{12,6},{14,4},{1,11},{3,9}... | collective-permute-start | bytes 196616 | tf_op jit(solution)/shard_map/ppermute | solution.py:192
  22.1 10.6 %collective-permute-start.9 = (f32[64,256]{1,0:T(8,128)S(1)}, f32[64,256]{1,0:T(8,128)S(1)}, u32[]{:S(2)}, u32[]{:S(2)}) collective-permute-start(f32[64,256]{1,0:T(8,128)S(1)} %get-tuple-element.42), channel_id=1, source_target_pairs={{0,8},{2,10},{4,12},{6,14},{8,0},{10,2},{12,4},{14,6},{1,9},{3,11}... | collective-permute-start | bytes 196616 | tf_op jit(solution)/shard_map/ppermute | solution.py:192
  25.3 7.4 %collective-permute-start.10 = (f32[64,256]{1,0:T(8,128)S(1)}, f32[64,256]{1,0:T(8,128)S(1)}, u32[]{:S(2)}, u32[]{:S(2)}) collective-permute-start(f32[64,256]{1,0:T(8,128)S(1)} %get-tuple-element.43), channel_id=1, source_target_pairs={{0,6},{2,4},{4,2},{6,0},{8,14},{10,12},{12,10},{14,8},{1,7},{3,5},... | collective-permute-start | bytes 196616 | tf_op jit(solution)/shard_map/ppermute | solution.py:192
  27.0 6.2 %collective-permute-start.11 = (f32[64,256]{1,0:T(8,128)S(1)}, f32[64,256]{1,0:T(8,128)S(1)}, u32[]{:S(2)}, u32[]{:S(2)}) collective-permute-start(f32[64,256]{1,0:T(8,128)S(1)} %get-tuple-element.44), channel_id=1, source_target_pairs={{0,4},{2,6},{4,0},{6,2},{8,12},{10,14},{12,8},{14,10},{1,5},{3,7},... | collective-permute-start | bytes 196616 | tf_op jit(solution)/shard_map/ppermute | solution.py:192
  28.2 5.0 %collective-permute-start.12 = (f32[64,256]{1,0:T(8,128)S(1)}, f32[64,256]{1,0:T(8,128)S(1)}, u32[]{:S(2)}, u32[]{:S(2)}) collective-permute-start(f32[64,256]{1,0:T(8,128)S(1)} %get-tuple-element.45), channel_id=1, source_target_pairs={{0,2},{2,0},{4,6},{6,4},{8,10},{10,8},{12,14},{14,12},{1,3},{3,1},... | collective-permute-start | bytes 196616 | tf_op jit(solution)/shard_map/ppermute | solution.py:192
  31.2 2.0 %collective-permute-start.7 = (f32[64,256]{1,0:T(8,128)S(1)}, f32[64,256]{1,0:T(8,128)S(1)}, u32[]{:S(2)}, u32[]{:S(2)}) collective-permute-start(f32[64,256]{1,0:T(8,128)S(1)} %get-tuple-element.40.refs_2_), channel_id=1, source_target_pairs={{0,1},{1,0},{2,3},{3,2},{4,5},{5,4},{6,7},{7,6},{8,9},{9,8},{10,11... | collective-permute-start | bytes 196616 | tf_op jit(solution)/shard_map/ppermute | solution.py:199

commit v4 on v3

--- a/solution.py
+++ b/solution.py
@@ -83,6 +83,13 @@
     return [[(1, 1), (2, 1), (3, 0)]] + [[(bit, 1)] for bit in bits]
 
 
+def send_order(rows):
+    half = rows // 2
+    far, near = list(range(rows - 1, half - 1, -1)), list(range(half - 1, 0, -1))
+    late = [k for pair in zip(near, far[2:]) for k in pair]
+    return far[:2] + late + near[len(far) - 2 :]
+
+
 def matrix_kernel(blocks, offsets, mine_ref, other_ref, logs_ref, psi_ref, matrix_ref, incoming_ref, *out_refs):
     slots, tile, _ = logs_ref.shape
     rows = slots
@@ -209,6 +216,13 @@
         scratch=[pltpu.SMEM((slots,), jnp.int32), DMA(()), DMA((slots,))],
     )(tile_pos, counts)
 
+    gathered = packet
+    offsets = [(0, 0)]
+    for stage in stages(rows):
+        gathered, held = lax.optimization_barrier((gathered, held))
+        sent = [across(gathered, k, odd) for k, odd in stage]
+        gathered = jnp.concatenate([gathered] + sent)
+        offsets += [(r ^ k, c ^ odd) for k, odd in stage for r, c in offsets]
     logs, chosen, held_psi = call(
         lambda *refs: prepare_kernel(blocks, *refs),
         "prepare",
@@ -218,12 +232,6 @@
         cost=pl.CostEstimate(flops=40 * counts.size, bytes_accessed=6 * counts.size, transcendentals=counts.size),
     )(tile_pos, held, omega_t, psi)
 
-    gathered = packet
-    offsets = [(0, 0)]
-    for stage in stages(rows):
-        sent = [across(gathered, k, odd) for k, odd in stage]
-        gathered = jnp.concatenate([gathered] + sent)
-        offsets += [(r ^ k, c ^ odd) for k, odd in stage for r, c in offsets]
     gathered = jnp.concatenate([gathered, row_part])
     gathered, logs, chosen, held_psi = lax.optimization_barrier((gathered, logs, chosen, held_psi))
     other = other_col(gathered)
@@ -235,7 +243,7 @@
         [VMEM] * 4,
     )(gathered, other, logs, held_psi)
 
-    order = list(range(rows - 1, 0, -1))
+    order = send_order(rows)
     arrived = [row_xor(parts[k], k) for k in order]
     half = 2
 

time: 34.6 us -> 33.8 us (0.977)
  waiting for transfers between devices: 8.49 us -> 7.75 us
    ppermute x7, waiting for transfers between devices: 4.65 us -> 3.89 us  [row_xor(): return lax.ppermute(x, 'row', [(i, i ^ k) for i in range(rows)])]
  transfers between devices with their start and end apart: 13 -> 13, of which waited for: 7 -> 9; matrix products, arithmetic and copies ran while one was open for 0% -> 0% of each run, Pallas kernels for 6% -> 6%
where the time goes in v4:
time: 33.8 us; the launch traced here: 33.5 us
  starting transfers between devices  19.2 us (57%)
  waiting for transfers between devices  7.75 us (23%)
  Pallas kernels  5.9 us (17%)
  between operations  0.68 us (2%)
    ppermute x7, starting transfers between devices, row_xor(): return lax.ppermute(x, 'row', [(i, i ^ k) for i in range(rows)])  10.4 us
    ppermute x4, starting transfers between devices, across(): return lax.ppermute(x, ('row', 'col'), pairs)  7.16 us
    ppermute x7, waiting for transfers between devices, row_xor(): return lax.ppermute(x, 'row', [(i, i ^ k) for i in range(rows)])  3.89 us
    ppermute x4, waiting for transfers between devices, across(): return lax.ppermute(x, ('row', 'col'), pairs)  2.89 us
    ppermute x2, starting transfers between devices, other_col(): return lax.ppermute(x, 'col', [(0, 1), (1, 0)])  1.64 us
    pallas_call x1, Pallas kernels, on_device(): call(lambda *refs: prepare_kernel(blocks, *refs), 'prepare', (f32(slots,...  1.63 us
    pallas_call x1, Pallas kernels, on_device(): call(sums_kernel, 'sums', (f32(slots, tile + LANES), f32(8, tile + LANES)...  1.6 us
    pallas_call x1, Pallas kernels, on_device(): call(lambda *refs: late_kernel(order[half:], *refs), 'late', (f32(rank, t...  1.11 us
  transfers between devices with their start and end apart: 13, of which 9 were waited for; matrix products, arithmetic and copies ran while one was open for 0% of the time, Pallas kernels for 6%

profile of v4, /device:TPU:0, one launch (start us, length us, event | category | flops | bytes accessed | tf_op | source)
XLA Modules:
  0.0 33.5 jit_solution(4696119248261888287)
XLA Ops:
  0.6 1.6 %sums.1 = (f32[8,384]{1,0:T(8,128)S(1)}, f32[8,384]{1,0:T(8,128)S(1)}, bf16[8,256,256]{2,1,0:T(8,128)(2,1)S(1)}) custom-call(s32[8]{0:T(128)} %refs_0_.1, bf16[8,256,256]{2,1,0:T(8,128)(2,1)} %counts_hbm.1), custom_call_target="tpu_custom_call" | custom-call | tf_op jit(solution)/shard_map/sums/pallas_call | solution.py:211
  2.2 4.0 %collective-permute-start.2 = (f32[8,384]{1,0:T(8,128)S(1)}, f32[8,384]{1,0:T(8,128)S(1)}, u32[]{:S(2)}, u32[]{:S(2)}) collective-permute-start(f32[8,384]{1,0:T(8,128)S(1)} %get-tuple-element.30), channel_id=1, source_target_pairs={{0,6},{1,7},{2,4},{3,5},{4,2},{5,3},{6,0},{7,1},{8,14},{9,15},{10,... | collective-permute-start | bytes 36872 | tf_op jit(solution)/shard_map/ppermute | solution.py:203
  6.3 0.0 collective-permute-start.1
  6.3 0.4 %collective-permute-start = (f32[8,384]{1,0:T(8,128)S(1)}, f32[8,384]{1,0:T(8,128)S(1)}, u32[]{:S(2)}, u32[]{:S(2)}) collective-permute-start(f32[8,384]{1,0:T(8,128)S(1)} %get-tuple-element.30), channel_id=1, source_target_pairs={{0,3},{1,2},{2,1},{3,0},{4,7},{5,6},{6,5},{7,4},{8,11},{9,10},{10,... | collective-permute-start | bytes 36872 | tf_op jit(solution)/shard_map/ppermute | solution.py:203
  6.6 1.3 %collective-permute-done.2 = f32[8,384]{1,0:T(8,128)S(1)} collective-permute-done((f32[8,384]{1,0:T(8,128)S(1)}, f32[8,384]{1,0:T(8,128)S(1)}, u32[]{:S(2)}, u32[]{:S(2)}) %collective-permute-start.2) | collective-permute-done | bytes 12320 | tf_op jit(solution)/shard_map/ppermute | solution.py:203
  8.0 1.4 %collective-permute-done.1 = f32[8,384]{1,0:T(8,128)S(1)} collective-permute-done((f32[8,384]{1,0:T(8,128)S(1)}, f32[8,384]{1,0:T(8,128)S(1)}, u32[]{:S(2)}, u32[]{:S(2)}) %collective-permute-start.1) | collective-permute-done | bytes 12320 | tf_op jit(solution)/shard_map/ppermute | solution.py:203
  9.4 0.0 collective-permute-done
  9.4 2.8 %collective-permute-start.3 = (f32[32,384]{1,0:T(8,128)S(1)}, f32[32,384]{1,0:T(8,128)S(1)}, u32[]{:S(2)}, u32[]{:S(2)}) collective-permute-start(f32[32,384]{1,0:T(8,128)S(1)} %pad_maximum_fusion.1), channel_id=1, source_target_pairs={{0,9},{1,8},{2,11},{3,10},{4,13},{5,12},{6,15},{7,14},{8,1},{9,0},... | collective-permute-start | bytes 147464 | tf_op jit(solution)/shard_map/ppermute | solution.py:203
  12.2 1.6 %prepare.1 = (f32[8,256,256]{2,1,0:T(8,128)S(1)}, bf16[8,64,256]{2,1,0:T(8,128)(2,1)S(1)}, bf16[64,256]{1,0:T(8,128)(2,1)S(1)}) custom-call(s32[8]{0:T(128)} %refs_0_.1, bf16[8,256,256]{2,1,0:T(8,128)(2,1)S(1)} %get-tuple-element.34.refs_1_, bf16[64,16384]{1,0:T(8,128)(2,1)} %refs_2_.1, bf16[64,256]{1,0:T(8,128)(2,1)} %refs_3_.1), custom_call_target="tpu_custom_call" | custom-call | flops 20971520 | bytes 3145728 | tf_op jit(solution)/shard_map/prepare/pallas_call | solution.py:226
  13.8 0.1 collective-permute-done.3
  14.0 1.6 %collective-permute-start.4 = (f32[72,384]{1,0:T(8,128)S(1)}, f32[72,384]{1,0:T(8,128)S(1)}, u32[]{:S(2)}, u32[]{:S(2)}) collective-permute-start(f32[72,384]{1,0:T(8,128)S(1)} %pad_maximum_fusion.refs_0_), channel_id=1, source_target_pairs={{0,1},{1,0},{2,3},{3,2},{4,5},{5,4},{6,7},{7,6},{8,9},{9,8},{10,11... | collective-permute-start | bytes 331784 | tf_op jit(solution)/shard_map/ppermute | solution.py:206
  15.5 1.0 %collective-permute-done.4.refs_1_ = f32[72,384]{1,0:T(8,128)S(1)} collective-permute-done((f32[72,384]{1,0:T(8,128)S(1)}, f32[72,384]{1,0:T(8,128)S(1)}, u32[]{:S(2)}, u32[]{:S(2)}) %collective-permute-start.4) | collective-permute-done | bytes 110624 | tf_op jit(solution)/shard_map/ppermute | solution.py:206
  16.5 1.1 %matrix.1 = (bf16[8,256,256]{2,1,0:T(8,128)(2,1)S(1)}, s32[8,128]{1,0:T(8,128)S(1)}, f32[64,256]{1,0:T(8,128)S(1)}, f32[64,256]{1,0:T(8,128)S(1)}, f32[64,256]{1...) custom-call(f32[72,384]{1,0:T(8,128)S(1)} %pad_maximum_fusion.refs_0, ...), custom_call_target="tpu_custom_call" | custom-call | tf_op jit(solution)/shard_map/matrix/pallas_call | solution.py:239
  17.6 3.8 %collective-permute-start.5 = (f32[64,256]{1,0:T(8,128)S(1)}, f32[64,256]{1,0:T(8,128)S(1)}, u32[]{:S(2)}, u32[]{:S(2)}) collective-permute-start(f32[64,256]{1,0:T(8,128)S(1)} %get-tuple-element.45), channel_id=1, source_target_pairs={{0,14},{2,12},{4,10},{6,8},{8,6},{10,4},{12,2},{14,0},{1,15},{3,13... | collective-permute-start | bytes 196616 | tf_op jit(solution)/shard_map/ppermute | solution.py:199
  21.4 0.0 collective-permute-start.6
  21.4 0.0 collective-permute-start.8
  21.4 5.3 %collective-permute-start.9 = (f32[64,256]{1,0:T(8,128)S(1)}, f32[64,256]{1,0:T(8,128)S(1)}, u32[]{:S(2)}, u32[]{:S(2)}) collective-permute-start(f32[64,256]{1,0:T(8,128)S(1)} %get-tuple-element.50), channel_id=1, source_target_pairs={{0,10},{2,8},{4,14},{6,12},{8,2},{10,0},{12,6},{14,4},{1,11},{3,9}... | collective-permute-start | bytes 196616 | tf_op jit(solution)/shard_map/ppermute | solution.py:199
  26.6 0.0 collective-permute-start.10
  26.6 0.0 collective-permute-done.5.refs_4_
  26.6 0.6 %collective-permute-start.11 = (f32[64,256]{1,0:T(8,128)S(1)}, f32[64,256]{1,0:T(8,128)S(1)}, u32[]{:S(2)}, u32[]{:S(2)}) collective-permute-start(f32[64,256]{1,0:T(8,128)S(1)} %get-tuple-element.52), channel_id=1, source_target_pairs={{0,8},{2,10},{4,12},{6,14},{8,0},{10,2},{12,4},{14,6},{1,9},{3,11}... | collective-permute-start | bytes 196616 | tf_op jit(solution)/shard_map/ppermute | solution.py:199
  27.2 0.9 %collective-permute-done.6.refs_5_ = f32[64,256]{1,0:T(8,128)S(1)} collective-permute-done((f32[64,256]{1,0:T(8,128)S(1)}, f32[64,256]{1,0:T(8,128)S(1)}, u32[]{:S(2)}, u32[]{:S(2)}) %collective-permute-start.6) | collective-permute-done | bytes 65568 | tf_op jit(solution)/shard_map/ppermute | solution.py:199
  28.1 0.8 %collective-permute-start.12 = (f32[64,256]{1,0:T(8,128)S(1)}, f32[64,256]{1,0:T(8,128)S(1)}, u32[]{:S(2)}, u32[]{:S(2)}) collective-permute-start(f32[64,256]{1,0:T(8,128)S(1)} %get-tuple-element.53), channel_id=1, source_target_pairs={{0,2},{2,0},{4,6},{6,4},{8,10},{10,8},{12,14},{14,12},{1,3},{3,1},... | collective-permute-start | bytes 196616 | tf_op jit(solution)/shard_map/ppermute | solution.py:199
  28.9 0.4 %early.1 = (f32[64,256]{1,0:T(8,128)S(1)}, f32[64,2048]{1,0:T(8,128)S(1)}) custom-call(s32[8,128]{1,0:T(8,128)S(1)} %get-tuple-element.41.refs_0_, bf16[8,256,256]{2,1,0:T(8,128)(2,1)S(1)} %get-tuple-element.42.refs_1_, bf16[8,64,256]{2,1,0:T(8,128)(2,1)S(1)} %get-tuple-element.43.refs_2_, f32[64,256]{1,0:T(8,128)S(1)} %get-tuple-element.44.refs_3_, ...), custom_call_target="tpu_custom_call" | custom-call | tf_op jit(solution)/shard_map/early/pallas_call | solution.py:250
  29.3 0.0 collective-permute-done.8.refs_4_
  29.3 0.1 collective-permute-start.7
  29.4 0.3 collective-permute-done.9.refs_5_
  29.7 1.6 %collective-permute-done.10.refs_6_ = f32[64,256]{1,0:T(8,128)S(1)} collective-permute-done((f32[64,256]{1,0:T(8,128)S(1)}, f32[64,256]{1,0:T(8,128)S(1)}, u32[]{:S(2)}, u32[]{:S(2)}) %collective-permute-start.10) | collective-permute-done | bytes 65568 | tf_op jit(solution)/shard_map/ppermute | solution.py:199
  31.4 0.8 %collective-permute-done.11.refs_7_ = f32[64,256]{1,0:T(8,128)S(1)} collective-permute-done((f32[64,256]{1,0:T(8,128)S(1)}, f32[64,256]{1,0:T(8,128)S(1)}, u32[]{:S(2)}, u32[]{:S(2)}) %collective-permute-start.11) | collective-permute-done | bytes 65568 | tf_op jit(solution)/shard_map/ppermute | solution.py:199
  32.2 0.2 collective-permute-done.12.refs_8_
  32.4 0.0 collective-permute-done.7.refs_3_
  32.4 1.1 %late.1 = (f32[64,256]{1,0:T(8,128)}, f32[64,2048]{1,0:T(8,128)}) custom-call(s32[8,128]{1,0:T(8,128)S(1)} %get-tuple-element.41.refs_0_, f32[64,2048]{1,0:T(8,128)S(1)} %get-tuple-element.47.refs_1_, f32[64,256]{1,0:T(8,128)S(1)} %get-tuple-element.48.refs_2_, f32[64,256]{1,0:T(8,128)S(1)} %collective-permute-done.7.refs_3_, ...), custom_call_target="tpu_custom_call" | custom-call | tf_op jit(solution)/shard_map/late/pallas_call | solution.py:257
  (2 shorter events, 0.0 us)
Async XLA Ops:
  2.2 5.7 %collective-permute-start.2 = (f32[8,384]{1,0:T(8,128)S(1)}, f32[8,384]{1,0:T(8,128)S(1)}, u32[]{:S(2)}, u32[]{:S(2)}) collective-permute-start(f32[8,384]{1,0:T(8,128)S(1)} %get-tuple-element.30), channel_id=1, source_target_pairs={{0,6},{1,7},{2,4},{3,5},{4,2},{5,3},{6,0},{7,1},{8,14},{9,15},{10,... | collective-permute-start | bytes 36872 | tf_op jit(solution)/shard_map/ppermute | solution.py:203
  6.3 3.1 %collective-permute-start.1 = (f32[8,384]{1,0:T(8,128)S(1)}, f32[8,384]{1,0:T(8,128)S(1)}, u32[]{:S(2)}, u32[]{:S(2)}) collective-permute-start(f32[8,384]{1,0:T(8,128)S(1)} %get-tuple-element.30), channel_id=1, source_target_pairs={{0,5},{1,4},{2,7},{3,6},{4,1},{5,0},{6,3},{7,2},{8,13},{9,12},{10,... | collective-permute-start | bytes 36872 | tf_op jit(solution)/shard_map/ppermute | solution.py:203
  6.3 3.1 %collective-permute-start = (f32[8,384]{1,0:T(8,128)S(1)}, f32[8,384]{1,0:T(8,128)S(1)}, u32[]{:S(2)}, u32[]{:S(2)}) collective-permute-start(f32[8,384]{1,0:T(8,128)S(1)} %get-tuple-element.30), channel_id=1, source_target_pairs={{0,3},{1,2},{2,1},{3,0},{4,7},{5,6},{6,5},{7,4},{8,11},{9,10},{10,... | collective-permute-start | bytes 36872 | tf_op jit(solution)/shard_map/ppermute | solution.py:203
  9.4 4.5 %collective-permute-start.3 = (f32[32,384]{1,0:T(8,128)S(1)}, f32[32,384]{1,0:T(8,128)S(1)}, u32[]{:S(2)}, u32[]{:S(2)}) collective-permute-start(f32[32,384]{1,0:T(8,128)S(1)} %pad_maximum_fusion.1), channel_id=1, source_target_pairs={{0,9},{1,8},{2,11},{3,10},{4,13},{5,12},{6,15},{7,14},{8,1},{9,0},... | collective-permute-start | bytes 147464 | tf_op jit(solution)/shard_map/ppermute | solution.py:203
  14.0 2.5 %collective-permute-start.4 = (f32[72,384]{1,0:T(8,128)S(1)}, f32[72,384]{1,0:T(8,128)S(1)}, u32[]{:S(2)}, u32[]{:S(2)}) collective-permute-start(f32[72,384]{1,0:T(8,128)S(1)} %pad_maximum_fusion.refs_0_), channel_id=1, source_target_pairs={{0,1},{1,0},{2,3},{3,2},{4,5},{5,4},{6,7},{7,6},{8,9},{9,8},{10,11... | collective-permute-start | bytes 331784 | tf_op jit(solution)/shard_map/ppermute | solution.py:206
  17.6 9.1 %collective-permute-start.5 = (f32[64,256]{1,0:T(8,128)S(1)}, f32[64,256]{1,0:T(8,128)S(1)}, u32[]{:S(2)}, u32[]{:S(2)}) collective-permute-start(f32[64,256]{1,0:T(8,128)S(1)} %get-tuple-element.45), channel_id=1, source_target_pairs={{0,14},{2,12},{4,10},{6,8},{8,6},{10,4},{12,2},{14,0},{1,15},{3,13... | collective-permute-start | bytes 196616 | tf_op jit(solution)/shard_map/ppermute | solution.py:199
  21.4 6.8 %collective-permute-start.6 = (f32[64,256]{1,0:T(8,128)S(1)}, f32[64,256]{1,0:T(8,128)S(1)}, u32[]{:S(2)}, u32[]{:S(2)}) collective-permute-start(f32[64,256]{1,0:T(8,128)S(1)} %get-tuple-element.46), channel_id=1, source_target_pairs={{0,12},{2,14},{4,8},{6,10},{8,4},{10,6},{12,0},{14,2},{1,13},{3,15... | collective-permute-start | bytes 196616 | tf_op jit(solution)/shard_map/ppermute | solution.py:199
  21.4 8.0 %collective-permute-start.8 = (f32[64,256]{1,0:T(8,128)S(1)}, f32[64,256]{1,0:T(8,128)S(1)}, u32[]{:S(2)}, u32[]{:S(2)}) collective-permute-start(f32[64,256]{1,0:T(8,128)S(1)} %get-tuple-element.49), channel_id=1, source_target_pairs={{0,6},{2,4},{4,2},{6,0},{8,14},{10,12},{12,10},{14,8},{1,7},{3,5},... | collective-permute-start | bytes 196616 | tf_op jit(solution)/shard_map/ppermute | solution.py:199
  21.4 8.4 %collective-permute-start.9 = (f32[64,256]{1,0:T(8,128)S(1)}, f32[64,256]{1,0:T(8,128)S(1)}, u32[]{:S(2)}, u32[]{:S(2)}) collective-permute-start(f32[64,256]{1,0:T(8,128)S(1)} %get-tuple-element.50), channel_id=1, source_target_pairs={{0,10},{2,8},{4,14},{6,12},{8,2},{10,0},{12,6},{14,4},{1,11},{3,9}... | collective-permute-start | bytes 196616 | tf_op jit(solution)/shard_map/ppermute | solution.py:199
  26.6 4.7 %collective-permute-start.10 = (f32[64,256]{1,0:T(8,128)S(1)}, f32[64,256]{1,0:T(8,128)S(1)}, u32[]{:S(2)}, u32[]{:S(2)}) collective-permute-start(f32[64,256]{1,0:T(8,128)S(1)} %get-tuple-element.51), channel_id=1, source_target_pairs={{0,4},{2,6},{4,0},{6,2},{8,12},{10,14},{12,8},{14,10},{1,5},{3,7},... | collective-permute-start | bytes 196616 | tf_op jit(solution)/shard_map/ppermute | solution.py:199
  26.6 5.5 %collective-permute-start.11 = (f32[64,256]{1,0:T(8,128)S(1)}, f32[64,256]{1,0:T(8,128)S(1)}, u32[]{:S(2)}, u32[]{:S(2)}) collective-permute-start(f32[64,256]{1,0:T(8,128)S(1)} %get-tuple-element.52), channel_id=1, source_target_pairs={{0,8},{2,10},{4,12},{6,14},{8,0},{10,2},{12,4},{14,6},{1,9},{3,11}... | collective-permute-start | bytes 196616 | tf_op jit(solution)/shard_map/ppermute | solution.py:199
  28.1 4.3 %collective-permute-start.12 = (f32[64,256]{1,0:T(8,128)S(1)}, f32[64,256]{1,0:T(8,128)S(1)}, u32[]{:S(2)}, u32[]{:S(2)}) collective-permute-start(f32[64,256]{1,0:T(8,128)S(1)} %get-tuple-element.53), channel_id=1, source_target_pairs={{0,2},{2,0},{4,6},{6,4},{8,10},{10,8},{12,14},{14,12},{1,3},{3,1},... | collective-permute-start | bytes 196616 | tf_op jit(solution)/shard_map/ppermute | solution.py:199
  29.3 3.1 %collective-permute-start.7 = (f32[64,256]{1,0:T(8,128)S(1)}, f32[64,256]{1,0:T(8,128)S(1)}, u32[]{:S(2)}, u32[]{:S(2)}) collective-permute-start(f32[64,256]{1,0:T(8,128)S(1)} %get-tuple-element.48.refs_2_), channel_id=1, source_target_pairs={{0,1},{1,0},{2,3},{3,2},{4,5},{5,4},{6,7},{7,6},{8,9},{9,8},{10,11... | collective-permute-start | bytes 196616 | tf_op jit(solution)/shard_map/ppermute | solution.py:206

commit v5 on v3

--- a/solution.py
+++ b/solution.py
@@ -47,8 +47,7 @@
         packet_ref[g : g + 8, :] = jnp.concatenate(columns)
     narrow = sum(values[:, k : k + LANES] for k in range(0, tile, LANES))
     rows = jnp.sum(jnp.transpose(narrow), axis=0, keepdims=True)
-    row_ref[:, :tile] = jnp.broadcast_to(rows, (8, tile))
-    row_ref[:, tile:] = jnp.zeros((8, LANES), jnp.float32)
+    row_ref[...] = jnp.broadcast_to(rows, (8, tile))
 
 
 def prepare_kernel(blocks, pos_hbm, counts_ref, omega_hbm, psi_hbm, logs_ref, chosen_ref, psi_ref, pos_ref, sems):
@@ -83,19 +82,34 @@
     return [[(1, 1), (2, 1), (3, 0)]] + [[(bit, 1)] for bit in bits]
 
 
-def matrix_kernel(blocks, offsets, mine_ref, other_ref, logs_ref, psi_ref, matrix_ref, incoming_ref, *out_refs):
+def outer(row):
+    return ((row >> 2) ^ (row >> 1)) & 1 == 0
+
+
+def rounds(rows):
+    if rows == 8:
+        return [(4, 4), (6, 1), (7, 7), (3, 3), (5, 5), (2, 2), (1, 6)]
+    return [(k, k) for k in range(rows - 1, 0, -1)]
+
+
+def matrix_kernel(blocks, near, far, order, mine_ref, other_ref, logs_ref, psi_ref, matrix_ref, incoming_ref, *out_refs):
     slots, tile, _ = logs_ref.shape
     rows = slots
-    wide = tile // LANES
-
-    def column_sums(swapped):
+    group = LANES // len(near)
+    packets = {}
+    for g, (r, c) in enumerate(far):
+        some = slice(g * slots, (g + 1) * slots)
+        for j, (r2, c2) in enumerate(near):
+            for core, ref in enumerate((mine_ref, other_ref)):
+                at = ref[some, len(near) * tile + j * group :][:, :1]
+                value = ref[some, j * tile : (j + 1) * tile]
+                packets[r ^ r2, c ^ c2 ^ core] = value, jnp.broadcast_to(at, (slots, tile))
+
+    def column_sums(core):
         sums = [jnp.zeros((slots, tile), jnp.float32)] * blocks
-        for k, (_, c) in enumerate(offsets):
-            ref = other_ref if c != swapped else mine_ref
-            value = ref[k * slots : (k + 1) * slots, :tile]
-            at = ref[k * slots : (k + 1) * slots, tile:]
-            at = jnp.concatenate([at] * wide, axis=1)
-            sums = [s + jnp.where(at == p, value, 0.0) for p, s in enumerate(sums)]
+        for (_, c), (value, at) in packets.items():
+            if c == core:
+                sums = [s + jnp.where(at == p, value, 0.0) for p, s in enumerate(sums)]
         return sums
 
     def smooth_total(sums):
@@ -108,8 +122,7 @@
     sums = column_sums(0)
     first, second = smooth_total(sums), smooth_total(column_sums(1))
     total = first + second
-    own = mine_ref[:slots, tile:]
-    own = jnp.concatenate([own] * wide, axis=1)
+    own = packets[0, 0][1]
     chosen = jnp.zeros((slots, tile), jnp.float32)
     for p in range(blocks):
         chosen = chosen + jnp.where(own == p, sums[p], 0.0)
@@ -117,12 +130,16 @@
 
     me = lax.axis_index("row")
     mine = lax.broadcasted_iota(jnp.int32, (slots, LANES), 0) == me
-    for k, (r, c) in enumerate(offsets):
-        ref = other_ref if c else mine_ref
-        at = jnp.where(mine, ref[k * slots : (k + 1) * slots, tile:], 0.0)
-        incoming_ref[r : r + 1, :] = jnp.sum(at, axis=0, keepdims=True).astype(jnp.int32)
-
-    both = mine_ref[rows * slots :, :tile] + other_ref[rows * slots :, :tile]
+    position = {}
+    for (r, c), (_, at) in packets.items():
+        if c == 0:
+            at = jnp.where(mine, at[:, :LANES], 0.0)
+            position[r] = jnp.sum(at, axis=0, keepdims=True).astype(jnp.int32)
+    for k, (a, b) in enumerate(order):
+        at = position[a] if a == b else jnp.where(outer(me), position[a], position[b])
+        incoming_ref[k : k + 1, :] = at
+
+    both = mine_ref[:8, -tile:] + other_ref[:8, -tile:]
     shift = jnp.log(jnp.full((8, tile), total)) - jnp.log(both) - shift_log
     shift = jnp.transpose(shift)[:, :1]
 
@@ -130,8 +147,8 @@
         x = logs_ref[s] + shift + terms[s : s + 1]
         matrix_ref[s] = jnp.maximum(x, 0.0).astype(jnp.bfloat16)
     psi = psi_ref[...]
-    for k, out_ref in enumerate(out_refs):
-        s = jnp.bitwise_xor(me, k)
+    for (a, b), out_ref in zip(order, out_refs, strict=True):
+        s = jnp.bitwise_xor(me, a if a == b else jnp.where(outer(me), a, b))
         out_ref[...] = lax.dot_general(psi, matrix_ref[s], NN, preferred_element_type=jnp.float32)
 
 
@@ -174,6 +191,7 @@
     rank, width = omega_t.shape
     blocks = width // (slots * tile)
     rows = slots
+    order = [(0, 0)] + rounds(rows)
     DMA = pltpu.SemaphoreType.DMA
 
     def call(kernel, name, outs, ins, out_specs=None, scratch=(), cost=None):
@@ -188,8 +206,8 @@
             name=name,
         )
 
-    def row_xor(x, k):
-        return lax.ppermute(x, "row", [(i, i ^ k) for i in range(rows)])
+    def swap(x, far, near):
+        return lax.ppermute(x, "row", [(i, i ^ (far if outer(i) else near)) for i in range(rows)])
 
     def across(x, k, odd):
         pairs = [(2 * i + c, 2 * (i ^ k) + (c ^ odd)) for i in range(rows) for c in range(2)]
@@ -204,11 +222,24 @@
     packet, row_part, held = call(
         sums_kernel,
         "sums",
-        (f32(slots, tile + LANES), f32(8, tile + LANES), bf16(slots, tile, tile)),
+        (f32(slots, tile + LANES), f32(8, tile), bf16(slots, tile, tile)),
         [HBM, HBM],
         scratch=[pltpu.SMEM((slots,), jnp.int32), DMA(()), DMA((slots,))],
     )(tile_pos, counts)
 
+    first, *later = stages(rows)
+    packets = [packet] + [across(packet, k, odd) for k, odd in first]
+    group = LANES // len(packets)
+    lane = lax.broadcasted_iota(jnp.int32, (slots, LANES), 1)
+    at = packet[:, tile:]
+    for j, other in enumerate(packets):
+        at = jnp.where(lane >= j * group, other[:, tile:], at)
+    gathered = jnp.concatenate([x[:, :tile] for x in packets] + [at], axis=1)
+    gathered, held = lax.optimization_barrier((gathered, held))
+    near, far = [(0, 0)] + first, [(0, 0)]
+    for ((k, odd),) in later:
+        gathered = jnp.concatenate([gathered, across(gathered, k, odd)])
+        far += [(r ^ k, c ^ odd) for r, c in far]
     logs, chosen, held_psi = call(
         lambda *refs: prepare_kernel(blocks, *refs),
         "prepare",
@@ -218,36 +249,30 @@
         cost=pl.CostEstimate(flops=40 * counts.size, bytes_accessed=6 * counts.size, transcendentals=counts.size),
     )(tile_pos, held, omega_t, psi)
 
-    gathered = packet
-    offsets = [(0, 0)]
-    for stage in stages(rows):
-        sent = [across(gathered, k, odd) for k, odd in stage]
-        gathered = jnp.concatenate([gathered] + sent)
-        offsets += [(r ^ k, c ^ odd) for k, odd in stage for r, c in offsets]
-    gathered = jnp.concatenate([gathered, row_part])
+    row_part = jnp.concatenate([row_part] * (gathered.shape[0] // row_part.shape[0]))
+    gathered = jnp.concatenate([gathered, row_part], axis=1)
     gathered, logs, chosen, held_psi = lax.optimization_barrier((gathered, logs, chosen, held_psi))
     other = other_col(gathered)
 
     matrix, incoming_at, *parts = call(
-        lambda *refs: matrix_kernel(blocks, offsets, *refs),
+        lambda *refs: matrix_kernel(blocks, near, far, order, *refs),
         "matrix",
         (bf16(*counts.shape), jax.ShapeDtypeStruct((rows, LANES), jnp.int32)) + (f32(rank, tile),) * rows,
         [VMEM] * 4,
     )(gathered, other, logs, held_psi)
 
-    order = list(range(rows - 1, 0, -1))
-    arrived = [row_xor(parts[k], k) for k in order]
+    arrived = [swap(part, *ks) for part, ks in zip(parts[1:], order[1:], strict=True)]
     half = 2
 
     partial_range, early = call(
-        lambda *refs: early_kernel([0] + order[:half], *refs),
+        lambda *refs: early_kernel(range(half + 1), *refs),
         "early",
         (f32(rank, tile), f32(rank, blocks * tile)),
         [VMEM] * (4 + half),
     )(incoming_at, matrix, chosen, parts[0], *arrived[:half])
     other_range = other_col(partial_range)
     return call(
-        lambda *refs: late_kernel(order[half:], *refs),
+        lambda *refs: late_kernel(range(half + 1, rows), *refs),
         "late",
         (f32(rank, tile), f32(rank, blocks * tile)),
         [VMEM] * (4 + rows - 1 - half),

time: 34.6 us -> 32.9 us (0.951)
  waiting for transfers between devices: 8.49 us -> 6.92 us
    ppermute x7, waiting for transfers between devices: 4.65 us -> 3.23 us  [swap(): lax.ppermute(x, 'row', [(i, i ^ (far if outer(i) else near)) for i in ran...]
    ppermute x2, starting transfers between devices: 1.57 us -> 0.57 us  [other_col(): return lax.ppermute(x, 'col', [(0, 1), (1, 0)])]
    ppermute x7, starting transfers between devices: 10.5 us -> 11.3 us  [swap(): lax.ppermute(x, 'row', [(i, i ^ (far if outer(i) else near)) for i in ran...]
  transfers between devices with their start and end apart: 13 -> 13, of which waited for: 7 -> 5; matrix products, arithmetic and copies ran while one was open for 0% -> 0% of each run, Pallas kernels for 6% -> 6%
where the time goes in v5:
time: 32.9 us; the launch traced here: 32.7 us
  starting transfers between devices  19.1 us (58%)
  waiting for transfers between devices  6.92 us (21%)
  Pallas kernels  5.93 us (18%)
  between operations  0.71 us (2%)
    ppermute x7, starting transfers between devices, swap(): lax.ppermute(x, 'row', [(i, i ^ (far if outer(i) else near)) for i in ran...  11.3 us
    ppermute x4, starting transfers between devices, across(): return lax.ppermute(x, ('row', 'col'), pairs)  7.23 us
    ppermute x7, waiting for transfers between devices, swap(): lax.ppermute(x, 'row', [(i, i ^ (far if outer(i) else near)) for i in ran...  3.23 us
    ppermute x4, waiting for transfers between devices, across(): return lax.ppermute(x, ('row', 'col'), pairs)  2.75 us
    pallas_call x1, Pallas kernels, on_device(): call(lambda *refs: prepare_kernel(blocks, *refs), 'prepare', (f32(slots,...  1.63 us
    pallas_call x1, Pallas kernels, on_device(): call(sums_kernel, 'sums', (f32(slots, tile + LANES), f32(8, tile), bf16(s...  1.6 us
    pallas_call x1, Pallas kernels, on_device(): call(lambda *refs: matrix_kernel(blocks, near, far, order, *refs), 'matri...  1.14 us
    pallas_call x1, Pallas kernels, on_device(): call(lambda *refs: late_kernel(range(half + 1, rows), *refs), 'late', (f3...  1.11 us
  transfers between devices with their start and end apart: 13, of which 5 were waited for; matrix products, arithmetic and copies ran while one was open for 0% of the time, Pallas kernels for 6%

profile of v5, /device:TPU:0, one launch (start us, length us, event | category | flops | bytes accessed | tf_op | source)
XLA Modules:
  0.0 32.7 jit_solution(11550180341549503659)
XLA Ops:
  0.6 1.6 %sums.1 = (f32[8,384]{1,0:T(8,128)S(1)}, f32[8,256]{1,0:T(8,128)S(1)}, bf16[8,256,256]{2,1,0:T(8,128)(2,1)S(1)}) custom-call(s32[8]{0:T(128)} %refs_0_.1, bf16[8,256,256]{2,1,0:T(8,128)(2,1)} %counts_hbm.1), custom_call_target="tpu_custom_call" | custom-call | tf_op jit(solution)/shard_map/sums/pallas_call | solution.py:222
  2.2 4.0 %collective-permute-start.2 = (f32[8,384]{1,0:T(8,128)S(1)}, f32[8,384]{1,0:T(8,128)S(1)}, u32[]{:S(2)}, u32[]{:S(2)}) collective-permute-start(f32[8,384]{1,0:T(8,128)S(1)} %get-tuple-element.26), channel_id=1, source_target_pairs={{0,6},{1,7},{2,4},{3,5},{4,2},{5,3},{6,0},{7,1},{8,14},{9,15},{10,... | collective-permute-start | bytes 36872 | tf_op jit(solution)/shard_map/ppermute | solution.py:214
  6.3 0.0 collective-permute-start.1
  6.3 0.4 %collective-permute-start = (f32[8,384]{1,0:T(8,128)S(1)}, f32[8,384]{1,0:T(8,128)S(1)}, u32[]{:S(2)}, u32[]{:S(2)}) collective-permute-start(f32[8,384]{1,0:T(8,128)S(1)} %get-tuple-element.26), channel_id=1, source_target_pairs={{0,3},{1,2},{2,1},{3,0},{4,7},{5,6},{6,5},{7,4},{8,11},{9,10},{10,... | collective-permute-start | bytes 36872 | tf_op jit(solution)/shard_map/ppermute | solution.py:214
  6.7 2.7 %collective-permute-done = f32[8,384]{1,0:T(8,128)S(1)} collective-permute-done((f32[8,384]{1,0:T(8,128)S(1)}, f32[8,384]{1,0:T(8,128)S(1)}, u32[]{:S(2)}, u32[]{:S(2)}) %collective-permute-start) | collective-permute-done | bytes 12320 | tf_op jit(solution)/shard_map/ppermute | solution.py:214
  9.4 0.0 collective-permute-done.1
  9.4 0.0 collective-permute-done.2
  9.4 2.8 %collective-permute-start.3 = (f32[8,1152]{1,0:T(8,128)S(1)}, f32[8,1152]{1,0:T(8,128)S(1)}, u32[]{:S(2)}, u32[]{:S(2)}) collective-permute-start(f32[8,1152]{1,0:T(8,128)S(1)} %constant_dynamic-update-slice_fusion), channel_id=1, source_target_pairs={{0,9},{1,8},{2,11},{3,10},{4,13},{5,12},{6,15},{7,14},{8,1},{9,0},... | collective-permute-start | bytes 110600 | tf_op jit(solution)/shard_map/ppermute | solution.py:214
  12.3 1.6 %prepare.1 = (f32[8,256,256]{2,1,0:T(8,128)S(1)}, bf16[8,64,256]{2,1,0:T(8,128)(2,1)S(1)}, bf16[64,256]{1,0:T(8,128)(2,1)S(1)}) custom-call(s32[8]{0:T(128)} %refs_0_.1, bf16[8,256,256]{2,1,0:T(8,128)(2,1)S(1)} %get-tuple-element.30.refs_1_, bf16[64,16384]{1,0:T(8,128)(2,1)} %refs_2_.1, bf16[64,256]{1,0:T(8,128)(2,1)} %refs_3_.1), custom_call_target="tpu_custom_call" | custom-call | flops 20971520 | bytes 3145728 | tf_op jit(solution)/shard_map/prepare/pallas_call | solution.py:243
  13.9 0.0 collective-permute-done.3
  13.9 0.5 %collective-permute-start.4 = (f32[16,1408]{1,0:T(8,128)S(1)}, f32[16,1408]{1,0:T(8,128)S(1)}, u32[]{:S(2)}, u32[]{:S(2)}) collective-permute-start(f32[16,1408]{1,0:T(8,128)S(1)} %maximum_maximum_fusion.refs_0_), channel_id=1, source_target_pairs={{0,1},{1,0},{2,3},{3,2},{4,5},{5,4},{6,7},{7,6},{8,9},{9,8},{10,11... | collective-permute-start | bytes 270344 | tf_op jit(solution)/shard_map/ppermute | solution.py:217
  14.4 0.9 %collective-permute-done.4.refs_1_ = f32[16,1408]{1,0:T(8,128)S(1)} collective-permute-done((f32[16,1408]{1,0:T(8,128)S(1)}, f32[16,1408]{1,0:T(8,128)S(1)}, u32[]{:S(2)}, u32[]{:S(2)}) %collective-permute-start.4) | collective-permute-done | bytes 90144 | tf_op jit(solution)/shard_map/ppermute | solution.py:217
  15.4 1.1 %matrix.1 = (bf16[8,256,256]{2,1,0:T(8,128)(2,1)S(1)}, s32[8,128]{1,0:T(8,128)S(1)}, f32[64,256]{1,0:T(8,128)S(1)}, f32[64,256]{1,0:T(8,128)S(1)}, f32[64,256]{1...) custom-call(f32[16,1408]{1,0:T(8,128)S(1)} %maximum_maximum_fusion.r, ...), custom_call_target="tpu_custom_call" | custom-call | tf_op jit(solution)/shard_map/matrix/pallas_call | solution.py:257
  16.5 2.7 %collective-permute-start.5 = (f32[64,256]{1,0:T(8,128)S(1)}, f32[64,256]{1,0:T(8,128)S(1)}, u32[]{:S(2)}, u32[]{:S(2)}) collective-permute-start(f32[64,256]{1,0:T(8,128)S(1)} %get-tuple-element.41), channel_id=1, source_target_pairs={{0,8},{2,10},{4,12},{6,14},{8,0},{10,2},{12,4},{14,6},{1,9},{3,11}... | collective-permute-start | bytes 196616 | tf_op jit(solution)/shard_map/ppermute | solution.py:210
  19.2 1.4 %collective-permute-start.6 = (f32[64,256]{1,0:T(8,128)S(1)}, f32[64,256]{1,0:T(8,128)S(1)}, u32[]{:S(2)}, u32[]{:S(2)}) collective-permute-start(f32[64,256]{1,0:T(8,128)S(1)} %get-tuple-element.42), channel_id=1, source_target_pairs={{0,12},{2,14},{4,6},{6,4},{8,10},{10,8},{12,0},{14,2},{1,13},{3,15... | collective-permute-start | bytes 196616 | tf_op jit(solution)/shard_map/ppermute | solution.py:210
  20.5 2.4 %collective-permute-start.8 = (f32[64,256]{1,0:T(8,128)S(1)}, f32[64,256]{1,0:T(8,128)S(1)}, u32[]{:S(2)}, u32[]{:S(2)}) collective-permute-start(f32[64,256]{1,0:T(8,128)S(1)} %get-tuple-element.45), channel_id=1, source_target_pairs={{0,14},{2,12},{4,10},{6,8},{8,6},{10,4},{12,2},{14,0},{1,15},{3,13... | collective-permute-start | bytes 196616 | tf_op jit(solution)/shard_map/ppermute | solution.py:210
  22.9 0.0 collective-permute-start.9
  22.9 3.2 %collective-permute-start.10 = (f32[64,256]{1,0:T(8,128)S(1)}, f32[64,256]{1,0:T(8,128)S(1)}, u32[]{:S(2)}, u32[]{:S(2)}) collective-permute-start(f32[64,256]{1,0:T(8,128)S(1)} %get-tuple-element.47), channel_id=1, source_target_pairs={{0,10},{2,8},{4,14},{6,12},{8,2},{10,0},{12,6},{14,4},{1,11},{3,9}... | collective-permute-start | bytes 196616 | tf_op jit(solution)/shard_map/ppermute | solution.py:210
  26.2 0.0 collective-permute-done.5.refs_4_
  26.2 0.7 %collective-permute-start.11 = (f32[64,256]{1,0:T(8,128)S(1)}, f32[64,256]{1,0:T(8,128)S(1)}, u32[]{:S(2)}, u32[]{:S(2)}) collective-permute-start(f32[64,256]{1,0:T(8,128)S(1)} %get-tuple-element.48), channel_id=1, source_target_pairs={{0,4},{2,6},{4,0},{6,2},{8,12},{10,14},{12,8},{14,10},{1,5},{3,7},... | collective-permute-start | bytes 196616 | tf_op jit(solution)/shard_map/ppermute | solution.py:210
  26.9 0.0 collective-permute-done.6.refs_5_
  26.9 0.9 %collective-permute-start.12 = (f32[64,256]{1,0:T(8,128)S(1)}, f32[64,256]{1,0:T(8,128)S(1)}, u32[]{:S(2)}, u32[]{:S(2)}) collective-permute-start(f32[64,256]{1,0:T(8,128)S(1)} %get-tuple-element.49), channel_id=1, source_target_pairs={{0,2},{2,0},{4,8},{6,10},{8,4},{10,6},{12,14},{14,12},{1,3},{3,1},... | collective-permute-start | bytes 196616 | tf_op jit(solution)/shard_map/ppermute | solution.py:210
  27.8 0.5 %early.1 = (f32[64,256]{1,0:T(8,128)S(1)}, f32[64,2048]{1,0:T(8,128)S(1)}) custom-call(s32[8,128]{1,0:T(8,128)S(1)} %get-tuple-element.37.refs_0_, bf16[8,256,256]{2,1,0:T(8,128)(2,1)S(1)} %get-tuple-element.38.refs_1_, bf16[8,64,256]{2,1,0:T(8,128)(2,1)S(1)} %get-tuple-element.39.refs_2_, f32[64,256]{1,0:T(8,128)S(1)} %get-tuple-element.40.refs_3_, ...), custom_call_target="tpu_custom_call" | custom-call | tf_op jit(solution)/shard_map/early/pallas_call | solution.py:267
  28.2 0.0 collective-permute-done.8.refs_4_
  28.2 0.1 collective-permute-start.7
  28.3 2.1 %collective-permute-done.9.refs_5_ = f32[64,256]{1,0:T(8,128)S(1)} collective-permute-done((f32[64,256]{1,0:T(8,128)S(1)}, f32[64,256]{1,0:T(8,128)S(1)}, u32[]{:S(2)}, u32[]{:S(2)}) %collective-permute-start.9) | collective-permute-done | bytes 65568 | tf_op jit(solution)/shard_map/ppermute | solution.py:210
  30.5 0.0 collective-permute-done.10.refs_6_
  30.5 0.5 %collective-permute-done.11.refs_7_ = f32[64,256]{1,0:T(8,128)S(1)} collective-permute-done((f32[64,256]{1,0:T(8,128)S(1)}, f32[64,256]{1,0:T(8,128)S(1)}, u32[]{:S(2)}, u32[]{:S(2)}) %collective-permute-start.11) | collective-permute-done | bytes 65568 | tf_op jit(solution)/shard_map/ppermute | solution.py:210
  31.0 0.6 %collective-permute-done.12.refs_8_ = f32[64,256]{1,0:T(8,128)S(1)} collective-permute-done((f32[64,256]{1,0:T(8,128)S(1)}, f32[64,256]{1,0:T(8,128)S(1)}, u32[]{:S(2)}, u32[]{:S(2)}) %collective-permute-start.12) | collective-permute-done | bytes 65568 | tf_op jit(solution)/shard_map/ppermute | solution.py:210
  31.5 0.0 collective-permute-done.7.refs_3_
  31.5 1.1 %late.1 = (f32[64,256]{1,0:T(8,128)}, f32[64,2048]{1,0:T(8,128)}) custom-call(s32[8,128]{1,0:T(8,128)S(1)} %get-tuple-element.37.refs_0_, f32[64,2048]{1,0:T(8,128)S(1)} %get-tuple-element.43.refs_1_, f32[64,256]{1,0:T(8,128)S(1)} %get-tuple-element.44.refs_2_, f32[64,256]{1,0:T(8,128)S(1)} %collective-permute-done.7.refs_3_, ...), custom_call_target="tpu_custom_call" | custom-call | tf_op jit(solution)/shard_map/late/pallas_call | solution.py:274
  (8 shorter events, 0.0 us)
Async XLA Ops:
  2.2 7.2 %collective-permute-start.2 = (f32[8,384]{1,0:T(8,128)S(1)}, f32[8,384]{1,0:T(8,128)S(1)}, u32[]{:S(2)}, u32[]{:S(2)}) collective-permute-start(f32[8,384]{1,0:T(8,128)S(1)} %get-tuple-element.26), channel_id=1, source_target_pairs={{0,6},{1,7},{2,4},{3,5},{4,2},{5,3},{6,0},{7,1},{8,14},{9,15},{10,... | collective-permute-start | bytes 36872 | tf_op jit(solution)/shard_map/ppermute | solution.py:214
  6.3 3.1 %collective-permute-start.1 = (f32[8,384]{1,0:T(8,128)S(1)}, f32[8,384]{1,0:T(8,128)S(1)}, u32[]{:S(2)}, u32[]{:S(2)}) collective-permute-start(f32[8,384]{1,0:T(8,128)S(1)} %get-tuple-element.26), channel_id=1, source_target_pairs={{0,5},{1,4},{2,7},{3,6},{4,1},{5,0},{6,3},{7,2},{8,13},{9,12},{10,... | collective-permute-start | bytes 36872 | tf_op jit(solution)/shard_map/ppermute | solution.py:214
  6.3 3.1 %collective-permute-start = (f32[8,384]{1,0:T(8,128)S(1)}, f32[8,384]{1,0:T(8,128)S(1)}, u32[]{:S(2)}, u32[]{:S(2)}) collective-permute-start(f32[8,384]{1,0:T(8,128)S(1)} %get-tuple-element.26), channel_id=1, source_target_pairs={{0,3},{1,2},{2,1},{3,0},{4,7},{5,6},{6,5},{7,4},{8,11},{9,10},{10,... | collective-permute-start | bytes 36872 | tf_op jit(solution)/shard_map/ppermute | solution.py:214
  9.4 4.5 %collective-permute-start.3 = (f32[8,1152]{1,0:T(8,128)S(1)}, f32[8,1152]{1,0:T(8,128)S(1)}, u32[]{:S(2)}, u32[]{:S(2)}) collective-permute-start(f32[8,1152]{1,0:T(8,128)S(1)} %constant_dynamic-update-slice_fusion), channel_id=1, source_target_pairs={{0,9},{1,8},{2,11},{3,10},{4,13},{5,12},{6,15},{7,14},{8,1},{9,0},... | collective-permute-start | bytes 110600 | tf_op jit(solution)/shard_map/ppermute | solution.py:214
  13.9 1.4 %collective-permute-start.4 = (f32[16,1408]{1,0:T(8,128)S(1)}, f32[16,1408]{1,0:T(8,128)S(1)}, u32[]{:S(2)}, u32[]{:S(2)}) collective-permute-start(f32[16,1408]{1,0:T(8,128)S(1)} %maximum_maximum_fusion.refs_0_), channel_id=1, source_target_pairs={{0,1},{1,0},{2,3},{3,2},{4,5},{5,4},{6,7},{7,6},{8,9},{9,8},{10,11... | collective-permute-start | bytes 270344 | tf_op jit(solution)/shard_map/ppermute | solution.py:217
  16.5 9.6 %collective-permute-start.5 = (f32[64,256]{1,0:T(8,128)S(1)}, f32[64,256]{1,0:T(8,128)S(1)}, u32[]{:S(2)}, u32[]{:S(2)}) collective-permute-start(f32[64,256]{1,0:T(8,128)S(1)} %get-tuple-element.41), channel_id=1, source_target_pairs={{0,8},{2,10},{4,12},{6,14},{8,0},{10,2},{12,4},{14,6},{1,9},{3,11}... | collective-permute-start | bytes 196616 | tf_op jit(solution)/shard_map/ppermute | solution.py:210
  19.2 7.7 %collective-permute-start.6 = (f32[64,256]{1,0:T(8,128)S(1)}, f32[64,256]{1,0:T(8,128)S(1)}, u32[]{:S(2)}, u32[]{:S(2)}) collective-permute-start(f32[64,256]{1,0:T(8,128)S(1)} %get-tuple-element.42), channel_id=1, source_target_pairs={{0,12},{2,14},{4,6},{6,4},{8,10},{10,8},{12,0},{14,2},{1,13},{3,15... | collective-permute-start | bytes 196616 | tf_op jit(solution)/shard_map/ppermute | solution.py:210
  20.5 7.7 %collective-permute-start.8 = (f32[64,256]{1,0:T(8,128)S(1)}, f32[64,256]{1,0:T(8,128)S(1)}, u32[]{:S(2)}, u32[]{:S(2)}) collective-permute-start(f32[64,256]{1,0:T(8,128)S(1)} %get-tuple-element.45), channel_id=1, source_target_pairs={{0,14},{2,12},{4,10},{6,8},{8,6},{10,4},{12,2},{14,0},{1,15},{3,13... | collective-permute-start | bytes 196616 | tf_op jit(solution)/shard_map/ppermute | solution.py:210
  22.9 7.5 %collective-permute-start.9 = (f32[64,256]{1,0:T(8,128)S(1)}, f32[64,256]{1,0:T(8,128)S(1)}, u32[]{:S(2)}, u32[]{:S(2)}) collective-permute-start(f32[64,256]{1,0:T(8,128)S(1)} %get-tuple-element.46), channel_id=1, source_target_pairs={{0,6},{2,4},{4,2},{6,0},{8,14},{10,12},{12,10},{14,8},{1,7},{3,5},... | collective-permute-start | bytes 196616 | tf_op jit(solution)/shard_map/ppermute | solution.py:210
  22.9 7.5 %collective-permute-start.10 = (f32[64,256]{1,0:T(8,128)S(1)}, f32[64,256]{1,0:T(8,128)S(1)}, u32[]{:S(2)}, u32[]{:S(2)}) collective-permute-start(f32[64,256]{1,0:T(8,128)S(1)} %get-tuple-element.47), channel_id=1, source_target_pairs={{0,10},{2,8},{4,14},{6,12},{8,2},{10,0},{12,6},{14,4},{1,11},{3,9}... | collective-permute-start | bytes 196616 | tf_op jit(solution)/shard_map/ppermute | solution.py:210
  26.2 4.8 %collective-permute-start.11 = (f32[64,256]{1,0:T(8,128)S(1)}, f32[64,256]{1,0:T(8,128)S(1)}, u32[]{:S(2)}, u32[]{:S(2)}) collective-permute-start(f32[64,256]{1,0:T(8,128)S(1)} %get-tuple-element.48), channel_id=1, source_target_pairs={{0,4},{2,6},{4,0},{6,2},{8,12},{10,14},{12,8},{14,10},{1,5},{3,7},... | collective-permute-start | bytes 196616 | tf_op jit(solution)/shard_map/ppermute | solution.py:210
  26.9 4.7 %collective-permute-start.12 = (f32[64,256]{1,0:T(8,128)S(1)}, f32[64,256]{1,0:T(8,128)S(1)}, u32[]{:S(2)}, u32[]{:S(2)}) collective-permute-start(f32[64,256]{1,0:T(8,128)S(1)} %get-tuple-element.49), channel_id=1, source_target_pairs={{0,2},{2,0},{4,8},{6,10},{8,4},{10,6},{12,14},{14,12},{1,3},{3,1},... | collective-permute-start | bytes 196616 | tf_op jit(solution)/shard_map/ppermute | solution.py:210
  28.2 3.3 %collective-permute-start.7 = (f32[64,256]{1,0:T(8,128)S(1)}, f32[64,256]{1,0:T(8,128)S(1)}, u32[]{:S(2)}, u32[]{:S(2)}) collective-permute-start(f32[64,256]{1,0:T(8,128)S(1)} %get-tuple-element.44.refs_2_), channel_id=1, source_target_pairs={{0,1},{1,0},{2,3},{3,2},{4,5},{5,4},{6,7},{7,6},{8,9},{9,8},{10,11... | collective-permute-start | bytes 196616 | tf_op jit(solution)/shard_map/ppermute | solution.py:217

commit v6 on v5

--- a/solution.py
+++ b/solution.py
@@ -50,31 +50,20 @@
     row_ref[...] = jnp.broadcast_to(rows, (8, tile))
 
 
-def prepare_kernel(blocks, pos_hbm, counts_ref, omega_hbm, psi_hbm, logs_ref, chosen_ref, psi_ref, pos_ref, sems):
+def prepare_kernel(blocks, packet_ref, counts_ref, omega_hbm, psi_hbm, logs_ref, chosen_ref, psi_ref, sems):
     slots, tile, _ = counts_ref.shape
-    fetch_pos = pltpu.make_async_copy(pos_hbm, pos_ref, sems.at[slots])
-    fetch_psi = pltpu.make_async_copy(psi_hbm, psi_ref, sems.at[slots + 1])
-    fetch_pos.start()
-    fetch_psi.start()
-    fetch_pos.wait()
-
-    def fetch(s):
-        at = s * blocks + jnp.maximum(pos_ref[s], 0)
-        columns = pl.ds(pl.multiple_of(at * tile, tile), tile)
-        return pltpu.make_async_copy(omega_hbm.at[:, columns], chosen_ref.at[s], sems.at[s])
-
-    for s in range(slots):
-        fetch(s).start()
-
-    def one(s, carry):
+    fetches = [pltpu.make_async_copy(psi_hbm, psi_ref, sems.at[slots])]
+    fetches[0].start()
+    at = [jnp.max(packet_ref[s : s + 1, tile:]).astype(jnp.int32) for s in range(slots)]
+    for s, p in enumerate(at):
+        columns = pl.ds(pl.multiple_of((s * blocks + jnp.maximum(p, 0)) * tile, tile), tile)
+        fetches.append(pltpu.make_async_copy(omega_hbm.at[:, columns], chosen_ref.at[s], sems.at[s]))
+        fetches[-1].start()
+    for s, p in enumerate(at):
         x = counts_ref[s].astype(jnp.float32)
-        logs_ref[s] = jnp.log(jnp.where(pos_ref[s] >= 0, x, 1.0))
-        return carry
-
-    lax.fori_loop(0, slots, one, 0)
-    for s in range(slots):
-        fetch(s).wait()
-    fetch_psi.wait()
+        logs_ref[s] = jnp.log(jnp.where(p >= 0, x, 1.0))
+    for fetch in fetches:
+        fetch.wait()
 
 
 def stages(rows):
@@ -82,14 +71,25 @@
     return [[(1, 1), (2, 1), (3, 0)]] + [[(bit, 1)] for bit in bits]
 
 
-def outer(row):
-    return ((row >> 2) ^ (row >> 1)) & 1 == 0
-
-
-def rounds(rows):
+def partners(rows):
     if rows == 8:
-        return [(4, 4), (6, 1), (7, 7), (3, 3), (5, 5), (2, 2), (1, 6)]
-    return [(k, k) for k in range(rows - 1, 0, -1)]
+        return [
+            [4, 5, 6, 7, 0, 1, 2, 3],
+            [6, 7, 3, 2, 5, 4, 0, 1],
+            [7, 6, 5, 4, 3, 2, 1, 0],
+            [3, 2, 1, 0, 7, 6, 5, 4],
+            [5, 4, 7, 6, 1, 0, 3, 2],
+            [2, 3, 0, 1, 6, 7, 4, 5],
+            [1, 0, 4, 5, 2, 3, 7, 6],
+        ]
+    return [[row ^ k for row in range(rows)] for k in range(rows - 1, 0, -1)]
+
+
+def pick(table, me):
+    offsets = {row ^ other for row, other in enumerate(table)}
+    if len(offsets) == 1:
+        return jnp.bitwise_xor(me, offsets.pop())
+    return sum(jnp.where(me == row, other, 0) for row, other in enumerate(table))
 
 
 def matrix_kernel(blocks, near, far, order, mine_ref, other_ref, logs_ref, psi_ref, matrix_ref, incoming_ref, *out_refs):
@@ -135,26 +135,28 @@
         if c == 0:
             at = jnp.where(mine, at[:, :LANES], 0.0)
             position[r] = jnp.sum(at, axis=0, keepdims=True).astype(jnp.int32)
-    for k, (a, b) in enumerate(order):
-        at = position[a] if a == b else jnp.where(outer(me), position[a], position[b])
-        incoming_ref[k : k + 1, :] = at
+    for r, at in position.items():
+        incoming_ref[r : r + 1, :] = at
 
     both = mine_ref[:8, -tile:] + other_ref[:8, -tile:]
     shift = jnp.log(jnp.full((8, tile), total)) - jnp.log(both) - shift_log
     shift = jnp.transpose(shift)[:, :1]
 
-    for s in range(slots):
-        x = logs_ref[s] + shift + terms[s : s + 1]
-        matrix_ref[s] = jnp.maximum(x, 0.0).astype(jnp.bfloat16)
     psi = psi_ref[...]
-    for (a, b), out_ref in zip(order, out_refs, strict=True):
-        s = jnp.bitwise_xor(me, a if a == b else jnp.where(outer(me), a, b))
-        out_ref[...] = lax.dot_general(psi, matrix_ref[s], NN, preferred_element_type=jnp.float32)
-
-
-def place(at_ref, refs, first, out_ref):
+    row = lax.broadcasted_iota(jnp.int32, (slots, tile), 0)
+    for table, out_ref in zip(order, out_refs, strict=True):
+        s = pick(table, me)
+        term = jnp.sum(jnp.where(row == s, terms, 0.0), axis=0, keepdims=True)
+        x = jnp.maximum(logs_ref[s] + shift + term, 0.0).astype(jnp.bfloat16)
+        matrix_ref[s] = x
+        out_ref[...] = lax.dot_general(psi, x, NN, preferred_element_type=jnp.float32)
+
+
+def place(at_ref, refs, tables, out_ref):
     tile = refs[0].shape[1]
-    at = [jnp.max(at_ref[k : k + 1, :]) for k in first]
+    me = lax.axis_index("row")
+    offset = lax.broadcasted_iota(jnp.int32, at_ref.shape, 0)
+    at = [jnp.max(jnp.where(offset == jnp.bitwise_xor(me, pick(table, me)), at_ref[...], -1)) for table in tables]
     for p, ref in zip(at, refs, strict=True):
         columns = pl.ds(pl.multiple_of(jnp.maximum(p, 0) * tile, tile), tile)
         out_ref[:, columns] += jnp.where(p >= 0, ref[...], 0.0)
@@ -191,7 +193,7 @@
     rank, width = omega_t.shape
     blocks = width // (slots * tile)
     rows = slots
-    order = [(0, 0)] + rounds(rows)
+    order = [list(range(rows))] + partners(rows)
     DMA = pltpu.SemaphoreType.DMA
 
     def call(kernel, name, outs, ins, out_specs=None, scratch=(), cost=None):
@@ -206,8 +208,8 @@
             name=name,
         )
 
-    def swap(x, far, near):
-        return lax.ppermute(x, "row", [(i, i ^ (far if outer(i) else near)) for i in range(rows)])
+    def swap(x, table):
+        return lax.ppermute(x, "row", list(enumerate(table)))
 
     def across(x, k, odd):
         pairs = [(2 * i + c, 2 * (i ^ k) + (c ^ odd)) for i in range(rows) for c in range(2)]
@@ -244,10 +246,10 @@
         lambda *refs: prepare_kernel(blocks, *refs),
         "prepare",
         (f32(slots, tile, tile), bf16(slots, rank, tile), bf16(*psi.shape)),
-        [HBM, VMEM, HBM, HBM],
-        scratch=[pltpu.SMEM((slots,), jnp.int32), DMA((slots + 2,))],
+        [VMEM, VMEM, HBM, HBM],
+        scratch=[DMA((slots + 1,))],
         cost=pl.CostEstimate(flops=40 * counts.size, bytes_accessed=6 * counts.size, transcendentals=counts.size),
-    )(tile_pos, held, omega_t, psi)
+    )(packet, held, omega_t, psi)
 
     row_part = jnp.concatenate([row_part] * (gathered.shape[0] // row_part.shape[0]))
     gathered = jnp.concatenate([gathered, row_part], axis=1)
@@ -261,18 +263,18 @@
         [VMEM] * 4,
     )(gathered, other, logs, held_psi)
 
-    arrived = [swap(part, *ks) for part, ks in zip(parts[1:], order[1:], strict=True)]
-    half = 2
+    arrived = [swap(part, table) for part, table in zip(parts[1:], order[1:], strict=True)]
+    half = 3
 
     partial_range, early = call(
-        lambda *refs: early_kernel(range(half + 1), *refs),
+        lambda *refs: early_kernel(order[: half + 1], *refs),
         "early",
         (f32(rank, tile), f32(rank, blocks * tile)),
         [VMEM] * (4 + half),
     )(incoming_at, matrix, chosen, parts[0], *arrived[:half])
     other_range = other_col(partial_range)
     return call(
-        lambda *refs: late_kernel(range(half + 1, rows), *refs),
+        lambda *refs: late_kernel(order[half + 1 :], *refs),
         "late",
         (f32(rank, tile), f32(rank, blocks * tile)),
         [VMEM] * (4 + rows - 1 - half),

time: 32.9 us -> 32.7 us (level)
  Pallas kernels: 5.93 us -> 5.19 us
  waiting for transfers between devices: 6.92 us -> 7.49 us
    ppermute x4, waiting for transfers between devices: 2.75 us -> 3.31 us  [across(): return lax.ppermute(x, ('row', 'col'), pairs)]
    pallas_call x1, Pallas kernels: 1.63 us -> 1.08 us  [on_device(): call(lambda *refs: prepare_kernel(blocks, *refs), 'prepare', (f32(slots,...]
  transfers between devices with their start and end apart: 13 -> 13, of which waited for: 5 -> 7; matrix products, arithmetic and copies ran while one was open for 0% -> 0% of each run, Pallas kernels for 6% -> 5%
where the time goes in v6:
time: 32.7 us; the launch traced here: 32.5 us
  starting transfers between devices  19.1 us (58%)
  waiting for transfers between devices  7.49 us (23%)
  Pallas kernels  5.19 us (16%)
  between operations  0.69 us (2%)
    ppermute x7, starting transfers between devices, swap(): return lax.ppermute(x, 'row', list(enumerate(table)))  11.3 us
    ppermute x4, starting transfers between devices, across(): return lax.ppermute(x, ('row', 'col'), pairs)  7.23 us
    ppermute x4, waiting for transfers between devices, across(): return lax.ppermute(x, ('row', 'col'), pairs)  3.31 us
    ppermute x7, waiting for transfers between devices, swap(): return lax.ppermute(x, 'row', list(enumerate(table)))  3.24 us
    pallas_call x1, Pallas kernels, on_device(): call(sums_kernel, 'sums', (f32(slots, tile + LANES), f32(8, tile), bf16(s...  1.6 us
    pallas_call x1, Pallas kernels, on_device(): call(lambda *refs: late_kernel(order[half + 1:], *refs), 'late', (f32(ran...  1.1 us
    pallas_call x1, Pallas kernels, on_device(): call(lambda *refs: prepare_kernel(blocks, *refs), 'prepare', (f32(slots,...  1.08 us
    pallas_call x1, Pallas kernels, on_device(): call(lambda *refs: matrix_kernel(blocks, near, far, order, *refs), 'matri...  0.97 us
  transfers between devices with their start and end apart: 13, of which 7 were waited for; matrix products, arithmetic and copies ran while one was open for 0% of the time, Pallas kernels for 5%

profile of v6, /device:TPU:0, one launch (start us, length us, event | category | flops | bytes accessed | tf_op | source)
XLA Modules:
  0.0 32.5 jit_solution(1466213875232922639)
XLA Ops:
  0.6 1.6 %sums.1 = (f32[8,384]{1,0:T(8,128)S(1)}, f32[8,256]{1,0:T(8,128)S(1)}, bf16[8,256,256]{2,1,0:T(8,128)(2,1)S(1)}) custom-call(s32[8]{0:T(128)} %pos_hbm.1, bf16[8,256,256]{2,1,0:T(8,128)(2,1)} %counts_hbm.1), custom_call_target="tpu_custom_call" | custom-call | tf_op jit(solution)/shard_map/sums/pallas_call | solution.py:224
  2.2 4.0 %collective-permute-start.2 = (f32[8,384]{1,0:T(8,128)S(1)}, f32[8,384]{1,0:T(8,128)S(1)}, u32[]{:S(2)}, u32[]{:S(2)}) collective-permute-start(f32[8,384]{1,0:T(8,128)S(1)} %get-tuple-element.26.refs_0_), channel_id=1, source_target_pairs={{0,6},{1,7},{2,4},{3,5},{4,2},{5,3},{6,0},{7,1},{8,14},{9,15},{10,... | collective-permute-start | bytes 36872 | tf_op jit(solution)/shard_map/ppermute | solution.py:216
  6.3 0.0 collective-permute-start.1
  6.3 0.4 %collective-permute-start = (f32[8,384]{1,0:T(8,128)S(1)}, f32[8,384]{1,0:T(8,128)S(1)}, u32[]{:S(2)}, u32[]{:S(2)}) collective-permute-start(f32[8,384]{1,0:T(8,128)S(1)} %get-tuple-element.26.refs_0_), channel_id=1, source_target_pairs={{0,3},{1,2},{2,1},{3,0},{4,7},{5,6},{6,5},{7,4},{8,11},{9,10},{10,... | collective-permute-start | bytes 36872 | tf_op jit(solution)/shard_map/ppermute | solution.py:216
  6.7 2.7 %collective-permute-done = f32[8,384]{1,0:T(8,128)S(1)} collective-permute-done((f32[8,384]{1,0:T(8,128)S(1)}, f32[8,384]{1,0:T(8,128)S(1)}, u32[]{:S(2)}, u32[]{:S(2)}) %collective-permute-start) | collective-permute-done | bytes 12320 | tf_op jit(solution)/shard_map/ppermute | solution.py:216
  9.4 0.0 collective-permute-done.1
  9.4 0.0 collective-permute-done.2
  9.4 2.8 %collective-permute-start.3 = (f32[8,1152]{1,0:T(8,128)S(1)}, f32[8,1152]{1,0:T(8,128)S(1)}, u32[]{:S(2)}, u32[]{:S(2)}) collective-permute-start(f32[8,1152]{1,0:T(8,128)S(1)} %constant_dynamic-update-slice_fusion), channel_id=1, source_target_pairs={{0,9},{1,8},{2,11},{3,10},{4,13},{5,12},{6,15},{7,14},{8,1},{9,0},... | collective-permute-start | bytes 110600 | tf_op jit(solution)/shard_map/ppermute | solution.py:216
  12.3 1.1 %prepare.1 = (f32[8,256,256]{2,1,0:T(8,128)S(1)}, bf16[8,64,256]{2,1,0:T(8,128)(2,1)S(1)}, bf16[64,256]{1,0:T(8,128)(2,1)S(1)}) custom-call(f32[8,384]{1,0:T(8,128)S(1)} %get-tuple-element.26.refs_0_, bf16[8,256,256]{2,1,0:T(8,128)(2,1)S(1)} %get-tuple-element.30.refs_1_, bf16[64,16384]{1,0:T(8,128)(2,1)} %refs_2_.1, bf16[64,256]{1,0:T(8,128)(2,1)} %refs_3_.1), custom_call_target="tpu_custom_call" | custom-call | flops 20971520 | bytes 3145728 | tf_op jit(solution)/shard_map/prepare/pallas_call | solution.py:245
  13.4 0.6 %collective-permute-done.3 = f32[8,1152]{1,0:T(8,128)S(1)} collective-permute-done((f32[8,1152]{1,0:T(8,128)S(1)}, f32[8,1152]{1,0:T(8,128)S(1)}, u32[]{:S(2)}, u32[]{:S(2)}) %collective-permute-start.3) | collective-permute-done | bytes 36896 | tf_op jit(solution)/shard_map/ppermute | solution.py:216
  13.9 0.5 %collective-permute-start.4 = (f32[16,1408]{1,0:T(8,128)S(1)}, f32[16,1408]{1,0:T(8,128)S(1)}, u32[]{:S(2)}, u32[]{:S(2)}) collective-permute-start(f32[16,1408]{1,0:T(8,128)S(1)} %maximum_maximum_fusion.refs_0_), channel_id=1, source_target_pairs={{0,1},{1,0},{2,3},{3,2},{4,5},{5,4},{6,7},{7,6},{8,9},{9,8},{10,11... | collective-permute-start | bytes 270344 | tf_op jit(solution)/shard_map/ppermute | solution.py:219
  14.4 0.9 %collective-permute-done.4.refs_1_ = f32[16,1408]{1,0:T(8,128)S(1)} collective-permute-done((f32[16,1408]{1,0:T(8,128)S(1)}, f32[16,1408]{1,0:T(8,128)S(1)}, u32[]{:S(2)}, u32[]{:S(2)}) %collective-permute-start.4) | collective-permute-done | bytes 90144 | tf_op jit(solution)/shard_map/ppermute | solution.py:219
  15.4 1.0 %matrix.1 = (bf16[8,256,256]{2,1,0:T(8,128)(2,1)S(1)}, s32[8,128]{1,0:T(8,128)S(1)}, f32[64,256]{1,0:T(8,128)S(1)}, f32[64,256]{1,0:T(8,128)S(1)}, f32[64,256]{1...) custom-call(f32[16,1408]{1,0:T(8,128)S(1)} %maximum_maximum_fusion.r, ...), custom_call_target="tpu_custom_call" | custom-call | tf_op jit(solution)/shard_map/matrix/pallas_call | solution.py:259
  16.3 2.6 %collective-permute-start.5 = (f32[64,256]{1,0:T(8,128)S(1)}, f32[64,256]{1,0:T(8,128)S(1)}, u32[]{:S(2)}, u32[]{:S(2)}) collective-permute-start(f32[64,256]{1,0:T(8,128)S(1)} %get-tuple-element.41), channel_id=1, source_target_pairs={{0,8},{2,10},{4,12},{6,14},{8,0},{10,2},{12,4},{14,6},{1,9},{3,11}... | collective-permute-start | bytes 196616 | tf_op jit(solution)/shard_map/ppermute | solution.py:212
  19.0 1.4 %collective-permute-start.6 = (f32[64,256]{1,0:T(8,128)S(1)}, f32[64,256]{1,0:T(8,128)S(1)}, u32[]{:S(2)}, u32[]{:S(2)}) collective-permute-start(f32[64,256]{1,0:T(8,128)S(1)} %get-tuple-element.42), channel_id=1, source_target_pairs={{0,12},{2,14},{4,6},{6,4},{8,10},{10,8},{12,0},{14,2},{1,13},{3,15... | collective-permute-start | bytes 196616 | tf_op jit(solution)/shard_map/ppermute | solution.py:212
  20.4 2.4 %collective-permute-start.7 = (f32[64,256]{1,0:T(8,128)S(1)}, f32[64,256]{1,0:T(8,128)S(1)}, u32[]{:S(2)}, u32[]{:S(2)}) collective-permute-start(f32[64,256]{1,0:T(8,128)S(1)} %get-tuple-element.43), channel_id=1, source_target_pairs={{0,14},{2,12},{4,10},{6,8},{8,6},{10,4},{12,2},{14,0},{1,15},{3,13... | collective-permute-start | bytes 196616 | tf_op jit(solution)/shard_map/ppermute | solution.py:212
  22.8 0.0 collective-permute-start.9
  22.8 3.2 %collective-permute-start.10 = (f32[64,256]{1,0:T(8,128)S(1)}, f32[64,256]{1,0:T(8,128)S(1)}, u32[]{:S(2)}, u32[]{:S(2)}) collective-permute-start(f32[64,256]{1,0:T(8,128)S(1)} %get-tuple-element.47), channel_id=1, source_target_pairs={{0,10},{2,8},{4,14},{6,12},{8,2},{10,0},{12,6},{14,4},{1,11},{3,9}... | collective-permute-start | bytes 196616 | tf_op jit(solution)/shard_map/ppermute | solution.py:212
  26.0 0.0 collective-permute-done.5.refs_4_
  26.0 0.7 %collective-permute-start.11 = (f32[64,256]{1,0:T(8,128)S(1)}, f32[64,256]{1,0:T(8,128)S(1)}, u32[]{:S(2)}, u32[]{:S(2)}) collective-permute-start(f32[64,256]{1,0:T(8,128)S(1)} %get-tuple-element.48), channel_id=1, source_target_pairs={{0,4},{2,6},{4,0},{6,2},{8,12},{10,14},{12,8},{14,10},{1,5},{3,7},... | collective-permute-start | bytes 196616 | tf_op jit(solution)/shard_map/ppermute | solution.py:212
  26.7 0.0 collective-permute-done.6.refs_5_
  26.7 0.9 %collective-permute-start.12 = (f32[64,256]{1,0:T(8,128)S(1)}, f32[64,256]{1,0:T(8,128)S(1)}, u32[]{:S(2)}, u32[]{:S(2)}) collective-permute-start(f32[64,256]{1,0:T(8,128)S(1)} %get-tuple-element.49), channel_id=1, source_target_pairs={{0,2},{2,0},{4,8},{6,10},{8,4},{10,6},{12,14},{14,12},{1,3},{3,1},... | collective-permute-start | bytes 196616 | tf_op jit(solution)/shard_map/ppermute | solution.py:212
  27.6 0.2 collective-permute-done.7.refs_6_
  27.8 0.4 %early.1 = (f32[64,256]{1,0:T(8,128)S(1)}, f32[64,2048]{1,0:T(8,128)S(1)}) custom-call(s32[8,128]{1,0:T(8,128)S(1)} %get-tuple-element.37.refs_0_, bf16[8,256,256]{2,1,0:T(8,128)(2,1)S(1)} %get-tuple-element.38.refs_1_, bf16[8,64,256]{2,1,0:T(8,128)(2,1)S(1)} %get-tuple-element.39.refs_2_, f32[64,256]{1,0:T(8,128)S(1)} %get-tuple-element.40.refs_3_, ...), custom_call_target="tpu_custom_call" | custom-call | tf_op jit(solution)/shard_map/early/pallas_call | solution.py:269
  28.3 0.1 collective-permute-start.8
  28.4 1.9 %collective-permute-done.9.refs_4_ = f32[64,256]{1,0:T(8,128)S(1)} collective-permute-done((f32[64,256]{1,0:T(8,128)S(1)}, f32[64,256]{1,0:T(8,128)S(1)}, u32[]{:S(2)}, u32[]{:S(2)}) %collective-permute-start.9) | collective-permute-done | bytes 65568 | tf_op jit(solution)/shard_map/ppermute | solution.py:212
  30.3 0.0 collective-permute-done.10.refs_5_
  30.3 0.5 %collective-permute-done.11.refs_6_ = f32[64,256]{1,0:T(8,128)S(1)} collective-permute-done((f32[64,256]{1,0:T(8,128)S(1)}, f32[64,256]{1,0:T(8,128)S(1)}, u32[]{:S(2)}, u32[]{:S(2)}) %collective-permute-start.11) | collective-permute-done | bytes 65568 | tf_op jit(solution)/shard_map/ppermute | solution.py:212
  30.8 0.6 %collective-permute-done.12.refs_7_ = f32[64,256]{1,0:T(8,128)S(1)} collective-permute-done((f32[64,256]{1,0:T(8,128)S(1)}, f32[64,256]{1,0:T(8,128)S(1)}, u32[]{:S(2)}, u32[]{:S(2)}) %collective-permute-start.12) | collective-permute-done | bytes 65568 | tf_op jit(solution)/shard_map/ppermute | solution.py:212
  31.4 0.0 collective-permute-done.8.refs_3_
  31.4 1.1 %late.1 = (f32[64,256]{1,0:T(8,128)}, f32[64,2048]{1,0:T(8,128)}) custom-call(s32[8,128]{1,0:T(8,128)S(1)} %get-tuple-element.37.refs_0_, f32[64,2048]{1,0:T(8,128)S(1)} %get-tuple-element.44.refs_1_, f32[64,256]{1,0:T(8,128)S(1)} %get-tuple-element.45.refs_2_, f32[64,256]{1,0:T(8,128)S(1)} %collective-permute-done.8.refs_3_, ...), custom_call_target="tpu_custom_call" | custom-call | tf_op jit(solution)/shard_map/late/pallas_call | solution.py:276
  (8 shorter events, 0.0 us)
Async XLA Ops:
  2.2 7.2 %collective-permute-start.2 = (f32[8,384]{1,0:T(8,128)S(1)}, f32[8,384]{1,0:T(8,128)S(1)}, u32[]{:S(2)}, u32[]{:S(2)}) collective-permute-start(f32[8,384]{1,0:T(8,128)S(1)} %get-tuple-element.26.refs_0_), channel_id=1, source_target_pairs={{0,6},{1,7},{2,4},{3,5},{4,2},{5,3},{6,0},{7,1},{8,14},{9,15},{10,... | collective-permute-start | bytes 36872 | tf_op jit(solution)/shard_map/ppermute | solution.py:216
  6.3 3.1 %collective-permute-start.1 = (f32[8,384]{1,0:T(8,128)S(1)}, f32[8,384]{1,0:T(8,128)S(1)}, u32[]{:S(2)}, u32[]{:S(2)}) collective-permute-start(f32[8,384]{1,0:T(8,128)S(1)} %get-tuple-element.26.refs_0_), channel_id=1, source_target_pairs={{0,5},{1,4},{2,7},{3,6},{4,1},{5,0},{6,3},{7,2},{8,13},{9,12},{10,... | collective-permute-start | bytes 36872 | tf_op jit(solution)/shard_map/ppermute | solution.py:216
  6.3 3.1 %collective-permute-start = (f32[8,384]{1,0:T(8,128)S(1)}, f32[8,384]{1,0:T(8,128)S(1)}, u32[]{:S(2)}, u32[]{:S(2)}) collective-permute-start(f32[8,384]{1,0:T(8,128)S(1)} %get-tuple-element.26.refs_0_), channel_id=1, source_target_pairs={{0,3},{1,2},{2,1},{3,0},{4,7},{5,6},{6,5},{7,4},{8,11},{9,10},{10,... | collective-permute-start | bytes 36872 | tf_op jit(solution)/shard_map/ppermute | solution.py:216
  9.4 4.5 %collective-permute-start.3 = (f32[8,1152]{1,0:T(8,128)S(1)}, f32[8,1152]{1,0:T(8,128)S(1)}, u32[]{:S(2)}, u32[]{:S(2)}) collective-permute-start(f32[8,1152]{1,0:T(8,128)S(1)} %constant_dynamic-update-slice_fusion), channel_id=1, source_target_pairs={{0,9},{1,8},{2,11},{3,10},{4,13},{5,12},{6,15},{7,14},{8,1},{9,0},... | collective-permute-start | bytes 110600 | tf_op jit(solution)/shard_map/ppermute | solution.py:216
  13.9 1.5 %collective-permute-start.4 = (f32[16,1408]{1,0:T(8,128)S(1)}, f32[16,1408]{1,0:T(8,128)S(1)}, u32[]{:S(2)}, u32[]{:S(2)}) collective-permute-start(f32[16,1408]{1,0:T(8,128)S(1)} %maximum_maximum_fusion.refs_0_), channel_id=1, source_target_pairs={{0,1},{1,0},{2,3},{3,2},{4,5},{5,4},{6,7},{7,6},{8,9},{9,8},{10,11... | collective-permute-start | bytes 270344 | tf_op jit(solution)/shard_map/ppermute | solution.py:219
  16.3 9.6 %collective-permute-start.5 = (f32[64,256]{1,0:T(8,128)S(1)}, f32[64,256]{1,0:T(8,128)S(1)}, u32[]{:S(2)}, u32[]{:S(2)}) collective-permute-start(f32[64,256]{1,0:T(8,128)S(1)} %get-tuple-element.41), channel_id=1, source_target_pairs={{0,8},{2,10},{4,12},{6,14},{8,0},{10,2},{12,4},{14,6},{1,9},{3,11}... | collective-permute-start | bytes 196616 | tf_op jit(solution)/shard_map/ppermute | solution.py:212
  19.0 7.7 %collective-permute-start.6 = (f32[64,256]{1,0:T(8,128)S(1)}, f32[64,256]{1,0:T(8,128)S(1)}, u32[]{:S(2)}, u32[]{:S(2)}) collective-permute-start(f32[64,256]{1,0:T(8,128)S(1)} %get-tuple-element.42), channel_id=1, source_target_pairs={{0,12},{2,14},{4,6},{6,4},{8,10},{10,8},{12,0},{14,2},{1,13},{3,15... | collective-permute-start | bytes 196616 | tf_op jit(solution)/shard_map/ppermute | solution.py:212
  20.4 7.5 %collective-permute-start.7 = (f32[64,256]{1,0:T(8,128)S(1)}, f32[64,256]{1,0:T(8,128)S(1)}, u32[]{:S(2)}, u32[]{:S(2)}) collective-permute-start(f32[64,256]{1,0:T(8,128)S(1)} %get-tuple-element.43), channel_id=1, source_target_pairs={{0,14},{2,12},{4,10},{6,8},{8,6},{10,4},{12,2},{14,0},{1,15},{3,13... | collective-permute-start | bytes 196616 | tf_op jit(solution)/shard_map/ppermute | solution.py:212
  22.8 7.5 %collective-permute-start.9 = (f32[64,256]{1,0:T(8,128)S(1)}, f32[64,256]{1,0:T(8,128)S(1)}, u32[]{:S(2)}, u32[]{:S(2)}) collective-permute-start(f32[64,256]{1,0:T(8,128)S(1)} %get-tuple-element.46), channel_id=1, source_target_pairs={{0,6},{2,4},{4,2},{6,0},{8,14},{10,12},{12,10},{14,8},{1,7},{3,5},... | collective-permute-start | bytes 196616 | tf_op jit(solution)/shard_map/ppermute | solution.py:212
  22.8 7.5 %collective-permute-start.10 = (f32[64,256]{1,0:T(8,128)S(1)}, f32[64,256]{1,0:T(8,128)S(1)}, u32[]{:S(2)}, u32[]{:S(2)}) collective-permute-start(f32[64,256]{1,0:T(8,128)S(1)} %get-tuple-element.47), channel_id=1, source_target_pairs={{0,10},{2,8},{4,14},{6,12},{8,2},{10,0},{12,6},{14,4},{1,11},{3,9}... | collective-permute-start | bytes 196616 | tf_op jit(solution)/shard_map/ppermute | solution.py:212
  26.0 4.8 %collective-permute-start.11 = (f32[64,256]{1,0:T(8,128)S(1)}, f32[64,256]{1,0:T(8,128)S(1)}, u32[]{:S(2)}, u32[]{:S(2)}) collective-permute-start(f32[64,256]{1,0:T(8,128)S(1)} %get-tuple-element.48), channel_id=1, source_target_pairs={{0,4},{2,6},{4,0},{6,2},{8,12},{10,14},{12,8},{14,10},{1,5},{3,7},... | collective-permute-start | bytes 196616 | tf_op jit(solution)/shard_map/ppermute | solution.py:212
  26.7 4.7 %collective-permute-start.12 = (f32[64,256]{1,0:T(8,128)S(1)}, f32[64,256]{1,0:T(8,128)S(1)}, u32[]{:S(2)}, u32[]{:S(2)}) collective-permute-start(f32[64,256]{1,0:T(8,128)S(1)} %get-tuple-element.49), channel_id=1, source_target_pairs={{0,2},{2,0},{4,8},{6,10},{8,4},{10,6},{12,14},{14,12},{1,3},{3,1},... | collective-permute-start | bytes 196616 | tf_op jit(solution)/shard_map/ppermute | solution.py:212
  28.3 3.1 %collective-permute-start.8 = (f32[64,256]{1,0:T(8,128)S(1)}, f32[64,256]{1,0:T(8,128)S(1)}, u32[]{:S(2)}, u32[]{:S(2)}) collective-permute-start(f32[64,256]{1,0:T(8,128)S(1)} %get-tuple-element.45.refs_2_), channel_id=1, source_target_pairs={{0,1},{1,0},{2,3},{3,2},{4,5},{5,4},{6,7},{7,6},{8,9},{9,8},{10,11... | collective-permute-start | bytes 196616 | tf_op jit(solution)/shard_map/ppermute | solution.py:219
